TPU v7x, 32 devices: a whole 2x2x4 slice. The times are simulated.
32 devices in a mesh: dp: 8 (over z, y), rows: 2 (over core), cols: 2 (over x).
Axes of the slice: x: 2, y: 2, z: 4, core: 2. Of those that a mesh axis runs over, the one named last changes fastest.
Arguments:
- tokens: bfloat16 [1536, 16384], P('rows', ('dp', 'cols')), may hold values from -6 to 6
- lengths: int32 [16], P('dp'), may hold values from 256 to 1024, as said below
- mix_gain: float32 [1536], P('rows'), may hold values from 0.5 to 1.5
- rec_weight: bfloat16 [1536, 2048], P('rows', 'cols'), may hold values from -0.15625 to 0.15625
- gate_weight: bfloat16 [1536, 2048], P('rows', 'cols'), may hold values from -0.15625 to 0.15625
- conv_weight: float32 [4, 2048], P(None, 'cols'), may hold values from -3 to 3
- conv_bias: float32 [2048], P('cols'), may hold values from -2 to 2
- recur_weight: bfloat16 [16, 128, 128], P('cols'), may hold values from -0.5 to 0.5
- recur_bias: float32 [2048], P('cols'), may hold values from -3 to 3
- input_weight: bfloat16 [16, 128, 128], P('cols'), may hold values from -0.5 to 0.5
- input_bias: float32 [2048], P('cols'), may hold values from -3 to 3
- decay_param: float32 [2048], P('cols'), may hold values from 1 to 8
- out_weight: bfloat16 [1536, 2048], P('rows', 'cols'), may hold values from -0.5 to 0.5
- ffn_gain: float32 [1536], P('rows'), may hold values from 0.5 to 1.5
- ffn_gate: bfloat16 [1536, 4608], P('rows', 'cols'), may hold values from -0.15625 to 0.15625
- ffn_up: bfloat16 [1536, 4608], P('rows', 'cols'), may hold values from -0.15625 to 0.15625
- ffn_down: bfloat16 [1536, 4608], P('rows', 'cols'), may hold values from -0.125 to 0.125
- cotangent: bfloat16 [1536, 16384], P('rows', ('dp', 'cols')), may hold values from -6 to 6
Outputs:
- result: bfloat16 [1536, 16384], P('rows', ('dp', 'cols'))
- grad_tokens: bfloat16 [1536, 16384], P('rows', ('dp', 'cols'))
- grad_mix_gain: float32 [1536], P('rows')
- grad_rec_weight: float32 [1536, 2048], P('rows', 'cols')
- grad_gate_weight: float32 [1536, 2048], P('rows', 'cols')
- grad_conv_weight: float32 [4, 2048], P(None, 'cols')
- grad_conv_bias: float32 [2048], P('cols')
- grad_recur_weight: float32 [16, 128, 128], P('cols')
- grad_recur_bias: float32 [2048], P('cols')
- grad_input_weight: float32 [16, 128, 128], P('cols')
- grad_input_bias: float32 [2048], P('cols')
- grad_decay_param: float32 [2048], P('cols')
- grad_out_weight: float32 [1536, 2048], P('rows', 'cols')
- grad_ffn_gain: float32 [1536], P('rows')
- grad_ffn_gate: float32 [1536, 4608], P('rows', 'cols')
- grad_ffn_up: float32 [1536, 4608], P('rows', 'cols')
- grad_ffn_down: float32 [1536, 4608], P('rows', 'cols')
Inputs may be any that keep to these rules, and one draw needn't show every extreme that they name: `lengths`: live slots of each sequence, counted from its first slot; some sequence has 1024.
All inputs are finite; a program needn't handle non-finite values.
Results may differ from a plain program's by a relative error of at most 0.014.
Values may be sent and summed in bfloat16 or wider, within the bound.
A program may use at most 384 MiB of HBM per device.

v0:
```python
import math

import jax
import jax.numpy as jnp
from jax import lax
from jax.sharding import PartitionSpec as P

D = 1536
KCONV = 4
LEN = 1024


EPS = 1e-06
GATE_SCALE = 8.0
TANH_COEF = math.sqrt(2.0 / math.pi)
CUBIC_COEF = 0.044715


def gelu_pair(values):
    inner_arg = TANH_COEF * (values + CUBIC_COEF * values * values * values)
    tanh_val = jnp.tanh(inner_arg)
    output = 0.5 * values * (1.0 + tanh_val)
    slope = 0.5 * (1.0 + tanh_val) + 0.5 * values * (1.0 - tanh_val * tanh_val) * TANH_COEF * (
        1.0 + 3.0 * CUBIC_COEF * values * values
    )
    return (output, slope)


def feature_total(values):
    return lax.psum(values, "rows")


def rms_scale(residual):
    total = feature_total(jnp.sum(residual * residual, axis=1))
    return lax.rsqrt(total / D + EPS)


def norm_back(residual, scale, gain, grad_normed):
    weighted = grad_normed * gain
    grad_gain = jnp.sum(grad_normed * residual * scale[:, None], axis=0)
    inner_sum = feature_total(jnp.sum(weighted * residual, axis=1))
    grad_resid = (
        scale[:, None] * weighted - residual * (scale * scale * scale * inner_sum / D)[:, None]
    )
    return (grad_resid, grad_gain)


def linear_step(earlier, latter):
    return (earlier[0] * latter[0], latter[0] * earlier[1] + latter[1])


def cols_to_rows(activation, weight):
    gathered = lax.all_gather(activation, "cols", axis=0, tiled=True)
    total = lax.psum_scatter(
        jnp.dot(gathered, weight, preferred_element_type=jnp.float32),
        "rows",
        scatter_dimension=0,
        tiled=True,
    )
    return (gathered, total)


def rows_to_cols(activation, weight):
    gathered = lax.all_gather(activation, "rows", axis=0, tiled=True)
    total = lax.psum_scatter(
        jnp.dot(gathered, weight, preferred_element_type=jnp.float32),
        "cols",
        scatter_dimension=0,
        tiled=True,
    )
    return (gathered, total)


def body(
    tokens,
    lengths,
    mix_gain,
    rec_weight,
    gate_weight,
    conv_weight,
    conv_bias,
    recur_weight,
    recur_bias,
    input_weight,
    input_bias,
    decay_param,
    out_weight,
    ffn_gain,
    ffn_gate,
    ffn_up,
    ffn_down,
    cotangent,
):
    residual = tokens.astype(jnp.float32).T
    count_model = residual.shape[0]
    positions = lax.axis_index("cols") * count_model + jnp.arange(count_model, dtype=jnp.int32)
    seq_ids = positions // LEN
    within = positions % LEN
    seq_match = seq_ids[:, None] == jnp.arange(lengths.shape[0], dtype=jnp.int32)[None, :]
    token_len = jnp.sum(jnp.where(seq_match, lengths[None, :], 0), axis=1)
    live_mask = (within < token_len).astype(jnp.float32)[:, None]
    scale_one = rms_scale(residual)
    normed_one = (residual * scale_one[:, None] * mix_gain).astype(jnp.bfloat16)
    first_in = jnp.concatenate([rec_weight, gate_weight], axis=1)
    normed_one_g, projected = cols_to_rows(normed_one, first_in)
    branch_width = rec_weight.shape[1]
    rows_mid = projected.shape[0]
    seqs_here = rows_mid // LEN
    rec_seq = projected[:, :branch_width].reshape(seqs_here, LEN, branch_width)
    gate_seq = projected[:, branch_width:].reshape(seqs_here, LEN, branch_width)
    padded = jnp.pad(rec_seq, ((0, 0), (KCONV - 1, 0), (0, 0)))
    conv_out = conv_bias + jnp.zeros_like(rec_seq)
    for offset in range(KCONV):
        conv_out = (
            conv_out
            + conv_weight[offset] * padded[:, KCONV - 1 - offset : KCONV - 1 - offset + LEN]
        )
    conv_low = conv_out.astype(jnp.bfloat16)
    heads_here = recur_weight.shape[0]
    block_size = recur_weight.shape[1]
    conv_heads = conv_low.reshape(seqs_here, LEN, heads_here, block_size)
    recur_pre = (
        jnp.einsum(
            "slhi,hij->slhj", conv_heads, recur_weight, preferred_element_type=jnp.float32
        ).reshape(seqs_here, LEN, branch_width)
        + recur_bias
    )
    input_pre = (
        jnp.einsum(
            "slhi,hij->slhj", conv_heads, input_weight, preferred_element_type=jnp.float32
        ).reshape(seqs_here, LEN, branch_width)
        + input_bias
    )
    recur_gate = jax.nn.sigmoid(recur_pre)
    input_gate = jax.nn.sigmoid(input_pre)
    soft_decay = jax.nn.softplus(-decay_param)
    log_decay = -GATE_SCALE * recur_gate * soft_decay
    decay = jnp.exp(log_decay)
    scaling = jnp.sqrt(-jnp.expm1(2.0 * log_decay))
    conv_val = conv_low.astype(jnp.float32)
    drive = scaling * input_gate * conv_val
    state = lax.associative_scan(linear_step, (decay, drive), axis=1)[1]
    gate_act, gate_slope = gelu_pair(gate_seq)
    branch = (state * gate_act).astype(jnp.bfloat16).reshape(rows_mid, branch_width)
    branch_g, mixed = rows_to_cols(branch, out_weight.T)
    residual_one = residual + mixed
    scale_two = rms_scale(residual_one)
    normed_two = (residual_one * scale_two[:, None] * ffn_gain).astype(jnp.bfloat16)
    second_in = jnp.concatenate([ffn_gate, ffn_up], axis=1)
    normed_two_g, ffn_pre = cols_to_rows(normed_two, second_in)
    ffn_width = ffn_gate.shape[1]
    ffn_a = ffn_pre[:, :ffn_width]
    ffn_b = ffn_pre[:, ffn_width:]
    act_a, slope_a = gelu_pair(ffn_a)
    hidden = (act_a * ffn_b).astype(jnp.bfloat16)
    hidden_g, ffn_out = rows_to_cols(hidden, ffn_down.T)
    residual_two = residual_one + ffn_out
    result = (live_mask * residual_two).astype(jnp.bfloat16).T
    grad_two = live_mask * cotangent.astype(jnp.float32).T
    grad_two_low = grad_two.astype(jnp.bfloat16)
    grad_down_g, grad_hidden = cols_to_rows(grad_two_low, ffn_down)
    grad_ffn_down = jnp.einsum(
        "tk,td->dk", hidden_g, grad_down_g, preferred_element_type=jnp.float32
    )
    grad_a = grad_hidden * ffn_b * slope_a
    grad_b = grad_hidden * act_a
    grad_ab = jnp.concatenate([grad_a.astype(jnp.bfloat16), grad_b.astype(jnp.bfloat16)], axis=1)
    second_back = jnp.concatenate([ffn_gate.T, ffn_up.T], axis=0)
    grad_ab_g, grad_normed_two = rows_to_cols(grad_ab, second_back)
    grad_ffn_gate = jnp.einsum(
        "td,tk->dk", normed_two_g, grad_ab_g[:, :ffn_width], preferred_element_type=jnp.float32
    )
    grad_ffn_up = jnp.einsum(
        "td,tk->dk", normed_two_g, grad_ab_g[:, ffn_width:], preferred_element_type=jnp.float32
    )
    grad_norm_two, grad_gain_two = norm_back(residual_one, scale_two, ffn_gain, grad_normed_two)
    grad_one = grad_two + grad_norm_two
    grad_one_low = grad_one.astype(jnp.bfloat16)
    grad_out_g, grad_branch = cols_to_rows(grad_one_low, out_weight)
    grad_out_weight = jnp.einsum(
        "tk,td->dk", branch_g, grad_out_g, preferred_element_type=jnp.float32
    )
    grad_branch = grad_branch.reshape(seqs_here, LEN, branch_width)
    grad_state = grad_branch * gate_act
    grad_gate_pre = (
        (grad_branch * state * gate_slope).astype(jnp.bfloat16).reshape(rows_mid, branch_width)
    )
    decay_next = jnp.concatenate([decay[:, 1:], jnp.zeros_like(decay[:, :1])], axis=1)
    carried = lax.associative_scan(linear_step, (decay_next, grad_state), reverse=True, axis=1)[1]
    state_prev = jnp.concatenate([jnp.zeros_like(state[:, :1]), state[:, :-1]], axis=1)
    grad_log = (
        carried * state_prev * decay - carried * input_gate * conv_val * decay * decay / scaling
    )
    grad_recur_pre = grad_log * (-GATE_SCALE * soft_decay) * recur_gate * (1.0 - recur_gate)
    grad_input_pre = carried * scaling * conv_val * input_gate * (1.0 - input_gate)
    grad_recur_bias = jnp.sum(grad_recur_pre, axis=(0, 1))
    grad_input_bias = jnp.sum(grad_input_pre, axis=(0, 1))
    grad_soft = jnp.sum(grad_log * (-GATE_SCALE * recur_gate), axis=(0, 1))
    grad_decay_param = grad_soft * -jax.nn.sigmoid(-decay_param)
    recur_low = grad_recur_pre.astype(jnp.bfloat16).reshape(seqs_here, LEN, heads_here, block_size)
    input_low = grad_input_pre.astype(jnp.bfloat16).reshape(seqs_here, LEN, heads_here, block_size)
    grad_recur_weight = jnp.einsum(
        "slhi,slhj->hij", conv_heads, recur_low, preferred_element_type=jnp.float32
    )
    grad_input_weight = jnp.einsum(
        "slhi,slhj->hij", conv_heads, input_low, preferred_element_type=jnp.float32
    )
    grad_conv = carried * scaling * input_gate
    grad_conv = grad_conv + jnp.einsum(
        "slhj,hij->slhi", recur_low, recur_weight, preferred_element_type=jnp.float32
    ).reshape(seqs_here, LEN, branch_width)
    grad_conv = grad_conv + jnp.einsum(
        "slhj,hij->slhi", input_low, input_weight, preferred_element_type=jnp.float32
    ).reshape(seqs_here, LEN, branch_width)
    grad_conv_bias = jnp.sum(grad_conv, axis=(0, 1))
    grad_conv_weight = jnp.stack(
        [
            jnp.sum(
                grad_conv * padded[:, KCONV - 1 - offset : KCONV - 1 - offset + LEN], axis=(0, 1)
            )
            for offset in range(KCONV)
        ]
    )
    padded_back = jnp.pad(grad_conv, ((0, 0), (0, KCONV - 1), (0, 0)))
    grad_rec = jnp.zeros_like(grad_conv)
    for offset in range(KCONV):
        grad_rec = grad_rec + conv_weight[offset] * padded_back[:, offset : offset + LEN]
    grad_first = jnp.concatenate(
        [grad_rec.astype(jnp.bfloat16).reshape(rows_mid, branch_width), grad_gate_pre], axis=1
    )
    first_back = jnp.concatenate([rec_weight.T, gate_weight.T], axis=0)
    grad_first_g, grad_normed_one = rows_to_cols(grad_first, first_back)
    grad_rec_weight = jnp.einsum(
        "td,tk->dk",
        normed_one_g,
        grad_first_g[:, :branch_width],
        preferred_element_type=jnp.float32,
    )
    grad_gate_weight = jnp.einsum(
        "td,tk->dk",
        normed_one_g,
        grad_first_g[:, branch_width:],
        preferred_element_type=jnp.float32,
    )
    grad_norm_one, grad_gain_one = norm_back(residual, scale_one, mix_gain, grad_normed_one)
    grad_tokens = (grad_one + grad_norm_one).astype(jnp.bfloat16).T
    summed_big = (
        lax.psum(grad_rec_weight.astype(jnp.bfloat16), "dp").astype(jnp.float32),
        lax.psum(grad_gate_weight.astype(jnp.bfloat16), "dp").astype(jnp.float32),
        lax.psum(grad_out_weight.astype(jnp.bfloat16), "dp").astype(jnp.float32),
        lax.psum(grad_ffn_gate.astype(jnp.bfloat16), "dp").astype(jnp.float32),
        lax.psum(grad_ffn_up.astype(jnp.bfloat16), "dp").astype(jnp.float32),
        lax.psum(grad_ffn_down.astype(jnp.bfloat16), "dp").astype(jnp.float32),
    )
    summed_gate = lax.psum(
        (
            grad_conv_weight,
            grad_conv_bias,
            grad_recur_weight,
            grad_recur_bias,
            grad_input_weight,
            grad_input_bias,
            grad_decay_param,
        ),
        ("dp", "rows"),
    )
    summed_gain = lax.psum((grad_gain_one, grad_gain_two), ("dp", "cols"))
    return (
        result,
        grad_tokens,
        summed_gain[0],
        summed_big[0],
        summed_big[1],
        summed_gate[0],
        summed_gate[1],
        summed_gate[2],
        summed_gate[3],
        summed_gate[4],
        summed_gate[5],
        summed_gate[6],
        summed_big[2],
        summed_gain[1],
        summed_big[3],
        summed_big[4],
        summed_big[5],
    )


def solution(mesh):
    return jax.shard_map(
        body,
        mesh=mesh,
        in_specs=(
            P("rows", ("dp", "cols")),
            P("dp"),
            P("rows"),
            P("rows", "cols"),
            P("rows", "cols"),
            P(None, "cols"),
            P("cols"),
            P("cols", None, None),
            P("cols"),
            P("cols", None, None),
            P("cols"),
            P("cols"),
            P("rows", "cols"),
            P("rows"),
            P("rows", "cols"),
            P("rows", "cols"),
            P("rows", "cols"),
            P("rows", ("dp", "cols")),
        ),
        out_specs=(
            P("rows", ("dp", "cols")),
            P("rows", ("dp", "cols")),
            P("rows"),
            P("rows", "cols"),
            P("rows", "cols"),
            P(None, "cols"),
            P("cols"),
            P("cols", None, None),
            P("cols"),
            P("cols", None, None),
            P("cols"),
            P("cols"),
            P("rows", "cols"),
            P("rows"),
            P("rows", "cols"),
            P("rows", "cols"),
            P("rows", "cols"),
        ),
        check_vma=False,
    )
```

profile of v0, /device:TPU:0, one launch (start us, length us, event | category | flops | bytes accessed | tf_op | source)
XLA Modules:
  0.0 2183.1 jit_solution(10935123531896475512)
XLA Ops:
  18.0 47.6 %all-gather.10.cloned.1.call-done = bf16[2048,768]{1,0:T(8,128)(2,1)} async-done(((bf16[1024,768]{1,0:T(8,128)(2,1)}), bf16[2048,768]{1,0:T(8,128)(2,1)}) %all-gather.10.cloned.1.call-update) | async-done | bytes 3145744 | tf_op jit(solution)/shard_map/all_gather | solution.py:53
  80.4 24.3 %reduce-scatter.9.cloned.1.call-done = f32[1024,2048]{1,0:T(8,128)} async-done(((f32[2048,2048]{1,0:T(8,128)}), f32[1024,2048]{1,0:T(8,128)}) %reduce-scatter.9.cloned.1.call-update) | async-done | bytes 8388624 | tf_op jit(solution)/shard_map/reduce_scatter | solution.py:54
  451.0 16.5 pad.151
  504.6 72.7 %reduce-scatter.11.cloned.1.call-done = f32[1024,768]{1,0:T(8,128)} async-done(((f32[2048,768]{1,0:T(8,128)}), f32[1024,768]{1,0:T(8,128)}) %reduce-scatter.11.cloned.1.call-update) | async-done | bytes 3145744 | tf_op jit(solution)/shard_map/reduce_scatter | solution.py:65
  587.9 36.3 %all-gather.16.cloned.1.call-done = bf16[2048,768]{1,0:T(8,128)(2,1)} async-done(((bf16[1024,768]{1,0:T(8,128)(2,1)}), bf16[2048,768]{1,0:T(8,128)(2,1)}) %all-gather.16.cloned.1.call-update) | async-done | bytes 3145744 | tf_op jit(solution)/shard_map/all_gather | solution.py:53
  637.2 33.9 %all-gather.12.cloned.1.call-done = bf16[2048,768]{1,0:T(8,128)(2,1)} async-done(((bf16[1024,768]{1,0:T(8,128)(2,1)}), bf16[2048,768]{1,0:T(8,128)(2,1)}) %all-gather.12.cloned.1.call-update) | async-done | bytes 3145744 | tf_op jit(solution)/shard_map/all_gather | solution.py:53
  671.1 31.6 %fusion.11 = f32[2048,4608]{1,0:T(8,128)} fusion(bf16[2048,768]{1,0:T(8,128)(2,1)} %all-gather.12.cloned.1.call-done, bf16[768,2304]{1,0:T(8,128)(2,1)} %param.33, bf16[768,2304]{1,0:T(8,128)(2,1)} %param.32), kind=kOutput, calls=%fused_computation.17 | convolution fusion | flops 14509670400 | bytes 47972352 | tf_op jit(solution)/shard_map/dot_general | solution.py:55
  702.8 51.8 %reduce-scatter.13.cloned.1.call-done = f32[1024,4608]{1,0:T(8,128)} async-done(((f32[2048,4608]{1,0:T(8,128)}), f32[1024,4608]{1,0:T(8,128)}) %reduce-scatter.13.cloned.1.call-update) | async-done | bytes 18874384 | tf_op jit(solution)/shard_map/reduce_scatter | solution.py:54
  774.7 34.6 %all-gather.18.cloned.1.call-done = bf16[2048,4608]{1,0:T(8,128)(2,1)} async-done(((bf16[1024,4608]{1,0:T(8,128)(2,1)}), bf16[2048,4608]{1,0:T(8,128)(2,1)}) %all-gather.18.cloned.1.call-update) | async-done | bytes 18874384 | tf_op jit(solution)/shard_map/all_gather | solution.py:64
  809.3 21.2 fusion.15
  846.2 69.4 %reduce-scatter.19.cloned.1.call-done = f32[1024,768]{1,0:T(8,128)} async-done(((f32[2048,768]{1,0:T(8,128)}), f32[1024,768]{1,0:T(8,128)}) %reduce-scatter.19.cloned.1.call-update) | async-done | bytes 3145744 | tf_op jit(solution)/shard_map/reduce_scatter | solution.py:65
  921.2 74.2 %reduce-scatter.15.cloned.1.call-done = f32[1024,768]{1,0:T(8,128)} async-done(((f32[2048,768]{1,0:T(8,128)}), f32[1024,768]{1,0:T(8,128)}) %reduce-scatter.15.cloned.1.call-update) | async-done | bytes 3145744 | tf_op jit(solution)/shard_map/reduce_scatter | solution.py:65
  1001.1 45.0 %all-gather.20.cloned.1.call-done = bf16[2048,768]{1,0:T(8,128)(2,1)} async-done(((bf16[1024,768]{1,0:T(8,128)(2,1)}), bf16[2048,768]{1,0:T(8,128)(2,1)}) %all-gather.20.cloned.1.call-update) | async-done | bytes 3145744 | tf_op jit(solution)/shard_map/all_gather | solution.py:53
  1088.7 16.7 slice.642
  1105.4 16.7 slice.649
  1164.7 16.6 slice.644
  1359.0 17.2 slice.718
  1396.1 32.7 %rev.2 = f32[1,1024,1024]{2,1,0:T(8,128)} reverse(f32[1,1024,1024]{2,1,0:T(8,128)} %add.630), dimensions={1} | reverse | bytes 8388608 | tf_op jit(solution)/shard_map/rev | solution.py:189
  1460.7 18.5 multiply_reduce_fusion.3
  1483.7 20.0 all-gather.22.cloned.1.call-done
  1579.3 64.6 %all-reduce.45 = (f32[4,1024]{1,0:T(4,128)}, f32[1024]{0:T(1024)}, f32[1024]{0:T(1024)}, f32[1024]{0:T(1024)}, f32[1024]{0:T(1024)}) all-reduce(f32[4,1024]{1,0:T(4,128)S(1)} %pad_maximum_fusion.18, f32[1024]{0:T(1024)S(1)} %get-tuple-element.60, ...), channel_id=1, replica_groups=mesh['dp'=8,'rows'=2,'cols'=2] {'dp','rows'}, use_global_device_ids=true, to_apply=%region_25.26 | all-reduce | flops 8192 | bytes 65536 | tf_op jit(solution)/shard_map/psum | solution.py:255
  1654.8 41.5 %all-reduce.44 = (f32[768]{0:T(1024)}, f32[768]{0:T(1024)}) all-reduce(f32[768]{0:T(1024)S(1)} %get-tuple-element.58, f32[768]{0:T(1024)S(1)} %copy-done.50), channel_id=1, replica_groups=mesh['dp'=8,'rows'=2,'cols'=2] {'dp','cols'}, use_global_device_ids=true, to_apply=%region_18.19 | all-reduce | flops 1536 | bytes 12288 | tf_op jit(solution)/shard_map/psum | solution.py:267
  1696.4 379.0 %all-reduce.53.cloned.1.call-done = (bf16[768,1024]{1,0:T(8,128)(2,1)}, bf16[768,1024]{1,0:T(8,128)(2,1)}, bf16[768,1024]{1,0:T(8,128)(2,1)}, bf16[768,2304]{1,0...) async-done(((bf16[768,1024]{1,0:T(8,128)(2,1)}, bf16[768,1024]{1,0:T(8,128)(2,1)}, bf16[768,1024]{1,0:T(8,128)(2,1)}, bf16[768,2304]{1,0:T(8,128)(2,1)}, ...) | async-done | bytes 15335440 | tf_op jit(solution)/shard_map/psum | solution.py:248
  2094.3 78.0 %all-reduce.51.cloned.1.call-done = (f32[8,128,128]{2,1,0:T(8,128)}, f32[8,128,128]{2,1,0:T(8,128)}) async-done(((f32[8,128,128]{2,1,0:T(8,128)}, f32[8,128,128]{2,1,0:T(8,128)}), (f32[8,128,128]{2,1,0:T(8,128)}, f32[8,128,128]{2,1,0:T(8,128)})) %all-reduce.51.cloned.1.call-update) | async-done | bytes 1048592 | tf_op jit(solution)/shard_map/psum | solution.py:255
  (510 shorter events, 906.9 us)
Async XLA Ops:
  7.2 617.0 %copy-start = (bf16[768,2304]{1,0:T(8,128)(2,1)S(1)}, bf16[768,2304]{1,0:T(8,128)(2,1)}, u32[]{:S(2)}) copy-start(bf16[768,2304]{1,0:T(8,128)(2,1)} %param.34) | copy-start | bytes 10616836
  7.2 58.4 %all-gather.10.cloned.1.call-start = ((), (), s32[]{:S(2)}) async-start(), calls=%async_computation.8 | async-start | bytes 4718592 | tf_op jit(solution)/shard_map/all_gather | solution.py:53
  18.0 86.7 %reduce-scatter.9.cloned.1.call-start = ((), (), s32[]{:S(2)}) async-start(), calls=%async_computation.9 | async-start | bytes 25165824 | tf_op jit(solution)/shard_map/reduce_scatter | solution.py:54
  78.2 411.8 %all-gather.24.cloned.1.call-start = ((), (), s32[]{:S(2)}) async-start(), calls=%async_computation.23 | async-start | bytes 6291456 | tf_op jit(solution)/shard_map/all_gather | solution.py:64
  474.9 102.3 %reduce-scatter.11.cloned.1.call-start = ((), (), s32[]{:S(2)}) async-start(), calls=%async_computation.10 | async-start | bytes 9437184 | tf_op jit(solution)/shard_map/reduce_scatter | solution.py:65
  498.9 125.3 %all-gather.16.cloned.1.call-start = ((), (), s32[]{:S(2)}) async-start(), calls=%async_computation.15 | async-start | bytes 4718592 | tf_op jit(solution)/shard_map/all_gather | solution.py:53
  504.5 79.6 %copy-start.48 = (f32[768]{0:T(1024)S(1)}, f32[768]{0:T(1024)}, u32[]{:S(2)}) copy-start(f32[768]{0:T(1024)} %param.31) | copy-start | bytes 9220
  504.5 166.6 %all-gather.12.cloned.1.call-start = ((), (), s32[]{:S(2)}) async-start(), calls=%async_computation.11 | async-start | bytes 4718592 | tf_op jit(solution)/shard_map/all_gather | solution.py:53
  587.9 114.9 %reduce-scatter.17.cloned.1.call-start = ((), (), s32[]{:S(2)}) async-start(), calls=%async_computation.16 | async-start | bytes 28311552 | tf_op jit(solution)/shard_map/reduce_scatter | solution.py:54
  637.2 117.4 %reduce-scatter.13.cloned.1.call-start = ((), (), s32[]{:S(2)}) async-start(), calls=%async_computation.12 | async-start | bytes 56623104 | tf_op jit(solution)/shard_map/reduce_scatter | solution.py:54
  702.7 106.6 %all-gather.18.cloned.1.call-start = ((), (), s32[]{:S(2)}) async-start(), calls=%async_computation.17 | async-start | bytes 28311552 | tf_op jit(solution)/shard_map/all_gather | solution.py:64
  774.1 60.3 %all-gather.14.cloned.1.call-start = ((), (), s32[]{:S(2)}) async-start(), calls=%async_computation.13 | async-start | bytes 14155776 | tf_op jit(solution)/shard_map/all_gather | solution.py:64
  774.7 140.9 %reduce-scatter.19.cloned.1.call-start = ((), (), s32[]{:S(2)}) async-start(), calls=%async_computation.18 | async-start | bytes 9437184 | tf_op jit(solution)/shard_map/reduce_scatter | solution.py:65
  830.6 164.9 %reduce-scatter.15.cloned.1.call-start = ((), (), s32[]{:S(2)}) async-start(), calls=%async_computation.14 | async-start | bytes 9437184 | tf_op jit(solution)/shard_map/reduce_scatter | solution.py:65
  846.1 69.4 %copy-start.5 = (f32[1024,768]{1,0:T(8,128)S(1)}, f32[1024,768]{1,0:T(8,128)}, u32[]{:S(2)}) copy-start(f32[1024,768]{1,0:T(8,128)} %get-tuple-element.84) | copy-start | bytes 9437188
  846.1 200.0 %all-gather.20.cloned.1.call-start = ((), (), s32[]{:S(2)}) async-start(), calls=%async_computation.19 | async-start | bytes 4718592 | tf_op jit(solution)/shard_map/all_gather | solution.py:53
  1001.0 138.8 %reduce-scatter.21.cloned.1.call-start = ((), (), s32[]{:S(2)}) async-start(), calls=%async_computation.20 | async-start | bytes 12582912 | tf_op jit(solution)/shard_map/reduce_scatter | solution.py:54
  1055.3 448.5 %all-gather.22.cloned.1.call-start = ((), (), s32[]{:S(2)}) async-start(), calls=%async_computation.21 | async-start | bytes 12582912 | tf_op jit(solution)/shard_map/all_gather | solution.py:64
  1483.6 160.2 %reduce-scatter.23.cloned.1.call-start = ((), (), s32[]{:S(2)}) async-start(), calls=%async_computation.22 | async-start | bytes 9437184 | tf_op jit(solution)/shard_map/reduce_scatter | solution.py:65
  1515.0 560.4 %all-reduce.53.cloned.1.call-start = ((), (), s32[]{:S(2)}) async-start(), calls=%async_computation.25 | async-start | bytes 30670848 | tf_op jit(solution)/shard_map/psum | solution.py:248
  1571.2 601.1 %all-reduce.51.cloned.1.call-start = ((), (), s32[]{:S(2)}) async-start(), calls=%async_computation.24 | async-start | bytes 2097152 | tf_op jit(solution)/shard_map/psum | solution.py:255
  1577.5 66.4 %copy-start.30 = (f32[1024]{0:T(1024)S(1)}, f32[1024]{0:T(1024)}, u32[]{:S(2)}) copy-start(f32[1024]{0:T(1024)} %copy-done.29) | copy-start | bytes 12292
  1579.2 70.2 %copy-start.47 = (f32[1024]{0:T(1024)S(1)}, f32[1024]{0:T(1024)}, u32[]{:S(2)}) copy-start(f32[1024]{0:T(1024)} %copy-done.46) | copy-start | bytes 12292
  2090.2 85.8 %copy-start.1 = (bf16[768,2304]{1,0:T(8,128)(2,1)S(1)}, bf16[768,2304]{1,0:T(8,128)(2,1)}, u32[]{:S(2)}) copy-start(bf16[768,2304]{1,0:T(8,128)(2,1)} %param.34) | copy-start | bytes 10616836
  (74 other events, 1154.6 us)
Sparse Core Ops, SparseCore 0:
  18.1 47.4 all-gather.9
  78.3 26.2 reduce-scatter.8
  475.1 14.8 all-gather.23
  499.0 78.2 reduce-scatter.10
  579.2 44.9 all-gather.15
  626.2 44.9 all-gather.11
  673.4 28.2 reduce-scatter.16
  704.0 50.5 reduce-scatter.12
  774.2 35.1 all-gather.17
  811.3 23.0 all-gather.13
  837.3 78.2 reduce-scatter.18
  918.4 77.0 reduce-scatter.14
  1001.1 44.9 all-gather.19
  1055.4 16.8 reduce-scatter.20
  1483.8 19.9 all-gather.21
  1515.1 78.2 reduce-scatter.22
  1599.3 476.0 all-reduce.52
  2079.9 92.3 all-reduce.50
where the time goes:
time: 2200 us; the launch traced here: 2180 us
  waiting for transfers between devices  986 us (45%)
  local copies, waits for them, and re-layouts  617 us (28%)
  other arithmetic  252 us (11%)
  matrix products  195 us (9%)
  blocking collectives  116 us (5%)
    psum x1, waiting for transfers between devices, body(): lax.psum(grad_rec_weight.astype(jnp.bfloat16), 'dp').astype(jnp.float32)  379 us
    slice x66, local copies, waits for them, and re-layouts, body(): lax.associative_scan(linear_step, (decay_next, grad_state), reverse=True,...  234 us
    reduce_scatter x4, waiting for transfers between devices, rows_to_cols(): lax.psum_scatter(jnp.dot(gathered, weight, preferred_element_type=jnp.flo...  216 us
    slice x60, local copies, waits for them, and re-layouts, body(): state = lax.associative_scan(linear_step, (decay, drive), axis=1)[1]  172 us
    all_gather x4, waiting for transfers between devices, cols_to_rows(): gathered = lax.all_gather(activation, 'cols', axis=0, tiled=True)  163 us
    pad x18, local copies, waits for them, and re-layouts, body(): state = lax.associative_scan(linear_step, (decay, drive), axis=1)[1]  83.3 us
    psum x1, waiting for transfers between devices, body(): lax.psum((grad_conv_weight, grad_conv_bias, grad_recur_weight, grad_recur...  78 us
    reduce_scatter x4, waiting for transfers between devices, cols_to_rows(): lax.psum_scatter(jnp.dot(gathered, weight, preferred_element_type=jnp.flo...  76.1 us
  transfers between devices with their start and end apart: 18, of which 15 were waited for; matrix products, arithmetic and copies ran while one was open for 12% of the time, Pallas kernels for 0%

commit v1 on v0

v1 whole, which is shorter than its diff:
```python
import functools
import math

import jax
import jax.numpy as jnp
from jax import lax
from jax.experimental import pallas as pl
from jax.experimental.pallas import tpu as pltpu
from jax.sharding import PartitionSpec as P

D = 1536
KCONV = 4
LEN = 1024
EPS = 1e-06
GATE_SCALE = 8.0
TANH_COEF = math.sqrt(2.0 / math.pi)
CUBIC_COEF = 0.044715
F32 = jnp.float32
BF16 = jnp.bfloat16
MIB = 1024 * 1024


def swap(value, axis):
    return lax.ppermute(value, axis, [(0, 1), (1, 0)])


def dot(left, right):
    return lax.dot_general(left, right, (((1,), (0,)), ((), ())), preferred_element_type=F32)


def dot_nt(left, right):
    return lax.dot_general(left, right, (((1,), (1,)), ((), ())), preferred_element_type=F32)


def dot_tn(left, right):
    return lax.dot_general(left, right, (((0,), (0,)), ((), ())), preferred_element_type=F32)


def gelu_act(values):
    inner_arg = TANH_COEF * (values + CUBIC_COEF * values * values * values)
    return 0.5 * values * (1.0 + jnp.tanh(inner_arg))


def gelu_pair(values):
    square = values * values
    tanh_val = jnp.tanh(values * (TANH_COEF + (TANH_COEF * CUBIC_COEF) * square))
    half_up = 0.5 + 0.5 * tanh_val
    slope = half_up + 0.5 * values * (1.0 - tanh_val * tanh_val) * (
        TANH_COEF + (3.0 * TANH_COEF * CUBIC_COEF) * square
    )
    return (values * half_up, slope)


def decay_terms(recur_gate, soft_decay):
    u = (2.0 * GATE_SCALE) * recur_gate * soft_decay
    decay = jnp.exp(-0.5 * u)
    series = u * (
        1.0
        - u
        * (0.5 - u * (1.0 / 6 - u * (1.0 / 24 - u * (1.0 / 120 - u * (1.0 / 720)))))
    )
    em = jnp.where(u < 0.25, series, 1.0 - decay * decay)
    return (decay, em)


def scan_tile(decay, drive, row):
    for shift in (1, 2, 4):
        keep = row >= shift
        before_a = jnp.where(keep, pltpu.roll(decay, shift, 0), 1.0)
        before_b = jnp.where(keep, pltpu.roll(drive, shift, 0), 0.0)
        drive = decay * before_b + drive
        decay = decay * before_a
    return (decay, drive)


def scan_tile_back(decay, drive, row):
    for shift in (1, 2, 4):
        keep = row < 8 - shift
        after_a = jnp.where(keep, pltpu.roll(decay, 8 - shift, 0), 1.0)
        after_b = jnp.where(keep, pltpu.roll(drive, 8 - shift, 0), 0.0)
        drive = decay * after_b + drive
        decay = decay * after_a
    return (decay, drive)


def rec_forward_kernel(
    chunk, width,
    n1, wr0, wr1, wg0, wg1, gw, cw, cb, rb, ib, sp, ow0, ow1,
    rec_o, gate_o, cl_o, r_o, i_o, st_o, br_o, mix_o,
    halo, carry, recpad, pre,
):
    heads = width // 128
    half = wr0.shape[0]

    @pl.when(pl.program_id(0) == 0)
    def _():
        halo[...] = jnp.zeros_like(halo)
        carry[...] = jnp.zeros_like(carry)

    low0 = n1[:, :half]
    low1 = n1[:, half:]
    rec = dot(low0, wr0[...]) + dot(low1, wr1[...])
    recpad[0:8, :] = halo[...]
    recpad[8:, :] = rec
    halo[...] = rec[chunk - 8 :, :]
    rec_o[...] = rec
    gate_o[...] = dot(low0, wg0[...]) + dot(low1, wg1[...])

    def conv_step(i, _):
        base = pl.multiple_of(i * 16, 16)
        for h in range(heads):
            sl = slice(h * 128, (h + 1) * 128)
            window = recpad[pl.ds(base, 24), sl]
            out = cb[:, sl] + cw[0:1, sl] * window[8:]
            for k in range(1, KCONV):
                out = out + cw[k : k + 1, sl] * pltpu.roll(window, k, 0)[8:]
            cl_o[pl.ds(base, 16), sl] = out.astype(BF16)
        return 0

    lax.fori_loop(0, chunk // 16, conv_step, 0)
    for h in range(heads):
        pre[:, h * 256 : (h + 1) * 256] = dot(cl_o[:, h * 128 : (h + 1) * 128], gw[h])
    row = lax.broadcasted_iota(jnp.int32, (8, 128), 0)

    def main_step(i, _):
        base = pl.multiple_of(i * 16, 16)
        rows = pl.ds(base, 16)
        for h in range(heads):
            sl = slice(h * 128, (h + 1) * 128)
            r = jax.nn.sigmoid(pre[rows, h * 256 : h * 256 + 128] + rb[:, sl])
            g = jax.nn.sigmoid(pre[rows, h * 256 + 128 : (h + 1) * 256] + ib[:, sl])
            conv = cl_o[rows, sl].astype(F32)
            decay, em = decay_terms(r, sp[:, sl])
            drive = jnp.sqrt(em) * g * conv
            r_o[rows, sl] = r
            i_o[rows, sl] = g
            held = carry[0:1, sl]
            parts = []
            for p in range(2):
                a, b = scan_tile(decay[p * 8 : p * 8 + 8], drive[p * 8 : p * 8 + 8], row)
                state = a * held + b
                held = state[7:8]
                parts.append(state)
            carry[0:1, sl] = held
            state = jnp.concatenate(parts, axis=0)
            st_o[rows, sl] = state
            br_o[rows, sl] = (state * gelu_act(gate_o[rows, sl])).astype(BF16)
        return 0

    lax.fori_loop(0, chunk // 16, main_step, 0)
    branch = br_o[...]
    mix_o[:, :half] = dot_nt(branch, ow0[...]).astype(BF16)
    mix_o[:, half:] = dot_nt(branch, ow1[...]).astype(BF16)


def rec_forward(n1, wr, wg, gw, cw, cb, rb, ib, sp, ow, chunk=256):
    tokens = n1.shape[0]
    half, width = wr[0].shape
    heads = width // 128
    row_block = lambda cols: pl.BlockSpec((chunk, cols), lambda i: (i, 0))
    whole = lambda shape: pl.BlockSpec(
        shape, lambda i: (0,) * len(shape), pipeline_mode=pl.Buffered(1)
    )
    f32 = jax.ShapeDtypeStruct((tokens, width), F32)
    low = jax.ShapeDtypeStruct((tokens, width), BF16)
    return pl.pallas_call(
        functools.partial(rec_forward_kernel, chunk, width),
        grid=(tokens // chunk,),
        in_specs=[row_block(2 * half)]
        + [whole((half, width))] * 4
        + [whole((heads, 128, 256)), whole((KCONV, width))]
        + [whole((1, width))] * 4
        + [whole((half, width))] * 2,
        out_specs=[row_block(width)] * 7 + [row_block(2 * half)],
        out_shape=[f32, f32, low, f32, f32, f32, low,
                   jax.ShapeDtypeStruct((tokens, 2 * half), BF16)],
        scratch_shapes=[
            pltpu.VMEM((8, width), F32),
            pltpu.VMEM((8, width), F32),
            pltpu.VMEM((chunk + 8, width), F32),
            pltpu.VMEM((chunk, 2 * width), F32),
        ],
        compiler_params=pltpu.CompilerParams(vmem_limit_bytes=56 * MIB),
        name="recurrent_forward",
    )(n1, wr[0], wr[1], wg[0], wg[1], gw, cw, cb, rb, ib, sp, ow[0], ow[1])


def ffn_kernel(
    tile,
    n2, n2t, cot, cott, wg0, wg1, wu0, wu1, wd0, wd1,
    out_o, gn2_o, gg0, gg1, gu0, gu1, gd0, gd1,
    out_acc, gn2_acc, hid_s, ga_s, gb_s,
):
    step = pl.program_id(0)
    tokens = n2.shape[0]
    half = wg0.shape[0]

    @pl.when(step == 0)
    def _():
        out_acc[...] = jnp.zeros_like(out_acc)
        gn2_acc[...] = jnp.zeros_like(gn2_acc)

    def tile_step(i, _):
        rows = pl.ds(pl.multiple_of(i * tile, tile), tile)
        n0, n1 = n2[rows, :half], n2[rows, half:]
        c0, c1 = cot[rows, :half], cot[rows, half:]
        a = dot(n0, wg0[...]) + dot(n1, wg1[...])
        b = dot(n0, wu0[...]) + dot(n1, wu1[...])
        gh = dot(c0, wd0[...]) + dot(c1, wd1[...])
        act, slope = gelu_pair(a)
        hidden = (act * b).astype(BF16)
        ga = (gh * b * slope).astype(BF16)
        gb = (gh * act).astype(BF16)
        hid_s[rows, :] = hidden
        ga_s[rows, :] = ga
        gb_s[rows, :] = gb
        out_acc[rows, :half] += dot_nt(hidden, wd0[...])
        out_acc[rows, half:] += dot_nt(hidden, wd1[...])
        gn2_acc[rows, :half] += dot_nt(ga, wg0[...]) + dot_nt(gb, wu0[...])
        gn2_acc[rows, half:] += dot_nt(ga, wg1[...]) + dot_nt(gb, wu1[...])
        return 0

    lax.fori_loop(0, tokens // tile, tile_step, 0)
    gg0[...] = dot(n2t[:half], ga_s[...]).astype(BF16)
    gg1[...] = dot(n2t[half:], ga_s[...]).astype(BF16)
    gu0[...] = dot(n2t[:half], gb_s[...]).astype(BF16)
    gu1[...] = dot(n2t[half:], gb_s[...]).astype(BF16)
    gd0[...] = dot(cott[:half], hid_s[...]).astype(BF16)
    gd1[...] = dot(cott[half:], hid_s[...]).astype(BF16)

    @pl.when(step == pl.num_programs(0) - 1)
    def _():
        out_o[...] = out_acc[...].astype(BF16)
        gn2_o[...] = gn2_acc[...].astype(BF16)


def ffn(n2, n2t, cot, cott, wg, wu, wd, block=256, tile=256):
    tokens, wide = n2.shape
    half, width = wg[0].shape
    whole = lambda shape: pl.BlockSpec(shape, lambda i: (0, 0), pipeline_mode=pl.Buffered(1))
    col_block = pl.BlockSpec((half, block), lambda i: (0, i))
    act = jax.ShapeDtypeStruct((tokens, wide), BF16)
    grad = jax.ShapeDtypeStruct((half, width), BF16)
    return pl.pallas_call(
        functools.partial(ffn_kernel, tile),
        grid=(width // block,),
        in_specs=[whole((tokens, wide)), whole((wide, tokens))] * 2 + [col_block] * 6,
        out_specs=[whole((tokens, wide))] * 2 + [col_block] * 6,
        out_shape=[act, act] + [grad] * 6,
        scratch_shapes=[
            pltpu.VMEM((tokens, wide), F32),
            pltpu.VMEM((tokens, wide), F32),
            pltpu.VMEM((tokens, block), BF16),
            pltpu.VMEM((tokens, block), BF16),
            pltpu.VMEM((tokens, block), BF16),
        ],
        compiler_params=pltpu.CompilerParams(vmem_limit_bytes=60 * MIB),
        name="ffn",
    )(n2, n2t, cot, cott, wg[0], wg[1], wu[0], wu[1], wd[0], wd[1])


def rec_backward_kernel(
    tile,
    g1, g1t, n1t, st, gate, r_in, i_in, cl, rec, br, ow0, ow1, wr0, wr1, wg0, wg1, gw, cw, sp,
    gn1_o, go0, go1, gr0, gr1, gg0, gg1, ggw, gvec,
    acc, gb_s, gc_s, ggp_s, grp_s, gip_s, grec_s, sums,
):
    step = pl.program_id(0)
    tokens, block = gb_s.shape
    heads = block // 128
    half = ow0.shape[0]
    tiles = tokens // tile
    subs = tile // 8

    @pl.when(step == 0)
    def _():
        acc[...] = jnp.zeros_like(acc)

    gb_s[...] = dot(g1[:, :half], ow0[...]) + dot(g1[:, half:], ow1[...])
    go0[...] = dot(g1t[:half], br[...]).astype(BF16)
    go1[...] = dot(g1t[half:], br[...]).astype(BF16)
    sums[...] = jnp.zeros_like(sums)
    row = lax.broadcasted_iota(jnp.int32, (8, 128), 0)

    def back_step(j, held):
        i = tiles - 1 - j
        base = pl.multiple_of(i * tile, tile)
        rows = pl.ds(base, tile)
        before = pl.ds(pl.multiple_of(jnp.maximum(base - 8, 0), 8), 8)
        out = []
        for h in range(heads):
            sl = slice(h * 128, (h + 1) * 128)
            later_decay, later_carried = held[h]
            grad_branch = gb_s[rows, sl]
            act, slope = gelu_pair(gate[rows, sl])
            state = st[rows, sl]
            ggp_s[rows, sl] = (grad_branch * state * slope).astype(BF16)
            grad_state = grad_branch * act
            r = r_in[rows, sl]
            soft = sp[:, sl]
            decay, em = decay_terms(r, soft)
            parts = [None] * subs
            for p in range(subs - 1, -1, -1):
                own = decay[p * 8 : p * 8 + 8]
                after = jnp.where(row == 7, later_decay, pltpu.roll(own, 7, 0))
                a, b = scan_tile_back(after, grad_state[p * 8 : p * 8 + 8], row)
                carried = a * later_carried + b
                later_decay = own[0:1]
                later_carried = carried[0:1]
                parts[p] = carried
            out.append((later_decay, later_carried))
            carried = jnp.concatenate(parts, axis=0)
            edge = jnp.where(i > 0, st[before, sl][7:8], 0.0)
            prev = []
            for p in range(subs):
                prev.append(jnp.where(row == 0, edge, pltpu.roll(state[p * 8 : p * 8 + 8], 1, 0)))
                edge = state[p * 8 + 7 : p * 8 + 8]
            prev = jnp.concatenate(prev, axis=0)
            g = i_in[rows, sl]
            conv = cl[rows, sl].astype(F32)
            scaling = jnp.sqrt(em)
            gated = g * conv
            grad_log = carried * (prev * decay - gated * (decay * decay) / scaling)
            grad_soft = grad_log * (-GATE_SCALE * r)
            grp = grad_soft * soft * (1.0 - r)
            cs = carried * scaling
            gc_s[rows, sl] = cs * g
            gip = cs * gated * (1.0 - g)
            grp_s[rows, sl] = grp.astype(BF16)
            gip_s[rows, sl] = gip.astype(BF16)
            for n, term in enumerate((grp, gip, grad_soft)):
                total = term[0:8]
                for p in range(1, subs):
                    total = total + term[p * 8 : p * 8 + 8]
                sums[n * 8 : n * 8 + 8, sl] += total
        return tuple(out)

    zero = jnp.zeros((1, 128), F32)
    lax.fori_loop(0, tiles, back_step, tuple((zero, zero) for _ in range(heads)))
    for h in range(heads):
        sl = slice(h * 128, (h + 1) * 128)
        low = cl[:, sl]
        ggw[h, :, 0:128] = dot_tn(low, grp_s[:, sl])
        ggw[h, :, 128:256] = dot_tn(low, gip_s[:, sl])
        gc_s[:, sl] += dot_nt(grp_s[:, sl], gw[h, :, 0:128]) + dot_nt(gip_s[:, sl], gw[h, :, 128:256])

    def conv_step(j, held):
        i = tiles - 1 - j
        base = pl.multiple_of(i * tile, tile)
        rows = pl.ds(base, tile)
        before = pl.ds(pl.multiple_of(jnp.maximum(base - 8, 0), 8), 8)
        out = []
        for h in range(heads):
            sl = slice(h * 128, (h + 1) * 128)
            grad_conv = gc_s[rows, sl]
            window = jnp.concatenate([grad_conv, held[h]], axis=0)
            out.append(grad_conv[0:8])
            grad_rec = cw[0:1, sl] * grad_conv
            for k in range(1, KCONV):
                grad_rec = grad_rec + cw[k : k + 1, sl] * pltpu.roll(window, tile + 8 - k, 0)[:tile]
            grec_s[rows, sl] = grad_rec.astype(BF16)
            edge = jnp.where(i > 0, rec[before, sl], 0.0)
            past = jnp.concatenate([edge, rec[rows, sl]], axis=0)
            terms = [grad_conv * past[8:]]
            for k in range(1, KCONV):
                terms.append(grad_conv * pltpu.roll(past, k, 0)[8:])
            terms.append(grad_conv)
            for n, term in enumerate(terms):
                total = term[0:8]
                for p in range(1, subs):
                    total = total + term[p * 8 : p * 8 + 8]
                sums[24 + n * 8 : 32 + n * 8, sl] += total
        return tuple(out)

    lax.fori_loop(0, tiles, conv_step, tuple(jnp.zeros((8, 128), F32) for _ in range(heads)))
    for n in range(8):
        gvec[n : n + 1, :] = jnp.sum(sums[n * 8 : n * 8 + 8, :], axis=0, keepdims=True)
    grad_rec = grec_s[...]
    grad_gate = ggp_s[...]
    gr0[...] = dot(n1t[:half], grad_rec).astype(BF16)
    gr1[...] = dot(n1t[half:], grad_rec).astype(BF16)
    gg0[...] = dot(n1t[:half], grad_gate).astype(BF16)
    gg1[...] = dot(n1t[half:], grad_gate).astype(BF16)
    acc[:, :half] += dot_nt(grad_rec, wr0[...]) + dot_nt(grad_gate, wg0[...])
    acc[:, half:] += dot_nt(grad_rec, wr1[...]) + dot_nt(grad_gate, wg1[...])

    @pl.when(step == pl.num_programs(0) - 1)
    def _():
        gn1_o[...] = acc[...].astype(BF16)


def rec_backward(g1, g1t, n1t, st, gate, r, g, cl, rec, br, ow, wr, wg, gw, cw, sp, block=256, tile=32):
    tokens, wide = g1.shape
    half, width = wr[0].shape
    heads = block // 128
    whole = lambda shape: pl.BlockSpec(shape, lambda i: (0, 0), pipeline_mode=pl.Buffered(1))
    act = pl.BlockSpec((tokens, block), lambda i: (0, i))
    weight = pl.BlockSpec((half, block), lambda i: (0, i))
    thin = lambda n: pl.BlockSpec((n, block), lambda i: (0, i))
    gate_block = pl.BlockSpec((heads, 128, 256), lambda i: (i, 0, 0))
    grad = jax.ShapeDtypeStruct((half, width), BF16)
    return pl.pallas_call(
        functools.partial(rec_backward_kernel, tile),
        grid=(width // block,),
        in_specs=[whole((tokens, wide)), whole((wide, tokens)), whole((wide, tokens))]
        + [act] * 7
        + [weight] * 6
        + [gate_block, thin(KCONV), thin(1)],
        out_specs=[whole((tokens, wide))] + [weight] * 6 + [gate_block, thin(8)],
        out_shape=[jax.ShapeDtypeStruct((tokens, wide), BF16)]
        + [grad] * 6
        + [
            jax.ShapeDtypeStruct((width // 128, 128, 256), F32),
            jax.ShapeDtypeStruct((8, width), F32),
        ],
        scratch_shapes=[
            pltpu.VMEM((tokens, wide), F32),
            pltpu.VMEM((tokens, block), F32),
            pltpu.VMEM((tokens, block), F32),
            pltpu.VMEM((tokens, block), BF16),
            pltpu.VMEM((tokens, block), BF16),
            pltpu.VMEM((tokens, block), BF16),
            pltpu.VMEM((tokens, block), BF16),
            pltpu.VMEM((64, block), F32),
        ],
        compiler_params=pltpu.CompilerParams(vmem_limit_bytes=60 * MIB),
        name="recurrent_backward",
    )(
        g1, g1t, n1t, st, gate, r, g, cl, rec, br,
        ow[0], ow[1], wr[0], wr[1], wg[0], wg[1], gw, cw, sp,
    )


def body(
    tokens, lengths, mix_gain, rec_weight, gate_weight, conv_weight, conv_bias,
    recur_weight, recur_bias, input_weight, input_bias, decay_param, out_weight,
    ffn_gain, ffn_gate, ffn_up, ffn_down, cotangent,
):
    at_row = lax.axis_index("rows")
    at_col = lax.axis_index("cols")
    diag = at_row == at_col
    half = tokens.shape[0]
    wide = 2 * half

    def to_sequence(own):
        other = swap(own, "cols")
        mine = jnp.where(diag, own, other)
        partner = swap(jnp.where(diag, other, own), "rows")
        return jnp.concatenate([mine, partner], axis=0)

    def from_sequence(whole):
        partner = swap(whole[:, half:], "rows")
        own = whole[:, :half]
        keep = jnp.where(diag, own, partner)
        give = jnp.where(diag, partner, own)
        return keep, swap(give, "cols")

    both = lambda weight: (weight, swap(weight, "rows"))
    gains = lambda gain: jnp.concatenate(both(gain))

    positions = jnp.arange(LEN, dtype=jnp.int32)
    live_core = (positions < lengths[at_row]).astype(BF16)
    live_chip = (positions < lengths[at_col]).astype(F32)

    xt = to_sequence(tokens)
    wr = both(rec_weight)
    wg = both(gate_weight)
    ow = both(out_weight)
    cott = to_sequence(cotangent) * live_core[None, :]
    fg = both(ffn_gate)
    fu = both(ffn_up)
    fd = both(ffn_down)
    gain_one = gains(mix_gain)
    gain_two = gains(ffn_gain)
    x = xt.T
    xf = x.astype(F32)
    scale_one = lax.rsqrt(jnp.mean(xf * xf, axis=1, keepdims=True) + EPS)
    n1 = (xf * scale_one * gain_one).astype(BF16)
    n1t = n1.T
    gw = jnp.concatenate([recur_weight, input_weight], axis=2)
    sp = jax.nn.softplus(-decay_param)[None, :]
    rec, gate, cl, r, g, st, br, mixed = rec_forward(
        n1, wr, wg, gw, conv_weight, conv_bias[None, :], recur_bias[None, :],
        input_bias[None, :], sp, ow,
    )
    res1 = xf + (mixed.astype(F32) + swap(mixed, "cols").astype(F32))
    scale_two = lax.rsqrt(jnp.mean(res1 * res1, axis=1, keepdims=True) + EPS)
    n2 = (res1 * scale_two * gain_two).astype(BF16)
    n2t = n2.T
    cot = cott.T
    ffn_out, gn2_part, gg0, gg1, gu0, gu1, gd0, gd1 = ffn(n2, n2t, cot, cott, fg, fu, fd)
    gn2 = gn2_part.astype(F32) + swap(gn2_part, "cols").astype(F32)
    grad_gain_two = jnp.sum(gn2 * res1 * scale_two, axis=0)
    weighted = gn2 * gain_two
    inner = jnp.sum(weighted * res1, axis=1, keepdims=True)
    grad_one = (
        cot.astype(F32)
        + scale_two * weighted
        - res1 * (scale_two * scale_two * scale_two * inner / wide)
    )
    g1 = grad_one.astype(BF16)
    g1t = g1.T

    def over_rows(own, other):
        return (own.astype(F32) + swap(other, "rows").astype(F32)).astype(BF16)

    sum_gate = lax.psum(over_rows(gg0, gg1), "dp").astype(F32)
    sum_up = lax.psum(over_rows(gu0, gu1), "dp").astype(F32)
    sum_down = lax.psum(over_rows(gd0, gd1), "dp").astype(F32)
    gn1_part, go0, go1, gr0, gr1, gt0, gt1, ggw, gvec = rec_backward(
        g1, g1t, n1t, st, gate, r, g, cl, rec, br, ow, wr, wg, gw, conv_weight, sp
    )
    sum_out = lax.psum(over_rows(go0, go1), "dp").astype(F32)
    sum_rec = lax.psum(over_rows(gr0, gr1), "dp").astype(F32)
    sum_gatew = lax.psum(over_rows(gt0, gt1), "dp").astype(F32)

    with_res = ffn_out.astype(F32) + jnp.where(diag, res1, 0.0)
    keep, came = from_sequence(with_res.astype(BF16))
    result = ((keep.astype(F32) + came.astype(F32)).T * live_chip[None, :]).astype(BF16)

    keep, came = from_sequence(gn1_part)
    gn1 = (keep.astype(F32) + came.astype(F32)).T
    g1_partner = swap(g1[:, half:], "rows")
    g1_here = jnp.where(diag, g1[:, :half], g1_partner).T.astype(F32)
    xh = tokens.astype(F32)
    squares = jnp.sum(xh * xh, axis=0)
    s_here = lax.rsqrt((squares + swap(squares, "rows")) / wide + EPS)[None, :]
    weighted = gn1 * mix_gain[:, None]
    inner = jnp.sum(weighted * xh, axis=0)
    inner = (inner + swap(inner, "rows"))[None, :]
    grad_tokens = (
        g1_here + s_here * weighted - xh * (s_here * s_here * s_here * inner / wide)
    ).astype(BF16)
    grad_gain_one = jnp.sum(gn1 * xh * s_here, axis=1)

    both_gain_two = grad_gain_two[:half] + swap(grad_gain_two[half:], "rows")
    small = lax.psum((gvec, ggw), ("dp", "rows"))
    vec, gates = small
    summed_gain = lax.psum(grad_gain_one, ("dp", "cols"))
    summed_gain_two = lax.psum(both_gain_two, "dp")
    grad_decay = vec[2] * -jax.nn.sigmoid(-decay_param)
    return (
        result,
        grad_tokens,
        summed_gain,
        sum_rec,
        sum_gatew,
        vec[3:7],
        vec[7],
        gates[:, :, :128],
        vec[0],
        gates[:, :, 128:],
        vec[1],
        grad_decay,
        sum_out,
        summed_gain_two,
        sum_gate,
        sum_up,
        sum_down,
    )


def solution(mesh):
    return jax.shard_map(
        body,
        mesh=mesh,
        in_specs=(
            P("rows", ("dp", "cols")),
            P("dp"),
            P("rows"),
            P("rows", "cols"),
            P("rows", "cols"),
            P(None, "cols"),
            P("cols"),
            P("cols", None, None),
            P("cols"),
            P("cols", None, None),
            P("cols"),
            P("cols"),
            P("rows", "cols"),
            P("rows"),
            P("rows", "cols"),
            P("rows", "cols"),
            P("rows", "cols"),
            P("rows", ("dp", "cols")),
        ),
        out_specs=(
            P("rows", ("dp", "cols")),
            P("rows", ("dp", "cols")),
            P("rows"),
            P("rows", "cols"),
            P("rows", "cols"),
            P(None, "cols"),
            P("cols"),
            P("cols", None, None),
            P("cols"),
            P("cols", None, None),
            P("cols"),
            P("cols"),
            P("rows", "cols"),
            P("rows"),
            P("rows", "cols"),
            P("rows", "cols"),
            P("rows", "cols"),
        ),
        check_vma=False,
    )
```

time: 2200 us -> 1030 us (0.47)
  local copies, waits for them, and re-layouts: 617 us -> 48.7 us
  waiting for transfers between devices: 986 us -> 548 us
  matrix products: 195 us -> 0 us
  Pallas kernels: 0 us -> 177 us
  other arithmetic: 252 us -> 98.2 us
    slice x128 -> x7, local copies, waits for them, and re-layouts: 410 us -> 6.66 us  [the longest x1 2.38 us: body(): gates[:, :, 128:]]
    reduce_scatter x8 -> x0, waiting for transfers between devices: 292 us -> none  [the longest x4 216 us: rows_to_cols(): lax.psum_scatter(jnp.dot(gathered, weight, preferred_element_type=jnp.flo...]
    all_gather x8 -> x0, waiting for transfers between devices: 236 us -> none  [the longest x4 163 us: cols_to_rows(): gathered = lax.all_gather(activation, 'cols', axis=0, tiled=True)]
    dot_general x20 -> x0, matrix products: 195 us -> none  [the longest x4 66.2 us: cols_to_rows(): jnp.dot(gathered, weight, preferred_element_type=jnp.float32)]
    pallas_call x0 -> x3, Pallas kernels: none -> 177 us  [the longest x1 89.4 us: ffn(): pl.pallas_call(functools.partial(ffn_kernel, tile), grid=(width // block,...]
    ppermute x0 -> x28, waiting for transfers between devices: none -> 152 us  [swap(): return lax.ppermute(value, axis, [(0, 1), (1, 0)])]
    pad x36 -> x0, local copies, waits for them, and re-layouts: 123 us -> none  [the longest x18 83.3 us: body(): state = lax.associative_scan(linear_step, (decay, drive), axis=1)[1]]
    psum x2, waiting for transfers between devices: 457 us -> 396 us  [the longest x1 396 us: body(): sum_rec = lax.psum(over_rows(gr0, gr1), 'dp').astype(F32)]
  transfers between devices with their start and end apart: 18 -> 30, of which waited for: 15 -> 7; matrix products, arithmetic and copies ran while one was open for 12% -> 11% of each run, Pallas kernels for 0% -> 9%
where the time goes in v1:
time: 1030 us
  waiting for transfers between devices  548 us (53%)
  Pallas kernels  177 us (17%)
  blocking collectives  123 us (12%)
  other arithmetic  98.2 us (10%)
  local copies, waits for them, and re-layouts  48.7 us (5%)
  starting transfers between devices  15.6 us (2%)
  between operations  14.9 us (1%)
    psum x1, waiting for transfers between devices, body(): sum_rec = lax.psum(over_rows(gr0, gr1), 'dp').astype(F32)  396 us
    ppermute x28, waiting for transfers between devices, swap(): return lax.ppermute(value, axis, [(0, 1), (1, 0)])  152 us
    pallas_call x1, Pallas kernels, ffn(): pl.pallas_call(functools.partial(ffn_kernel, tile), grid=(width // block,...  89.4 us
    psum x1, blocking collectives, body(): small = lax.psum((gvec, ggw), ('dp', 'rows'))  62.6 us
    pallas_call x1, Pallas kernels, rec_backward(): pl.pallas_call(functools.partial(rec_backward_kernel, tile), grid=(width...  55.5 us
    psum x1, blocking collectives, body(): summed_gain = lax.psum(grad_gain_one, ('dp', 'cols'))  42.2 us
    pallas_call x1, Pallas kernels, rec_forward(): pl.pallas_call(functools.partial(rec_forward_kernel, chunk, width), grid=...  32.6 us
  transfers between devices with their start and end apart: 30, of which 7 were waited for; matrix products, arithmetic and copies ran while one was open for 11% of the time, Pallas kernels for 9%

profile of v1, /device:TPU:0, one launch (start us, length us, event | category | flops | bytes accessed | tf_op | source)
XLA Modules:
  0.0 1025.7 jit_solution(354135797851358305)
XLA Ops:
  10.3 34.6 %collective-permute-done = bf16[768,1024]{1,0:T(8,128)(2,1)S(1)} collective-permute-done((bf16[768,1024]{1,0:T(8,128)(2,1)}, bf16[768,1024]{1,0:T(8,128)(2,1)S(1)}, u32[]{:S(2)}, u32[]{:S(2)}) %collective-permute-start) | collective-permute-done | bytes 1572896 | tf_op jit(solution)/shard_map/ppermute | solution.py:24
  56.8 4.6 copy.35.n1
  61.5 32.6 %recurrent_forward.1 = (f32[1024,1024]{1,0:T(8,128)}, f32[1024,1024]{1,0:T(8,128)}, bf16[1024,1024]{1,0:T(8,128)(2,1)}, f32[1024,1024]{1,0:T(8,128)}, f32[1024,1...) custom-call(bf16[1024,1536]{1,0:T(8,128)(2,1)} %copy.35.n1, ...), custom_call_target="tpu_custom_call" | custom-call | tf_op jit(solution)/shard_map/recurrent_forward/pallas_call | solution.py:166
  94.0 4.8 copy.36
  115.4 53.8 %collective-permute-done.6 = bf16[1024,1536]{0,1:T(8,128)(2,1)} collective-permute-done((bf16[1024,1536]{0,1:T(8,128)(2,1)}, bf16[1024,1536]{0,1:T(8,128)(2,1)}, u32[]{:S(2)}, u32[]{:S(2)}) %collective-permute-start.6) | collective-permute-done | bytes 3145760 | tf_op jit(solution)/shard_map/ppermute | solution.py:24
  179.9 5.0 fusion.26.n2t
  185.0 89.4 %ffn.1 = (bf16[1024,1536]{1,0:T(8,128)(2,1)}, bf16[1024,1536]{1,0:T(8,128)(2,1)}, bf16[768,2304]{1,0:T(8,128)(2,1)}, bf16[768,2304]{1,0:T(8,128)(2,1)}, bf16[768...) custom-call(bf16[1024,1536]{1,0:T(8,128)(2,1)} %copy.38.n2, ...), custom_call_target="tpu_custom_call" | custom-call | tf_op jit(solution)/shard_map/ffn/pallas_call | solution.py:244
  274.4 4.8 copy.41
  284.7 4.8 copy.40
  289.6 59.2 %collective-permute-done.15 = bf16[1024,1536]{0,1:T(8,128)(2,1)} collective-permute-done((bf16[1024,1536]{0,1:T(8,128)(2,1)}, bf16[1024,1536]{0,1:T(8,128)(2,1)}, u32[]{:S(2)}, u32[]{:S(2)}) %collective-permute-start.15) | collective-permute-done | bytes 3145760 | tf_op jit(solution)/shard_map/ppermute | solution.py:24
  348.8 5.9 multiply_reduce_fusion
  354.7 7.9 subtract_convert_fusion
  362.7 4.6 copy.43.g1
  367.3 55.5 %recurrent_backward.1 = (bf16[1024,1536]{1,0:T(8,128)(2,1)}, bf16[768,1024]{1,0:T(8,128)(2,1)}, bf16[768,1024]{1,0:T(8,128)(2,1)}, bf16[768,1024]{1,0:T(8,128)(2...) custom-call(bf16[1024,1536]{1,0:T(8,128)(2,1)} %copy.43.g1, ...), custom_call_target="tpu_custom_call" | custom-call | tf_op jit(solution)/shard_map/recurrent_backward/pallas_call | solution.py:402
  423.6 4.8 add_convert_fusion.2
  428.4 5.1 add_convert_fusion.1
  433.5 5.0 add_convert_fusion
  444.1 5.0 copy.44
  462.0 62.6 %psum.73 = f32[8,1024]{1,0:T(8,128)S(1)} all-reduce(f32[8,1024]{1,0:T(8,128)S(1)} %copy-done.34), channel_id=1, replica_groups=mesh['dp'=8,'rows'=2,'cols'=2] {'dp','rows'}, use_global_device_ids=true, to_apply=%region_9.10 | all-reduce | flops 8192 | bytes 65536 | tf_op jit(solution)/shard_map/psum | solution.py:537
  526.4 18.2 %psum.76 = f32[768]{0:T(1024)} all-reduce(f32[768]{0:T(1024)S(1)} %slice_add_fusion), channel_id=1, replica_groups=mesh['dp'=8,'rows'=2,'cols'=2] {'dp'}, use_global_device_ids=true, to_apply=%region_13.14 | all-reduce | flops 768 | bytes 6144 | tf_op jit(solution)/shard_map/psum | solution.py:540
  547.0 4.9 fusion.14
  555.5 42.2 %psum.70 = f32[768]{0:T(1024)} all-reduce(f32[768]{0:T(1024)S(1)} %get-tuple-element.69), channel_id=1, replica_groups=mesh['dp'=8,'rows'=2,'cols'=2] {'dp','cols'}, use_global_device_ids=true, to_apply=%region_6.7 | all-reduce | flops 768 | bytes 6144 | tf_op jit(solution)/shard_map/psum | solution.py:539
  597.8 5.6 fusion.12
  603.4 395.7 %all-reduce.6.cloned.1.call-done = (bf16[768,1024]{1,0:T(8,128)(2,1)}, bf16[768,1024]{1,0:T(8,128)(2,1)}, bf16[768,1024]{1,0:T(8,128)(2,1)}, bf16[768,2304]{1,0:...) async-done(((bf16[768,1024]{1,0:T(8,128)(2,1)}, bf16[768,1024]{1,0:T(8,128)(2,1)}, bf16[768,1024]{1,0:T(8,128)(2,1)}, bf16[768,2304]{1,0:T(8,128)(2,1)}, ...) | async-done | bytes 15335440 | tf_op jit(solution)/shard_map/psum | solution.py:514
  (186 shorter events, 94.3 us)
Async XLA Ops:
  7.2 537.4 %all-reduce.4.cloned.1.call-start = ((), (), s32[]{:S(2)}) async-start(), calls=%async_computation | async-start | bytes 2097152 | tf_op jit(solution)/shard_map/psum | solution.py:537
  7.2 37.6 %collective-permute-start = (bf16[768,1024]{1,0:T(8,128)(2,1)}, bf16[768,1024]{1,0:T(8,128)(2,1)S(1)}, u32[]{:S(2)}, u32[]{:S(2)}) collective-permute-start(bf16[768,1024]{1,0:T(8,128)(2,1)} %param.18), channel_id=1, source_target_pairs={{0,1},{1,0},{2,3},{3,2},{4,5},{5,4},{6,7},{7,6},{8,9},{9,8},{10,11... | collective-permute-start | bytes 4718600 | tf_op jit(solution)/shard_map/ppermute | solution.py:24
  48.1 13.3 %collective-permute-start.3 = (bf16[768,1024]{1,0:T(8,128)(2,1)}, bf16[768,1024]{1,0:T(8,128)(2,1)}, u32[]{:S(2)}, u32[]{:S(2)}) collective-permute-start(bf16[768,1024]{1,0:T(8,128)(2,1)} %wr0.3), channel_id=1, source_target_pairs={{0,2},{2,0},{1,3},{3,1},{4,6},{6,4},{5,7},{7,5},{8,10},{10,8},{9,1... | collective-permute-start | bytes 4718600 | tf_op jit(solution)/shard_map/ppermute | solution.py:24
  48.2 13.3 %collective-permute-start.4 = (bf16[768,1024]{1,0:T(8,128)(2,1)}, bf16[768,1024]{1,0:T(8,128)(2,1)}, u32[]{:S(2)}, u32[]{:S(2)}) collective-permute-start(bf16[768,1024]{1,0:T(8,128)(2,1)} %wg0.5), channel_id=1, source_target_pairs={{0,2},{2,0},{1,3},{3,1},{4,6},{6,4},{5,7},{7,5},{8,10},{10,8},{9,1... | collective-permute-start | bytes 4718600 | tf_op jit(solution)/shard_map/ppermute | solution.py:24
  48.6 12.8 %collective-permute-start.5 = (bf16[768,1024]{1,0:T(8,128)(2,1)}, bf16[768,1024]{1,0:T(8,128)(2,1)}, u32[]{:S(2)}, u32[]{:S(2)}) collective-permute-start(bf16[768,1024]{1,0:T(8,128)(2,1)} %ow0.3), channel_id=1, source_target_pairs={{0,2},{2,0},{1,3},{3,1},{4,6},{6,4},{5,7},{7,5},{8,10},{10,8},{9,1... | collective-permute-start | bytes 4718600 | tf_op jit(solution)/shard_map/ppermute | solution.py:24
  50.8 49.8 %collective-permute-start.8 = (bf16[768,1024]{1,0:T(8,128)(2,1)}, bf16[768,1024]{1,0:T(8,128)(2,1)}, u32[]{:S(2)}, u32[]{:S(2)}) collective-permute-start(bf16[768,1024]{1,0:T(8,128)(2,1)} %param.35), channel_id=1, source_target_pairs={{0,1},{1,0},{2,3},{3,2},{4,5},{5,4},{6,7},{7,6},{8,9},{9,8},{10,11... | collective-permute-start | bytes 4718600 | tf_op jit(solution)/shard_map/ppermute | solution.py:24
  98.8 70.5 %collective-permute-start.6 = (bf16[1024,1536]{0,1:T(8,128)(2,1)}, bf16[1024,1536]{0,1:T(8,128)(2,1)}, u32[]{:S(2)}, u32[]{:S(2)}) collective-permute-start(bf16[1024,1536]{0,1:T(8,128)(2,1)} %copy.36), channel_id=1, source_target_pairs={{0,1},{1,0},{2,3},{3,2},{4,5},{5,4},{6,7},{7,6},{8,9},{9,8},{10,11... | collective-permute-start | bytes 9437192 | tf_op jit(solution)/shard_map/ppermute | solution.py:24
  103.8 81.1 %collective-permute-start.10 = (bf16[768,2304]{1,0:T(8,128)(2,1)}, bf16[768,2304]{1,0:T(8,128)(2,1)}, u32[]{:S(2)}, u32[]{:S(2)}) collective-permute-start(bf16[768,2304]{1,0:T(8,128)(2,1)} %wg0.4), channel_id=1, source_target_pairs={{0,2},{2,0},{1,3},{3,1},{4,6},{6,4},{5,7},{7,5},{8,10},{10,8},{9,1... | collective-permute-start | bytes 10616840 | tf_op jit(solution)/shard_map/ppermute | solution.py:24
  103.8 81.1 %collective-permute-start.11 = (bf16[768,2304]{1,0:T(8,128)(2,1)}, bf16[768,2304]{1,0:T(8,128)(2,1)}, u32[]{:S(2)}, u32[]{:S(2)}) collective-permute-start(bf16[768,2304]{1,0:T(8,128)(2,1)} %wu0.1), channel_id=1, source_target_pairs={{0,2},{2,0},{1,3},{3,1},{4,6},{6,4},{5,7},{7,5},{8,10},{10,8},{9,1... | collective-permute-start | bytes 10616840 | tf_op jit(solution)/shard_map/ppermute | solution.py:24
  106.7 78.2 %collective-permute-start.12 = (bf16[768,2304]{1,0:T(8,128)(2,1)}, bf16[768,2304]{1,0:T(8,128)(2,1)}, u32[]{:S(2)}, u32[]{:S(2)}) collective-permute-start(bf16[768,2304]{1,0:T(8,128)(2,1)} %wd0.1), channel_id=1, source_target_pairs={{0,2},{2,0},{1,3},{3,1},{4,6},{6,4},{5,7},{7,5},{8,10},{10,8},{9,1... | collective-permute-start | bytes 10616840 | tf_op jit(solution)/shard_map/ppermute | solution.py:24
  279.1 69.6 %collective-permute-start.15 = (bf16[1024,1536]{0,1:T(8,128)(2,1)}, bf16[1024,1536]{0,1:T(8,128)(2,1)}, u32[]{:S(2)}, u32[]{:S(2)}) collective-permute-start(bf16[1024,1536]{0,1:T(8,128)(2,1)} %copy.41), channel_id=1, source_target_pairs={{0,1},{1,0},{2,3},{3,2},{4,5},{5,4},{6,7},{7,6},{8,9},{9,8},{10,11... | collective-permute-start | bytes 9437192 | tf_op jit(solution)/shard_map/ppermute | solution.py:24
  280.9 142.6 %collective-permute-start.25 = (bf16[768,2304]{1,0:T(8,128)(2,1)}, bf16[768,2304]{1,0:T(8,128)(2,1)}, u32[]{:S(2)}, u32[]{:S(2)}) collective-permute-start(bf16[768,2304]{1,0:T(8,128)(2,1)} %get-tuple-element.62), channel_id=1, source_target_pairs={{0,2},{2,0},{1,3},{3,1},{4,6},{6,4},{5,7},{7,5},{8,10},{10,8},{9,1... | collective-permute-start | bytes 10616840 | tf_op jit(solution)/shard_map/ppermute | solution.py:24
  280.9 147.5 %collective-permute-start.26 = (bf16[768,2304]{1,0:T(8,128)(2,1)}, bf16[768,2304]{1,0:T(8,128)(2,1)}, u32[]{:S(2)}, u32[]{:S(2)}) collective-permute-start(bf16[768,2304]{1,0:T(8,128)(2,1)} %get-tuple-element.64), channel_id=1, source_target_pairs={{0,2},{2,0},{1,3},{3,1},{4,6},{6,4},{5,7},{7,5},{8,10},{10,8},{9,1... | collective-permute-start | bytes 10616840 | tf_op jit(solution)/shard_map/ppermute | solution.py:24
  289.5 143.9 %collective-permute-start.27 = (bf16[768,2304]{1,0:T(8,128)(2,1)}, bf16[768,2304]{1,0:T(8,128)(2,1)}, u32[]{:S(2)}, u32[]{:S(2)}) collective-permute-start(bf16[768,2304]{1,0:T(8,128)(2,1)} %get-tuple-element.66), channel_id=1, source_target_pairs={{0,2},{2,0},{1,3},{3,1},{4,6},{6,4},{5,7},{7,5},{8,10},{10,8},{9,1... | collective-permute-start | bytes 10616840 | tf_op jit(solution)/shard_map/ppermute | solution.py:24
  422.9 576.2 %all-reduce.6.cloned.1.call-start = ((), (), s32[]{:S(2)}) async-start(), calls=%async_computation.1 | async-start | bytes 30670848 | tf_op jit(solution)/shard_map/psum | solution.py:514
  422.9 15.5 %collective-permute-start.21 = (bf16[768,1024]{1,0:T(8,128)(2,1)}, bf16[768,1024]{1,0:T(8,128)(2,1)S(1)}, u32[]{:S(2)}, u32[]{:S(2)}) collective-permute-start(bf16[768,1024]{1,0:T(8,128)(2,1)} %get-tuple-element.54), channel_id=1, source_target_pairs={{0,2},{2,0},{1,3},{3,1},{4,6},{6,4},{5,7},{7,5},{8,10},{10,8},{9,1... | collective-permute-start | bytes 4718600 | tf_op jit(solution)/shard_map/ppermute | solution.py:24
  423.0 17.3 %collective-permute-start.22 = (bf16[768,1024]{1,0:T(8,128)(2,1)}, bf16[768,1024]{1,0:T(8,128)(2,1)S(1)}, u32[]{:S(2)}, u32[]{:S(2)}) collective-permute-start(bf16[768,1024]{1,0:T(8,128)(2,1)} %get-tuple-element.56), channel_id=1, source_target_pairs={{0,2},{2,0},{1,3},{3,1},{4,6},{6,4},{5,7},{7,5},{8,10},{10,8},{9,1... | collective-permute-start | bytes 4718600 | tf_op jit(solution)/shard_map/ppermute | solution.py:24
  423.5 18.6 %collective-permute-start.23 = (bf16[768,1024]{1,0:T(8,128)(2,1)}, bf16[768,1024]{1,0:T(8,128)(2,1)S(1)}, u32[]{:S(2)}, u32[]{:S(2)}) collective-permute-start(bf16[768,1024]{1,0:T(8,128)(2,1)} %get-tuple-element.60), channel_id=1, source_target_pairs={{0,2},{2,0},{1,3},{3,1},{4,6},{6,4},{5,7},{7,5},{8,10},{10,8},{9,1... | collective-permute-start | bytes 4718600 | tf_op jit(solution)/shard_map/ppermute | solution.py:24
  452.0 8.2 collective-permute-start.17
  455.9 91.1 %collective-permute-start.19 = (bf16[1024,768]{0,1:T(8,128)(2,1)}, bf16[1024,768]{0,1:T(8,128)(2,1)}, u32[]{:S(2)}, u32[]{:S(2)}) collective-permute-start(bf16[1024,768]{0,1:T(8,128)(2,1)} %broadcast_select_fusion.4), channel_id=1, source_target_pairs={{0,1},{1,0},{2,3},{3,2},{4,5},{5,4},{6,7},{7,6},{8,9},{9,8},{10,11... | collective-permute-start | bytes 4718600 | tf_op jit(solution)/shard_map/ppermute | solution.py:24
  459.7 92.1 %collective-permute-start.14 = (bf16[1024,768]{0,1:T(8,128)(2,1)}, bf16[1024,768]{0,1:T(8,128)(2,1)}, u32[]{:S(2)}, u32[]{:S(2)}) collective-permute-start(bf16[1024,768]{0,1:T(8,128)(2,1)} %broadcast_select_fusion.6), channel_id=1, source_target_pairs={{0,1},{1,0},{2,3},{3,2},{4,5},{5,4},{6,7},{7,6},{8,9},{9,8},{10,11... | collective-permute-start | bytes 4718600 | tf_op jit(solution)/shard_map/ppermute | solution.py:24
  461.5 64.9 %collective-permute-start.24 = (f32[768]{0:T(1024)S(1)}, f32[768]{0:T(1024)S(1)}, u32[]{:S(2)}, u32[]{:S(2)}) collective-permute-start(f32[768]{0:T(1024)S(1)} %slice.74), channel_id=1, source_target_pairs={{0,2},{2,0},{1,3},{3,1},{4,6},{6,4},{5,7},{7,5},{8,10},{10,8},{9,1... | collective-permute-start | bytes 9224 | tf_op jit(solution)/shard_map/ppermute | solution.py:24
  461.5 136.3 %collective-permute-start.16 = (bf16[1024,768]{0,1:T(8,128)(2,1)}, bf16[1024,768]{0,1:T(8,128)(2,1)}, u32[]{:S(2)}, u32[]{:S(2)}) collective-permute-start(bf16[1024,768]{0,1:T(8,128)(2,1)} %slice.63), channel_id=1, source_target_pairs={{0,2},{2,0},{1,3},{3,1},{4,6},{6,4},{5,7},{7,5},{8,10},{10,8},{9,1... | collective-permute-start | bytes 4718600 | tf_op jit(solution)/shard_map/ppermute | solution.py:24
  551.9 45.9 %collective-permute-start.20 = (f32[1024]{0:T(1024)S(1)}, f32[1024]{0:T(1024)S(1)}, u32[]{:S(2)}, u32[]{:S(2)}) collective-permute-start(f32[1024]{0:T(1024)S(1)} %get-tuple-element.70), channel_id=1, source_target_pairs={{0,2},{2,0},{1,3},{3,1},{4,6},{6,4},{5,7},{7,5},{8,10},{10,8},{9,1... | collective-permute-start | bytes 12296 | tf_op jit(solution)/shard_map/ppermute | solution.py:24
  (46 other events, 640.7 us)
Sparse Core Ops, SparseCore 0:
  423.0 94.8 all-reduce.3
  524.5 474.5 all-reduce.5

commit v2 on v1

v2 whole, which is shorter than its diff:
```python
import functools
import math

import jax
import jax.numpy as jnp
from jax import lax
from jax.experimental import pallas as pl
from jax.experimental.pallas import tpu as pltpu
from jax.sharding import PartitionSpec as P

D = 1536
KCONV = 4
LEN = 1024
OFFLOAD = 1536
EPS = 1e-06
GATE_SCALE = 8.0
TANH_COEF = math.sqrt(2.0 / math.pi)
CUBIC_COEF = 0.044715
F32 = jnp.float32
BF16 = jnp.bfloat16
MIB = 1024 * 1024


def swap(value, axis):
    return lax.ppermute(value, axis, [(0, 1), (1, 0)])


def dot(left, right):
    return lax.dot_general(left, right, (((1,), (0,)), ((), ())), preferred_element_type=F32)


def dot_nt(left, right):
    return lax.dot_general(left, right, (((1,), (1,)), ((), ())), preferred_element_type=F32)


def dot_tn(left, right):
    return lax.dot_general(left, right, (((0,), (0,)), ((), ())), preferred_element_type=F32)


def gelu_act(values):
    inner_arg = TANH_COEF * (values + CUBIC_COEF * values * values * values)
    return 0.5 * values * (1.0 + jnp.tanh(inner_arg))


def gelu_pair(values):
    square = values * values
    tanh_val = jnp.tanh(values * (TANH_COEF + (TANH_COEF * CUBIC_COEF) * square))
    half_up = 0.5 + 0.5 * tanh_val
    slope = half_up + 0.5 * values * (1.0 - tanh_val * tanh_val) * (
        TANH_COEF + (3.0 * TANH_COEF * CUBIC_COEF) * square
    )
    return (values * half_up, slope)


def decay_terms(recur_gate, soft_decay):
    u = (2.0 * GATE_SCALE) * recur_gate * soft_decay
    decay = jnp.exp(-0.5 * u)
    series = u * (
        1.0
        - u
        * (0.5 - u * (1.0 / 6 - u * (1.0 / 24 - u * (1.0 / 120 - u * (1.0 / 720)))))
    )
    em = jnp.where(u < 0.25, series, 1.0 - decay * decay)
    return (decay, em)


def scan_tile(decay, drive, row):
    for shift in (1, 2, 4):
        keep = row >= shift
        before_a = jnp.where(keep, pltpu.roll(decay, shift, 0), 1.0)
        before_b = jnp.where(keep, pltpu.roll(drive, shift, 0), 0.0)
        drive = decay * before_b + drive
        decay = decay * before_a
    return (decay, drive)


def scan_tile_back(decay, drive, row):
    for shift in (1, 2, 4):
        keep = row < 8 - shift
        after_a = jnp.where(keep, pltpu.roll(decay, 8 - shift, 0), 1.0)
        after_b = jnp.where(keep, pltpu.roll(drive, 8 - shift, 0), 0.0)
        drive = decay * after_b + drive
        decay = decay * after_a
    return (decay, drive)


def group_barrier(core, chip):
    barrier = pltpu.get_barrier_semaphore()
    for peer in ((1 - core, chip), (core, 1 - chip), (1 - core, 1 - chip)):
        pl.semaphore_signal(barrier, inc=1, device_id={"rows": peer[0], "cols": peer[1]})
    pl.semaphore_wait(barrier, 3)


def rec_forward_kernel(
    chunk, count, cot_parts,
    tokens, cotangent, wr_h, wg_h, ow_h, gain_h, rw, iw, cw, cb, rb, ib, sp,
    x_o, n1t_o, rec_o, gate_o, cl_o, r_o, i_o, st_o, br_o, mix_o, cot_o, far_o,
    tok_b, mix_s, wr, wg, ow, gain, gw, halo, carry, recpad, pre,
    tok_send, tok_recv, w_send, w_recv, w_own, cot_send, cot_recv, mix_send, mix_recv,
):
    step = pl.program_id(0)
    width = wr_h.shape[1]
    half = wr_h.shape[0]
    heads = width // 128
    core = lax.axis_index("rows")
    chip = lax.axis_index("cols")
    slot = lax.select(core == chip, 0, 1)
    near = {"rows": 1 - core}
    far = {"rows": chip, "cols": 1 - chip}

    def piece_moves(src, dst, send, recv):
        return (
            pltpu.make_async_copy(src, dst, recv),
            pltpu.make_async_remote_copy(src, dst, send.at[0], recv, device_id=near),
            pltpu.make_async_remote_copy(src, dst, send.at[1], recv, device_id=far),
        )

    def token_moves(k):
        return piece_moves(
            tokens.at[:, pl.ds(k * chunk, chunk)], tok_b.at[k, slot], tok_send.at[k], tok_recv.at[k, slot]
        )

    def cot_moves(k):
        return piece_moves(
            cotangent.at[:, pl.ds(k * chunk, chunk)],
            cot_o.at[slot, :, pl.ds(k * chunk, chunk)],
            cot_send.at[k],
            cot_recv.at[k, slot],
        )

    def mix_move(k):
        return pltpu.make_async_remote_copy(
            mix_s.at[k],
            far_o.at[pl.ds(k * chunk, chunk), :],
            mix_send.at[k],
            mix_recv.at[k],
            device_id={"cols": 1 - chip},
        )

    def start(moves):
        moves[2].start()

        @pl.when(core == chip)
        def _():
            moves[0].start()

        @pl.when(core != chip)
        def _():
            moves[1].start()

    def finish_send(moves):
        moves[2].wait_send()

        @pl.when(core != chip)
        def _():
            moves[1].wait_send()

    weights = ((wr_h, wr), (wg_h, wg), (ow_h, ow), (gain_h, gain))

    def weight_moves(n):
        src, dst = weights[n]
        return (
            pltpu.make_async_copy(src, dst.at[0], w_own.at[n]),
            pltpu.make_async_remote_copy(src, dst.at[1], w_send.at[n], w_recv.at[n], device_id=near),
        )

    def wait_weight(n):
        own, other = weight_moves(n)
        own.wait()
        other.wait_recv()

    @pl.when(step == 0)
    def _():
        group_barrier(core, chip)
        start(token_moves(0))
        for n in (3, 0, 1, 2):
            for move in weight_moves(n):
                move.start()
        for k in range(1, count):
            start(token_moves(k))
        halo[...] = jnp.zeros_like(halo)
        carry[...] = jnp.zeros_like(carry)
        for h in range(heads):
            gw[h, :, 0:128] = rw[h]
            gw[h, :, 128:256] = iw[h]
        wait_weight(3)

    for s in range(2):
        pltpu.make_async_copy(
            tokens.at[:, pl.ds(0, chunk)], tok_b.at[step, s], tok_recv.at[step, s]
        ).wait()

    @pl.when(step == count - 2)
    def _():
        for k in range(cot_parts):
            start(cot_moves(k))

    xt0 = tok_b[step, 0].astype(F32)
    xt1 = tok_b[step, 1].astype(F32)
    squares = jnp.sum(xt0 * xt0, axis=0, keepdims=True) + jnp.sum(xt1 * xt1, axis=0, keepdims=True)
    scale = lax.rsqrt(squares / (2 * half) + EPS)
    nt0 = (xt0 * scale * gain[0]).astype(BF16)
    nt1 = (xt1 * scale * gain[1]).astype(BF16)
    n1t_o[0:half, :] = nt0
    n1t_o[half:, :] = nt1
    x_o[:, 0:half] = tok_b[step, 0].T
    x_o[:, half:] = tok_b[step, 1].T
    low0 = nt0.T
    low1 = nt1.T

    @pl.when(step == 0)
    def _():
        wait_weight(0)
        wait_weight(1)

    rec = dot(low0, wr[0]) + dot(low1, wr[1])
    recpad[0:8, :] = halo[...]
    recpad[8:, :] = rec
    halo[...] = rec[chunk - 8 :, :]
    rec_o[...] = rec
    gate_o[...] = dot(low0, wg[0]) + dot(low1, wg[1])

    def conv_step(i, _):
        base = pl.multiple_of(i * 16, 16)
        for h in range(heads):
            sl = slice(h * 128, (h + 1) * 128)
            window = recpad[pl.ds(base, 24), sl]
            out = cb[:, sl] + cw[0:1, sl] * window[8:]
            for k in range(1, KCONV):
                out = out + cw[k : k + 1, sl] * pltpu.roll(window, k, 0)[8:]
            cl_o[pl.ds(base, 16), sl] = out.astype(BF16)
        return 0

    lax.fori_loop(0, chunk // 16, conv_step, 0)
    for h in range(heads):
        pre[:, h * 256 : (h + 1) * 256] = dot(cl_o[:, h * 128 : (h + 1) * 128], gw[h])
    row = lax.broadcasted_iota(jnp.int32, (8, 128), 0)

    def main_step(i, _):
        base = pl.multiple_of(i * 16, 16)
        rows = pl.ds(base, 16)
        for h in range(heads):
            sl = slice(h * 128, (h + 1) * 128)
            r = jax.nn.sigmoid(pre[rows, h * 256 : h * 256 + 128] + rb[:, sl])
            g = jax.nn.sigmoid(pre[rows, h * 256 + 128 : (h + 1) * 256] + ib[:, sl])
            conv = cl_o[rows, sl].astype(F32)
            decay, em = decay_terms(r, sp[:, sl])
            drive = jnp.sqrt(em) * g * conv
            r_o[rows, sl] = r
            i_o[rows, sl] = g
            held = carry[0:1, sl]
            parts = []
            for p in range(2):
                a, b = scan_tile(decay[p * 8 : p * 8 + 8], drive[p * 8 : p * 8 + 8], row)
                state = a * held + b
                held = state[7:8]
                parts.append(state)
            carry[0:1, sl] = held
            state = jnp.concatenate(parts, axis=0)
            st_o[rows, sl] = state
            br_o[rows, sl] = (state * gelu_act(gate_o[rows, sl])).astype(BF16)
        return 0

    lax.fori_loop(0, chunk // 16, main_step, 0)

    @pl.when(step == 0)
    def _():
        wait_weight(2)

    branch = br_o[...]
    mix_o[:, :half] = dot_nt(branch, ow[0]).astype(BF16)
    mix_o[:, half:] = dot_nt(branch, ow[1]).astype(BF16)

    for k in range(cot_parts):

        @pl.when(step == k)
        def _():
            mix_s[k] = mix_o[...]
            mix_move(k).start()

    @pl.when(step == count - 1)
    def _():
        for k in range(cot_parts):
            for s in range(2):
                pltpu.make_async_copy(
                    cotangent.at[:, pl.ds(0, chunk)],
                    cot_o.at[s, :, pl.ds(k * chunk, chunk)],
                    cot_recv.at[k, s],
                ).wait()
            finish_send(cot_moves(k))
            mix_move(k).wait()
        for k in range(count):
            finish_send(token_moves(k))
        for n in range(4):
            weight_moves(n)[1].wait_send()


def rec_forward(tokens, cotangent, wr, wg, ow, gain, rw, iw, cw, cb, rb, ib, sp, chunk=256):
    half, length = tokens.shape
    width = wr.shape[1]
    heads = width // 128
    count = length // chunk
    cot_parts = count // 2
    wide = 2 * half
    row_block = lambda cols: pl.BlockSpec((chunk, cols), lambda i: (i, 0))
    whole = lambda shape: pl.BlockSpec(
        shape, lambda i: (0,) * len(shape), pipeline_mode=pl.Buffered(1)
    )
    hbm = pl.BlockSpec(memory_space=pl.ANY)
    f32 = jax.ShapeDtypeStruct((length, width), F32)
    low = jax.ShapeDtypeStruct((length, width), BF16)
    dma = pltpu.SemaphoreType.DMA
    return pl.pallas_call(
        functools.partial(rec_forward_kernel, chunk, count, cot_parts),
        grid=(count,),
        in_specs=[hbm] * 6
        + [whole((heads, 128, 128))] * 2
        + [whole((KCONV, width))]
        + [whole((1, width))] * 4,
        out_specs=[row_block(wide), pl.BlockSpec((wide, chunk), lambda i: (0, i))]
        + [row_block(width)] * 7
        + [row_block(wide), hbm, hbm],
        out_shape=[
            jax.ShapeDtypeStruct((length, wide), BF16),
            jax.ShapeDtypeStruct((wide, length), BF16),
            f32, f32, low, f32, f32, f32, low,
            jax.ShapeDtypeStruct((length, wide), BF16),
            jax.ShapeDtypeStruct((2, half, cot_parts * chunk), BF16),
            jax.ShapeDtypeStruct((cot_parts * chunk, wide), BF16),
        ],
        scratch_shapes=[
            pltpu.VMEM((count, 2, half, chunk), BF16),
            pltpu.VMEM((cot_parts, chunk, wide), BF16),
            pltpu.VMEM((2, half, width), BF16),
            pltpu.VMEM((2, half, width), BF16),
            pltpu.VMEM((2, half, width), BF16),
            pltpu.VMEM((2, half, 1), F32),
            pltpu.VMEM((heads, 128, 256), BF16),
            pltpu.VMEM((8, width), F32),
            pltpu.VMEM((8, width), F32),
            pltpu.VMEM((chunk + 8, width), F32),
            pltpu.VMEM((chunk, 2 * width), F32),
            dma((count, 2)),
            dma((count, 2)),
            dma((4,)),
            dma((4,)),
            dma((4,)),
            dma((count, 2)),
            dma((count, 2)),
            dma((cot_parts,)),
            dma((cot_parts,)),
        ],
        compiler_params=pltpu.CompilerParams(
            vmem_limit_bytes=60 * MIB, collective_id=2, has_side_effects=True
        ),
        name="recurrent_forward",
    )(tokens, cotangent, wr, wg, ow, gain, rw, iw, cw, cb, rb, ib, sp)


def exchange(srcs, dsts, send, recv, at, core, chip):
    def moves(m):
        src, dst = srcs[m], dsts[m]
        if len(dst.shape) == 2:
            return (
                pltpu.make_async_remote_copy(src, dst, send.at[m, 0], recv.at[m, 0], device_id={"cols": 1 - chip}),
            )
        slot = lax.select(core == chip, 0, 1)
        there = dst.at[slot]
        return (
            pltpu.make_async_copy(src, there, recv.at[m, slot]),
            pltpu.make_async_remote_copy(
                src, there, send.at[m, 0], recv.at[m, slot], device_id={"rows": 1 - core}
            ),
            pltpu.make_async_remote_copy(
                src, there, send.at[m, 1], recv.at[m, slot], device_id={"rows": chip, "cols": 1 - chip}
            ),
        )

    @pl.when(at == 0)
    def _():
        group_barrier(core, chip)
        for m in range(len(srcs)):
            move = moves(m)
            move[-1].start()
            if len(move) > 1:

                @pl.when(core == chip)
                def _():
                    move[0].start()

                @pl.when(core != chip)
                def _():
                    move[1].start()

    def finish():
        for m in range(len(srcs)):
            move = moves(m)
            if len(move) == 1:
                move[0].wait()
                continue
            for s in range(2):
                pltpu.make_async_copy(srcs[m], dsts[m].at[s], recv.at[m, s]).wait()
            move[2].wait_send()

            @pl.when(core != chip)
            def _():
                move[1].wait_send()

    return finish


def ffn_kernel(
    tile, moved,
    x, mix, mix_far, ct, live, gain, keep, wg0, wg1, wu0, wu1, wd0, wd1, *refs
):
    srcs, refs = refs[:moved], refs[moved:]
    (res_o, n2t_o, cott_o, cot_o, out_o, gn2_o, hid_o, ga_o, gb_o), refs = refs[:9], refs[9:]
    dsts, (n2_s, out_acc, gn2_acc, send, recv) = refs[:moved], refs[moved:]
    finish = exchange(
        srcs, dsts, send, recv, pl.program_id(0), lax.axis_index("rows"), lax.axis_index("cols")
    )
    step = pl.program_id(0)
    tokens, wide = x.shape
    half = wide // 2

    @pl.when(step == 0)
    def _():
        out_acc[...] = jnp.zeros_like(out_acc)
        gn2_acc[...] = jnp.zeros_like(gn2_acc)
        cott_o[:half] = ct[0] * live[...]
        cott_o[half:] = ct[1] * live[...]
        cot_o[...] = cott_o[...].T

        def norm_step(i, _):
            rows = pl.ds(pl.multiple_of(i * 16, 16), 16)
            res = x[rows, :].astype(F32) + (mix[rows, :].astype(F32) + mix_far[rows, :].astype(F32))
            res_o[rows, :] = res
            scale = lax.rsqrt(jnp.sum(res * res, axis=1, keepdims=True) / wide + EPS)
            n2_s[rows, :] = (res * scale * gain[...]).astype(BF16)
            return 0

        lax.fori_loop(0, tokens // 16, norm_step, 0)
        n2t_o[...] = n2_s[...].T

    def tile_step(i, _):
        rows = pl.ds(pl.multiple_of(i * tile, tile), tile)
        n0, n1 = n2_s[rows, :half], n2_s[rows, half:]
        c0, c1 = cot_o[rows, :half], cot_o[rows, half:]
        a = dot(n0, wg0[...]) + dot(n1, wg1[...])
        b = dot(n0, wu0[...]) + dot(n1, wu1[...])
        gh = dot(c0, wd0[...]) + dot(c1, wd1[...])
        act, slope = gelu_pair(a)
        hidden = (act * b).astype(BF16)
        ga = (gh * b * slope).astype(BF16)
        gb = (gh * act).astype(BF16)
        hid_o[rows, :] = hidden
        ga_o[rows, :] = ga
        gb_o[rows, :] = gb
        out_acc[rows, :half] += dot_nt(hidden, wd0[...])
        out_acc[rows, half:] += dot_nt(hidden, wd1[...])
        gn2_acc[rows, :half] += dot_nt(ga, wg0[...]) + dot_nt(gb, wu0[...])
        gn2_acc[rows, half:] += dot_nt(ga, wg1[...]) + dot_nt(gb, wu1[...])
        return 0

    lax.fori_loop(0, tokens // tile, tile_step, 0)

    @pl.when(step == pl.num_programs(0) - 1)
    def _():
        out_o[...] = (out_acc[...] + keep[...] * res_o[...]).astype(BF16)
        gn2_o[...] = gn2_acc[...].astype(BF16)
        finish()


def ffn(part, tokens, x, mix, mix_far, cott, live, gain, keep, wg, wu, wd, srcs, dsts, collective_id, block=256, tile=256):
    wide = x.shape[1]
    half, width = wg[0].shape
    whole = lambda shape, at=(0, 0): pl.BlockSpec(
        shape, lambda i: at, pipeline_mode=pl.Buffered(1)
    )
    hbm = pl.BlockSpec(memory_space=pl.ANY)
    rows = whole((tokens, wide), (part, 0))
    act = whole((tokens, wide))
    across = whole((wide, tokens))
    weight = pl.BlockSpec((half, block), lambda i: (0, i))
    mid = pl.BlockSpec((tokens, block), lambda i: (0, i))
    low = jax.ShapeDtypeStruct((tokens, wide), BF16)
    turned = jax.ShapeDtypeStruct((wide, tokens), BF16)
    hidden = jax.ShapeDtypeStruct((tokens, width), BF16)
    sems = pltpu.SemaphoreType.DMA((len(srcs), 2))
    return pl.pallas_call(
        functools.partial(ffn_kernel, tile, len(srcs)),
        grid=(width // block,),
        in_specs=[rows, rows, act, whole((2, half, tokens), (0, 0, 0)), whole((1, tokens), (0, part))]
        + [whole((1, wide)), whole((1, 1))]
        + [weight] * 6
        + [hbm] * len(srcs),
        out_specs=[act, across, across, act, act, act, mid, mid, mid] + [hbm] * len(srcs),
        out_shape=[
            jax.ShapeDtypeStruct((tokens, wide), F32),
            turned, turned, low, low, low, hidden, hidden, hidden,
        ]
        + [jax.ShapeDtypeStruct(shape, BF16) for shape in dsts],
        scratch_shapes=[
            pltpu.VMEM((tokens, wide), BF16),
            pltpu.VMEM((tokens, wide), F32),
            pltpu.VMEM((tokens, wide), F32),
            sems,
            sems,
        ],
        compiler_params=pltpu.CompilerParams(
            vmem_limit_bytes=60 * MIB, collective_id=collective_id, has_side_effects=True
        ),
        name=f"ffn_{part}",
    )(x, mix, mix_far, cott, live, gain, keep, wg[0], wg[1], wu[0], wu[1], wd[0], wd[1], *srcs)


def ffn_weights_kernel(parts, *refs):
    n2t, cott, hid, ga, gb = (refs[i * parts : (i + 1) * parts] for i in range(5))
    src, gg0, gg1, gu0, gu1, gd0, gd1, dst, send, recv = refs[5 * parts :]
    finish = exchange(
        [src], [dst], send, recv, pl.program_id(0), lax.axis_index("rows"), lax.axis_index("cols")
    )
    half = gg0.shape[0]
    total = lambda pairs: sum(dot(left, right) for left, right in pairs).astype(BF16)
    for left, right, out0, out1 in ((n2t, ga, gg0, gg1), (n2t, gb, gu0, gu1), (cott, hid, gd0, gd1)):
        out0[...] = total([(a[:half], b[...]) for a, b in zip(left, right)])
        out1[...] = total([(a[half:], b[...]) for a, b in zip(left, right)])

    @pl.when(pl.program_id(0) == pl.num_programs(0) - 1)
    def _():
        finish()


def ffn_weights(n2t, cott, hid, ga, gb, src, collective_id, block=256):
    parts = len(n2t)
    wide, tokens = n2t[0].shape
    half, width = wide // 2, hid[0].shape[1]
    whole = lambda shape: pl.BlockSpec(shape, lambda i: (0, 0), pipeline_mode=pl.Buffered(1))
    mid = pl.BlockSpec((tokens, block), lambda i: (0, i))
    grad = jax.ShapeDtypeStruct((half, width), BF16)
    hbm = pl.BlockSpec(memory_space=pl.ANY)
    sems = pltpu.SemaphoreType.DMA((1, 2))
    return pl.pallas_call(
        functools.partial(ffn_weights_kernel, parts),
        grid=(width // block,),
        in_specs=[whole((wide, tokens))] * (2 * parts) + [mid] * (3 * parts) + [hbm],
        out_specs=[pl.BlockSpec((half, block), lambda i: (0, i))] * 6 + [hbm],
        out_shape=[grad] * 6 + [jax.ShapeDtypeStruct(src.shape, src.dtype)],
        scratch_shapes=[sems, sems],
        compiler_params=pltpu.CompilerParams(
            vmem_limit_bytes=60 * MIB, collective_id=collective_id, has_side_effects=True
        ),
        name="ffn_weights",
    )(*n2t, *cott, *hid, *ga, *gb, src)


def norm_back_kernel(gn, gn_far, res, cot, gain, g1_o, g1t_o, gain_o):
    rows_all, wide = gn.shape

    @pl.when(pl.program_id(0) == 0)
    def _():
        gain_o[...] = jnp.zeros_like(gain_o)

    def step(i, _):
        rows = pl.ds(pl.multiple_of(i * 16, 16), 16)
        grad = gn[rows, :].astype(F32) + gn_far[rows, :].astype(F32)
        held = res[rows, :]
        scale = lax.rsqrt(jnp.sum(held * held, axis=1, keepdims=True) / wide + EPS)
        product = grad * held
        by_gain = product * scale
        gain_o[...] += by_gain[0:8] + by_gain[8:16]
        inner = jnp.sum(product * gain[...], axis=1, keepdims=True)
        grad_one = (
            cot[rows, :].astype(F32)
            + scale * (grad * gain[...])
            - held * (scale * scale * scale * inner / wide)
        )
        g1_o[rows, :] = grad_one.astype(BF16)
        return 0

    lax.fori_loop(0, rows_all // 16, step, 0)
    g1t_o[...] = g1_o[...].T


def norm_back(gn, gn_far, res, cot, gain, chunk=256):
    tokens, wide = gn.shape
    rows = pl.BlockSpec((chunk, wide), lambda i: (i, 0))
    return pl.pallas_call(
        norm_back_kernel,
        grid=(tokens // chunk,),
        in_specs=[rows] * 4 + [pl.BlockSpec((1, wide), lambda i: (0, 0))],
        out_specs=[
            rows,
            pl.BlockSpec((wide, chunk), lambda i: (0, i)),
            pl.BlockSpec((8, wide), lambda i: (0, 0)),
        ],
        out_shape=[
            jax.ShapeDtypeStruct((tokens, wide), BF16),
            jax.ShapeDtypeStruct((wide, tokens), BF16),
            jax.ShapeDtypeStruct((8, wide), F32),
        ],
        compiler_params=pltpu.CompilerParams(vmem_limit_bytes=48 * MIB),
        name="norm_back",
    )(gn, gn_far, res, cot, gain)


def rec_backward_kernel(
    tile,
    g1a, g1b, g1ta, g1tb, n1t, st, gate, r_in, i_in, cl, rec, br, ow0, ow1, wr0, wr1, wg0, wg1, gw, cw, sp,
    x, gain, gain_a, gain_b,
    gn1_o, go0, go1, gr0, gr1, gg0, gg1, ggw, sums, stat, gains0, gains1,
    acc, gb_s, gc_s, ggp_s, grp_s, gip_s, grec_s, gain_s,
):
    step = pl.program_id(0)
    tokens, block = gb_s.shape
    wide = n1t.shape[0]
    heads = block // 128
    half = ow0.shape[0]
    tiles = tokens // tile
    subs = tile // 8

    @pl.when(step == 0)
    def _():
        acc[...] = jnp.zeros_like(acc)

    mid = tokens // 2
    gb_s[:mid] = dot(g1a[:, :half], ow0[...]) + dot(g1a[:, half:], ow1[...])
    gb_s[mid:] = dot(g1b[:, :half], ow0[...]) + dot(g1b[:, half:], ow1[...])
    go0[...] = (dot(g1ta[:half], br[:mid]) + dot(g1tb[:half], br[mid:])).astype(BF16)
    go1[...] = (dot(g1ta[half:], br[:mid]) + dot(g1tb[half:], br[mid:])).astype(BF16)
    sums[...] = jnp.zeros_like(sums)
    row = lax.broadcasted_iota(jnp.int32, (8, 128), 0)

    def back_step(j, held):
        i = tiles - 1 - j
        base = pl.multiple_of(i * tile, tile)
        rows = pl.ds(base, tile)
        before = pl.ds(pl.multiple_of(jnp.maximum(base - 8, 0), 8), 8)
        out = []
        for h in range(heads):
            sl = slice(h * 128, (h + 1) * 128)
            later_decay, later_carried = held[h]
            grad_branch = gb_s[rows, sl]
            act, slope = gelu_pair(gate[rows, sl])
            state = st[rows, sl]
            ggp_s[rows, sl] = (grad_branch * state * slope).astype(BF16)
            grad_state = grad_branch * act
            r = r_in[rows, sl]
            soft = sp[:, sl]
            decay, em = decay_terms(r, soft)
            parts = [None] * subs
            for p in range(subs - 1, -1, -1):
                own = decay[p * 8 : p * 8 + 8]
                after = jnp.where(row == 7, later_decay, pltpu.roll(own, 7, 0))
                a, b = scan_tile_back(after, grad_state[p * 8 : p * 8 + 8], row)
                carried = a * later_carried + b
                later_decay = own[0:1]
                later_carried = carried[0:1]
                parts[p] = carried
            out.append((later_decay, later_carried))
            carried = jnp.concatenate(parts, axis=0)
            edge = jnp.where(i > 0, st[before, sl][7:8], 0.0)
            prev = []
            for p in range(subs):
                prev.append(jnp.where(row == 0, edge, pltpu.roll(state[p * 8 : p * 8 + 8], 1, 0)))
                edge = state[p * 8 + 7 : p * 8 + 8]
            prev = jnp.concatenate(prev, axis=0)
            g = i_in[rows, sl]
            conv = cl[rows, sl].astype(F32)
            scaling = jnp.sqrt(em)
            gated = g * conv
            grad_log = carried * (prev * decay - gated * (decay * decay) / scaling)
            grad_soft = grad_log * (-GATE_SCALE * r)
            grp = grad_soft * soft * (1.0 - r)
            cs = carried * scaling
            gc_s[rows, sl] = cs * g
            gip = cs * gated * (1.0 - g)
            grp_s[rows, sl] = grp.astype(BF16)
            gip_s[rows, sl] = gip.astype(BF16)
            for n, term in enumerate((grp, gip, grad_soft)):
                total = term[0:8]
                for p in range(1, subs):
                    total = total + term[p * 8 : p * 8 + 8]
                sums[n * 8 : n * 8 + 8, sl] += total
        return tuple(out)

    zero = jnp.zeros((1, 128), F32)
    lax.fori_loop(0, tiles, back_step, tuple((zero, zero) for _ in range(heads)))
    for h in range(heads):
        sl = slice(h * 128, (h + 1) * 128)
        low = cl[:, sl]
        ggw[h, :, 0:128] = dot_tn(low, grp_s[:, sl]).astype(BF16)
        ggw[h, :, 128:256] = dot_tn(low, gip_s[:, sl]).astype(BF16)
        gc_s[:, sl] += dot_nt(grp_s[:, sl], gw[h, :, 0:128]) + dot_nt(gip_s[:, sl], gw[h, :, 128:256])

    def conv_step(j, held):
        i = tiles - 1 - j
        base = pl.multiple_of(i * tile, tile)
        rows = pl.ds(base, tile)
        before = pl.ds(pl.multiple_of(jnp.maximum(base - 8, 0), 8), 8)
        out = []
        for h in range(heads):
            sl = slice(h * 128, (h + 1) * 128)
            grad_conv = gc_s[rows, sl]
            window = jnp.concatenate([grad_conv, held[h]], axis=0)
            out.append(grad_conv[0:8])
            grad_rec = cw[0:1, sl] * grad_conv
            for k in range(1, KCONV):
                grad_rec = grad_rec + cw[k : k + 1, sl] * pltpu.roll(window, tile + 8 - k, 0)[:tile]
            grec_s[rows, sl] = grad_rec.astype(BF16)
            edge = jnp.where(i > 0, rec[before, sl], 0.0)
            past = jnp.concatenate([edge, rec[rows, sl]], axis=0)
            terms = [grad_conv * past[8:]]
            for k in range(1, KCONV):
                terms.append(grad_conv * pltpu.roll(past, k, 0)[8:])
            terms.append(grad_conv)
            for n, term in enumerate(terms):
                total = term[0:8]
                for p in range(1, subs):
                    total = total + term[p * 8 : p * 8 + 8]
                sums[24 + n * 8 : 32 + n * 8, sl] += total
        return tuple(out)

    lax.fori_loop(0, tiles, conv_step, tuple(jnp.zeros((8, 128), F32) for _ in range(heads)))
    grad_rec = grec_s[...]
    grad_gate = ggp_s[...]
    gr0[...] = dot(n1t[:half], grad_rec).astype(BF16)
    gr1[...] = dot(n1t[half:], grad_rec).astype(BF16)
    gg0[...] = dot(n1t[:half], grad_gate).astype(BF16)
    gg1[...] = dot(n1t[half:], grad_gate).astype(BF16)
    acc[:, :half] += dot_nt(grad_rec, wr0[...]) + dot_nt(grad_gate, wg0[...])
    acc[:, half:] += dot_nt(grad_rec, wr1[...]) + dot_nt(grad_gate, wg1[...])

    @pl.when(step == pl.num_programs(0) - 1)
    def _():
        gain_s[...] = jnp.zeros_like(gain_s)

        def stat_step(i, _):
            rows = pl.ds(pl.multiple_of(i * 16, 16), 16)
            part = acc[rows, :]
            gn1_o[rows, :] = part.astype(BF16)
            held = x[rows, :].astype(F32)
            scale = lax.rsqrt(jnp.sum(held * held, axis=1, keepdims=True) / wide + EPS)
            product = part * held
            by_gain = product * scale
            gain_s[...] += by_gain[0:8] + by_gain[8:16]
            inner = jnp.sum(product * gain[...], axis=1, keepdims=True)
            stat[rows, 0:64] = jnp.broadcast_to(inner, (16, 64))
            stat[rows, 64:128] = jnp.broadcast_to(scale, (16, 64))
            return 0

        lax.fori_loop(0, tokens // 16, stat_step, 0)
        both = gain_a[...] + gain_b[...]
        for out, sl in ((gains0, slice(0, half)), (gains1, slice(half, wide))):
            out[...] = jnp.zeros_like(out)
            out[0:8, :] = gain_s[:, sl]
            out[8:16, :] = both[:, sl]


def rec_backward(
    g1, g1t, n1t, st, gate, r, g, cl, rec, br, ow, wr, wg, gw, cw, sp, x, gain, gain_a, gain_b, block=256, tile=32
):
    wide, tokens = n1t.shape
    half, width = wr[0].shape
    heads = block // 128
    mid = tokens // 2
    whole = lambda shape: pl.BlockSpec(shape, lambda i: (0, 0), pipeline_mode=pl.Buffered(1))
    act = pl.BlockSpec((tokens, block), lambda i: (0, i))
    weight = pl.BlockSpec((half, block), lambda i: (0, i))
    thin = lambda n: pl.BlockSpec((n, block), lambda i: (0, i))
    gate_block = pl.BlockSpec((heads, 128, 256), lambda i: (i, 0, 0))
    grad = jax.ShapeDtypeStruct((half, width), BF16)
    return pl.pallas_call(
        functools.partial(rec_backward_kernel, tile),
        grid=(width // block,),
        in_specs=[whole((mid, wide))] * 2 + [whole((wide, mid))] * 2 + [whole((wide, tokens))]
        + [act] * 7
        + [weight] * 6
        + [gate_block, thin(KCONV), thin(1)]
        + [whole((tokens, wide)), whole((1, wide)), whole((8, wide)), whole((8, wide))],
        out_specs=[whole((tokens, wide))]
        + [weight] * 6
        + [gate_block, thin(64), whole((tokens, 128)), whole((64, half)), whole((64, half))],
        out_shape=[jax.ShapeDtypeStruct((tokens, wide), BF16)]
        + [grad] * 6
        + [
            jax.ShapeDtypeStruct((width // 128, 128, 256), BF16),
            jax.ShapeDtypeStruct((64, width), F32),
            jax.ShapeDtypeStruct((tokens, 128), F32),
            jax.ShapeDtypeStruct((64, half), F32),
            jax.ShapeDtypeStruct((64, half), F32),
        ],
        scratch_shapes=[
            pltpu.VMEM((tokens, wide), F32),
            pltpu.VMEM((tokens, block), F32),
            pltpu.VMEM((tokens, block), F32),
            pltpu.VMEM((tokens, block), BF16),
            pltpu.VMEM((tokens, block), BF16),
            pltpu.VMEM((tokens, block), BF16),
            pltpu.VMEM((tokens, block), BF16),
            pltpu.VMEM((8, wide), F32),
        ],
        compiler_params=pltpu.CompilerParams(vmem_limit_bytes=60 * MIB),
        name="recurrent_backward",
    )(
        g1[0], g1[1], g1t[0], g1t[1], n1t, st, gate, r, g, cl, rec, br,
        ow[0], ow[1], wr[0], wr[1], wg[0], wg[1], gw, cw, sp, x, gain, gain_a, gain_b,
    )


def ring_kernel(n, count, *refs):
    own, other, refs = refs[:count], refs[count : 2 * count], refs[2 * count :]
    (gn1, out_a, out_b, stat, g1_a, g1_b), refs = refs[:6], refs[6:]
    outs, refs = refs[:count], refs[count:]
    (gn1_p, out_p, stat_p, g1_p), scratch = refs[:4], refs[4:]
    piece_send, piece_recv = scratch[-2:]
    scratch = scratch[:-2]
    own_b, part_b, ring_b = scratch[:count], scratch[count : 2 * count], scratch[2 * count : 3 * count]
    own_sem, part_send, part_recv, rs_send, rs_recv, ag_send, ag_recv, put_sem = scratch[3 * count :]
    at = lax.axis_index("dp")
    core = lax.axis_index("rows")
    chip = lax.axis_index("cols")

    def place_of(index):
        return lax.select(index % 2 == 0, index // 2, n - 1 - index // 2)

    def index_of(place):
        return lax.select(place < n // 2, 2 * place, 2 * (n - 1 - place) + 1)

    me = place_of(at)
    nexts = (index_of(lax.rem(me + 1, n)), index_of(lax.rem(me + n - 1, n)))
    barrier = pltpu.get_barrier_semaphore()
    for neighbour in nexts:
        pl.semaphore_signal(barrier, inc=1, device_id={"dp": neighbour})
    for peer in ((1 - core, chip), (core, 1 - chip), (1 - core, 1 - chip)):
        pl.semaphore_signal(barrier, inc=1, device_id={"rows": peer[0], "cols": peer[1]})
    pl.semaphore_wait(barrier, 5)

    half = gn1_p.shape[2]
    part = out_a.shape[0]
    first, second = slice(0, half), slice(half, 2 * half)
    everything = slice(None)
    pieces = [
        (gn1, gn1_p, slice(None), first, second),
        (out_a, out_p, slice(0, part), first, second),
        (out_b, out_p, slice(part, 2 * part), first, second),
        (stat, stat_p, slice(None), everything, everything),
    ]
    singles = [(g1_a, slice(0, part)), (g1_b, slice(part, 2 * part))]
    diag = core == chip

    def piece_moves(m):
        src, dst, rows, mine, theirs = pieces[m]
        there = dst.at[chip, rows, :]
        sems = lambda w: (piece_send.at[m, w], piece_recv.at[m, chip])
        near = src.at[:, mine]
        away = src.at[:, theirs]
        return (
            pltpu.make_async_copy(near, there, piece_recv.at[m, chip]),
            pltpu.make_async_remote_copy(near, there, *sems(0), device_id={"cols": 1 - chip}),
            pltpu.make_async_remote_copy(away, there, *sems(1), device_id={"rows": 1 - core}),
            pltpu.make_async_remote_copy(
                away, there, *sems(1), device_id={"rows": 1 - core, "cols": 1 - chip}
            ),
        )

    def single_moves(m):
        src, rows = singles[m]
        there = g1_p.at[rows, :]
        at = len(pieces) + m
        return (
            pltpu.make_async_copy(src.at[:, first], there, piece_recv.at[at, 0]),
            pltpu.make_async_remote_copy(
                src.at[:, second], there, piece_send.at[at, 1], piece_recv.at[at, 0],
                device_id={"rows": 1 - core},
            ),
        )

    @pl.when(diag)
    def _():
        for m in range(len(pieces)):
            moves = piece_moves(m)
            moves[0].start()
            moves[2].start()
        for m in range(len(singles)):
            moves = single_moves(m)
            moves[0].start()
            moves[1].start()

    @pl.when(jnp.logical_not(diag))
    def _():
        for m in range(len(pieces)):
            moves = piece_moves(m)
            moves[1].start()
            moves[3].start()

    def chunk_of(way, s):
        return lax.rem(me + n - s, n) if way == 0 else lax.rem(me + s, n)

    def rows_of(k, way, s):
        size = own[k].shape[0] // n
        return pl.ds(pl.multiple_of(chunk_of(way, s) * size, size), size)

    def cols_of(k, way):
        wide = own[k].shape[1] // 2
        return pl.ds(way * wide, wide)

    def own_copy(k, way, s):
        return pltpu.make_async_copy(
            own[k].at[rows_of(k, way, s), cols_of(k, way)], own_b[k].at[way, s], own_sem.at[k, way, s]
        )

    def part_copy(k, way, s):
        return pltpu.make_async_remote_copy(
            src_ref=other[k].at[rows_of(k, way, s), cols_of(k, way)],
            dst_ref=part_b[k].at[way, s],
            send_sem=part_send.at[k, way],
            recv_sem=part_recv.at[k, way, s],
            device_id={"rows": 1 - core},
        )

    def sum_copy(k, way, s):
        return pltpu.make_async_remote_copy(
            src_ref=ring_b[k].at[way, s],
            dst_ref=ring_b[k].at[way, s + 1],
            send_sem=rs_send.at[k, way],
            recv_sem=rs_recv.at[k, way, s],
            device_id={"dp": nexts[way]},
        )

    def first_gather(k, way):
        rows = rows_of(k, way, n - 1)
        return pltpu.make_async_remote_copy(
            src_ref=ring_b[k].at[way, n - 1],
            dst_ref=outs[k].at[rows, cols_of(k, way)],
            send_sem=ag_send.at[k, way, 0],
            recv_sem=ag_recv.at[k, way, 0],
            device_id={"dp": nexts[way]},
        )

    def gather_copy(k, way, s):
        rows = rows_of(k, way, s - 1)
        there = outs[k].at[rows, cols_of(k, way)]
        return pltpu.make_async_remote_copy(
            src_ref=there,
            dst_ref=there,
            send_sem=ag_send.at[k, way, s],
            recv_sem=ag_recv.at[k, way, s],
            device_id={"dp": nexts[way]},
        )

    def put_copy(k, way):
        return pltpu.make_async_copy(
            ring_b[k].at[way, n - 1],
            outs[k].at[rows_of(k, way, n - 1), cols_of(k, way)],
            put_sem.at[k, way],
        )

    both = [(k, way) for k in range(count) for way in range(2)]

    def load_step(s, _):
        for k, way in both:
            part_copy(k, way, s).start()
            own_copy(k, way, s).start()
        return 0

    lax.fori_loop(0, n, load_step, 0)

    def add_step(k, way, s, received):
        own_copy(k, way, s).wait()
        part_copy(k, way, s).wait_recv()
        total = own_b[k][way, s].astype(F32) + part_b[k][way, s].astype(F32)
        if received:
            sum_copy(k, way, s - 1).wait_recv()
            total = total + ring_b[k][way, s].astype(F32)
        ring_b[k][way, s] = total.astype(ring_b[k].dtype)

    for k, way in both:
        add_step(k, way, 0, False)
        sum_copy(k, way, 0).start()

    def sum_step(s, _):
        for k, way in both:
            add_step(k, way, s, True)
            sum_copy(k, way, s).start()
        return 0

    lax.fori_loop(1, n - 1, sum_step, 0)
    for k, way in both:
        add_step(k, way, n - 1, True)
        first_gather(k, way).start()
        put_copy(k, way).start()

    def gather_step(s, _):
        for k, way in both:
            gather_copy(k, way, s - 1).wait_recv()
            gather_copy(k, way, s).start()
        return 0

    for k, way in both:
        first_gather(k, way).wait_recv()
        gather_copy(k, way, 1).start()
    lax.fori_loop(2, n - 1, gather_step, 0)
    for k, way in both:
        gather_copy(k, way, n - 2).wait_recv()
        put_copy(k, way).wait()
        first_gather(k, way).wait_send()

    def drain_step(s, _):
        for k, way in both:
            gather_copy(k, way, s).wait_send()
        return 0

    lax.fori_loop(1, n - 1, drain_step, 0)
    for k, way in both:
        pltpu.make_async_remote_copy(
            ring_b[k].at[way, pl.ds(0, n - 1)],
            ring_b[k].at[way, pl.ds(1, n - 1)],
            rs_send.at[k, way],
            rs_recv.at[k, way, 0],
            device_id={"dp": nexts[way]},
        ).wait_send()
        pltpu.make_async_remote_copy(
            own_b[k].at[way],
            part_b[k].at[way],
            part_send.at[k, way],
            part_recv.at[k, way, 0],
            device_id={"rows": 1 - core},
        ).wait_send()

    for m in range(len(pieces)):
        src, dst, rows, mine, _ = pieces[m]
        for c in range(2):
            pltpu.make_async_copy(src.at[:, mine], dst.at[c, rows, :], piece_recv.at[m, c]).wait()
    for m in range(len(singles)):
        single_moves(m)[0].wait()

    @pl.when(diag)
    def _():
        for m in range(len(pieces)):
            piece_moves(m)[2].wait_send()
        for m in range(len(singles)):
            single_moves(m)[1].wait_send()

    @pl.when(jnp.logical_not(diag))
    def _():
        for m in range(len(pieces)):
            moves = piece_moves(m)
            moves[1].wait_send()
            moves[3].wait_send()


def ring_sum(n, own, other, pieces):
    count = len(own)
    own, other = list(own), list(other)
    rows = [a.shape[0] for a in own]
    unit = lambda a: (16 if a.dtype == BF16 else 8) * n
    pad = [-a.shape[0] % unit(a) for a in own]
    fit = lambda a, extra: jnp.pad(a, ((0, extra), (0, 0))) if extra else a
    own = [fit(a, e) for a, e in zip(own, pad)]
    other = [fit(a, e) for a, e in zip(other, pad)]
    slots = [pltpu.VMEM((2, n, a.shape[0] // n, a.shape[1] // 2), a.dtype) for a in own]
    sems = pltpu.SemaphoreType.DMA((count, 2, n))
    pair = pltpu.SemaphoreType.DMA((count, 2))
    tokens, wide = pieces[0].shape
    piece = jax.ShapeDtypeStruct((2, tokens, wide // 2), BF16)
    hbm = pl.BlockSpec(memory_space=pl.ANY)
    outs = pl.pallas_call(
        functools.partial(ring_kernel, n, count),
        in_specs=[hbm] * (2 * count + len(pieces)),
        out_specs=[hbm] * (count + 4),
        out_shape=[jax.ShapeDtypeStruct(a.shape, a.dtype) for a in own]
        + [
            piece,
            piece,
            jax.ShapeDtypeStruct((2, tokens, 128), F32),
            jax.ShapeDtypeStruct((tokens, wide // 2), BF16),
        ],
        scratch_shapes=slots * 3
        + [sems, pair, sems, pair] + [sems] * 3 + [pair]
        + [pltpu.SemaphoreType.DMA((6, 2))] * 2,
        compiler_params=pltpu.CompilerParams(
            collective_id=0, has_side_effects=True, vmem_limit_bytes=60 * MIB
        ),
        name="ring_sum",
    )(*own, *other, *pieces)
    return [a[:r] for a, r in zip(outs, rows)], outs[count:]


def final_kernel(gn, out, stat, g1, tokens, gain, live, result_o, grad_o):
    wide = 2 * tokens.shape[0]
    low = lambda ref: ref[0].astype(F32) + ref[1].astype(F32)
    result_o[...] = (low(out).T * live[...]).astype(BF16)
    grad = low(gn).T
    held = tokens[...].astype(F32)
    inner = (stat[0] + stat[1]).T[0:1, :]
    scale = stat[0].T[64:65, :]
    grad_o[...] = (
        g1[...].astype(F32).T
        + (scale * gain[...]) * grad
        - held * (scale * scale * scale * inner / wide)
    ).astype(BF16)


def final(gn, out, stat, g1, tokens, gain, live, chunk=256):
    half, length = tokens.shape
    pair = lambda cols: pl.BlockSpec((2, chunk, cols), lambda i: (0, i, 0))
    across = pl.BlockSpec((half, chunk), lambda i: (0, i))
    shape = jax.ShapeDtypeStruct((half, length), BF16)
    return pl.pallas_call(
        final_kernel,
        grid=(length // chunk,),
        in_specs=[
            pair(half), pair(half), pair(128),
            pl.BlockSpec((chunk, half), lambda i: (i, 0)),
            across,
            pl.BlockSpec((half, 1), lambda i: (0, 0)),
            pl.BlockSpec((1, chunk), lambda i: (0, i)),
        ],
        out_specs=[across, across],
        out_shape=[shape, shape],
        compiler_params=pltpu.CompilerParams(vmem_limit_bytes=48 * MIB),
        name="final",
    )(gn, out, stat, g1, tokens, gain, live)


def body(
    dp, tokens, lengths, mix_gain, rec_weight, gate_weight, conv_weight, conv_bias,
    recur_weight, recur_bias, input_weight, input_bias, decay_param, out_weight,
    ffn_gain, ffn_gate, ffn_up, ffn_down, cotangent,
):
    at_row = lax.axis_index("rows")
    at_col = lax.axis_index("cols")
    diag = at_row == at_col
    half = tokens.shape[0]
    wide = 2 * half

    def over_rows(own, other):
        return (own.astype(F32) + swap(other, "rows").astype(F32)).astype(BF16)

    both = lambda weight: (weight, swap(weight, "rows"))

    positions = jnp.arange(LEN, dtype=jnp.int32)
    live_core = (positions < lengths[at_row]).astype(BF16)[None, :]
    live_chip = (positions < lengths[at_col]).astype(F32)
    part = LEN // 2

    sp = jax.nn.softplus(-decay_param)[None, :]
    (x, n1t, rec, gate, cl, r, g, st, br, mixed, cot_a, far_a) = rec_forward(
        tokens, cotangent, rec_weight, gate_weight, out_weight, mix_gain[:, None],
        recur_weight, input_weight, conv_weight, conv_bias[None, :], recur_bias[None, :],
        input_bias[None, :], sp,
    )
    wr = both(rec_weight)
    wg = both(gate_weight)
    ow = both(out_weight)
    fg = both(ffn_gate)
    fu = both(ffn_up)
    fd = both(ffn_down)
    gain_two = jnp.concatenate(both(ffn_gain))[None, :]
    gain_one = jnp.concatenate(both(mix_gain))[None, :]
    keep = diag.astype(F32).reshape(1, 1)
    gw = jnp.concatenate([recur_weight, input_weight], axis=2)

    half_shape = (part, 2 * half)
    res_a, n2t_a, cott_a, ctok_a, out_a, gn2_a, hid_a, ga_a, gb_a, far_b, cot_b = ffn(
        0, part, x, mixed, far_a, cot_a, live_core, gain_two, keep, fg, fu, fd,
        [mixed[part:], cotangent[:, part:]], [half_shape, (2, half, part)], 3,
    )
    res_b, n2t_b, cott_b, ctok_b, out_b, gn2_b, hid_b, ga_b, gb_b, gn2_far_a = ffn(
        1, part, x, mixed, far_b, cot_b, live_core, gain_two, keep, fg, fu, fd,
        [gn2_a], [half_shape], 4,
    )
    gg0, gg1, gu0, gu1, gd0, gd1, gn2_far_b = ffn_weights(
        [n2t_a, n2t_b], [cott_a, cott_b], [hid_a, hid_b], [ga_a, ga_b], [gb_a, gb_b], gn2_b, 5
    )
    g1_a, g1t_a, gain_a = norm_back(gn2_a, gn2_far_a, res_a, ctok_a, gain_two)
    g1_b, g1t_b, gain_b = norm_back(gn2_b, gn2_far_b, res_b, ctok_b, gain_two)
    cut = OFFLOAD
    sum_gate = lax.psum(over_rows(gg0[:, :cut], gg1[:, :cut]), "dp")
    gn1_part, go0, go1, gr0, gr1, gt0, gt1, ggw, sums, stat, gains0, gains1 = rec_backward(
        [g1_a, g1_b], [g1t_a, g1t_b], n1t, st, gate, r, g, cl, rec, br, ow, wr, wg, gw,
        conv_weight, sp, x, gain_one, gain_a, gain_b,
    )
    sum_gate, gu0 = lax.optimization_barrier((sum_gate, gu0))
    gates = ggw.reshape(-1, 256)
    own = [gu0, gd0, go0, gr0, gt0, gates, sums, gains0]
    other = [gu1, gd1, go1, gr1, gt1, gates, sums, gains1]
    if cut < gg0.shape[1]:
        own.append(gg0[:, cut:])
        other.append(gg1[:, cut:])
    total, moved = ring_sum(dp, own, other, [gn1_part, out_a, out_b, stat, g1_a, g1_b])
    sum_up, sum_down, sum_out, sum_rec, sum_gatew, gates, sums, gains = total[:8]
    sum_gate = jnp.concatenate([sum_gate] + total[8:], axis=1)
    result, grad_tokens = final(*moved, tokens, mix_gain[:, None], live_chip[None, :])
    gates = gates.astype(F32).reshape(ggw.shape)
    vec = jnp.sum(sums.reshape(8, 8, -1), axis=1)
    gains = jnp.sum(gains[:16].reshape(2, 8, half), axis=1)
    grad_gain_one = gains[0] + swap(gains[0], "cols")
    grad_decay = vec[2] * -jax.nn.sigmoid(-decay_param)
    return (
        result,
        grad_tokens,
        grad_gain_one,
        sum_rec.astype(F32),
        sum_gatew.astype(F32),
        vec[3:7],
        vec[7],
        gates[:, :, :128],
        vec[0],
        gates[:, :, 128:],
        vec[1],
        grad_decay,
        sum_out.astype(F32),
        gains[1],
        sum_gate.astype(F32),
        sum_up.astype(F32),
        sum_down.astype(F32),
    )


def solution(mesh):
    return jax.shard_map(
        functools.partial(body, mesh.shape["dp"]),
        mesh=mesh,
        in_specs=(
            P("rows", ("dp", "cols")),
            P("dp"),
            P("rows"),
            P("rows", "cols"),
            P("rows", "cols"),
            P(None, "cols"),
            P("cols"),
            P("cols", None, None),
            P("cols"),
            P("cols", None, None),
            P("cols"),
            P("cols"),
            P("rows", "cols"),
            P("rows"),
            P("rows", "cols"),
            P("rows", "cols"),
            P("rows", "cols"),
            P("rows", ("dp", "cols")),
        ),
        out_specs=(
            P("rows", ("dp", "cols")),
            P("rows", ("dp", "cols")),
            P("rows"),
            P("rows", "cols"),
            P("rows", "cols"),
            P(None, "cols"),
            P("cols"),
            P("cols", None, None),
            P("cols"),
            P("cols", None, None),
            P("cols"),
            P("cols"),
            P("rows", "cols"),
            P("rows"),
            P("rows", "cols"),
            P("rows", "cols"),
            P("rows", "cols"),
        ),
        check_vma=False,
    )
```

time: 1030 us -> 699 us (0.68)
  waiting for transfers between devices: 548 us -> 20.1 us
  Pallas kernels: 177 us -> 602 us
  blocking collectives: 123 us -> 0 us
  other arithmetic: 98.2 us -> 28.2 us
  local copies, waits for them, and re-layouts: 48.7 us -> 32 us
  starting transfers between devices: 15.6 us -> 2.62 us
    pallas_call x2 -> x8, Pallas kernels: 122 us -> 538 us  [the longest x1 275 us: ring_sum(): pl.pallas_call(functools.partial(ring_kernel, n, count), in_specs=[hbm] *...]
    psum x2 -> x1, waiting for transfers between devices: 396 us -> 12.1 us  [body(): sum_gate = lax.psum(over_rows(gg0[:, :cut], gg1[:, :cut]), 'dp')]
    ppermute x28 -> x10, waiting for transfers between devices: 152 us -> 8.02 us  [swap(): return lax.ppermute(value, axis, [(0, 1), (1, 0)])]
    psum x3 -> x0, blocking collectives: 123 us -> none  [the longest x1 62.6 us: body(): small = lax.psum((gvec, ggw), ('dp', 'rows'))]
    convert_element_type x13 -> x7, other arithmetic: 43.3 us -> 19.3 us  [the longest x1 4.86 us: body(): sum_gate.astype(F32)]
    pallas_call x4 -> x0, local copies, waits for them, and re-layouts: 19.4 us -> none  [the longest x2 9.57 us: ffn(): pl.pallas_call(functools.partial(ffn_kernel, tile), grid=(width // block,...]
    convert_element_type x6 -> x1, other arithmetic: 20.4 us -> 1.97 us  [over_rows(): return (own.astype(F32) + swap(other, 'rows').astype(F32)).astype(BF16)]
    reduce_sum x5 -> x2, other arithmetic: 16.3 us -> 1.99 us  [the longest x1 1.02 us: body(): vec = jnp.sum(sums.reshape(8, 8, -1), axis=1)]
  transfers between devices with their start and end apart: 30 -> 11, of which waited for: 7 -> 3; matrix products, arithmetic and copies ran while one was open for 11% -> 6% of each run, Pallas kernels for 9% -> 25%
where the time goes in v2:
time: 699 us
  Pallas kernels  602 us (86%)
  local copies, waits for them, and re-layouts  32 us (5%)
  other arithmetic  28.2 us (4%)
  waiting for transfers between devices  20.1 us (3%)
  between operations  14.3 us (2%)
    pallas_call x1, Pallas kernels, ring_sum(): pl.pallas_call(functools.partial(ring_kernel, n, count), in_specs=[hbm] *...  275 us
    pallas_call x2, Pallas kernels, ffn(): pl.pallas_call(functools.partial(ffn_kernel, tile, len(srcs)), grid=(widt...  108 us
    pallas_call x1, Pallas kernels, rec_forward(): pl.pallas_call(functools.partial(rec_forward_kernel, chunk, count, cot_pa...  93 us
    pallas_call x1, Pallas kernels, rec_backward(): pl.pallas_call(functools.partial(rec_backward_kernel, tile), grid=(width...  63.4 us
    pallas_call x1, Pallas kernels, ffn_weights(): pl.pallas_call(functools.partial(ffn_weights_kernel, parts), grid=(width...  42.3 us
  transfers between devices with their start and end apart: 11, of which 3 were waited for; matrix products, arithmetic and copies ran while one was open for 6% of the time, Pallas kernels for 25%

profile of v2, /device:TPU:0, one launch (start us, length us, event | category | flops | bytes accessed | tf_op | source)
XLA Modules:
  0.0 698.9 jit_solution(9365605700684150664)
XLA Ops:
  13.8 2.1 slice.50.refs_1_
  15.9 93.0 %recurrent_forward.1 = (bf16[1024,1536]{1,0:T(8,128)(2,1)}, bf16[1536,1024]{1,0:T(8,128)(2,1)}, f32[1024,1024]{1,0:T(8,128)}, f32[1024,1024]{1,0:T(8,128)}, bf16...) custom-call(bf16[768,1024]{1,0:T(8,128)(2,1)} %tokens.3, ...), custom_call_target="tpu_custom_call" | custom-call | tf_op jit(solution)/shard_map/recurrent_forward/pallas_call | solution.py:313
  108.9 2.7 slice.49.refs_0_
  114.0 62.2 %ffn_0.1 = (f32[512,1536]{1,0:T(8,128)}, bf16[1536,512]{1,0:T(8,128)(2,1)}, bf16[1536,512]{1,0:T(8,128)(2,1)}, bf16[512,1536]{1,0:T(8,128)(2,1)}, bf16[512,1536]...) custom-call(bf16[1024,1536]{1,0:T(8,128)(2,1)} %get-tuple-element.92, ...), custom_call_target="tpu_custom_call" | custom-call | tf_op jit(solution)/shard_map/ffn_0/pallas_call | solution.py:490
  176.2 46.1 %ffn_1.1 = (f32[512,1536]{1,0:T(8,128)}, bf16[1536,512]{1,0:T(8,128)(2,1)}, bf16[1536,512]{1,0:T(8,128)(2,1)}, bf16[512,1536]{1,0:T(8,128)(2,1)}, bf16[512,1536]...) custom-call(bf16[1024,1536]{1,0:T(8,128)(2,1)} %get-tuple-element.92, ...), custom_call_target="tpu_custom_call" | custom-call | tf_op jit(solution)/shard_map/ffn_1/pallas_call | solution.py:490
  222.3 42.3 %ffn_weights.1 = (bf16[768,2304]{1,0:T(8,128)(2,1)}, bf16[768,2304]{1,0:T(8,128)(2,1)}, bf16[768,2304]{1,0:T(8,128)(2,1)}, bf16[768,2304]{1,0:T(8,128)(2,1)}, bf...) custom-call(bf16[1536,512]{1,0:T(8,128)(2,1)} %get-tuple-element.96.refs_0_, ...), custom_call_target="tpu_custom_call" | custom-call | tf_op jit(solution)/shard_map/ffn_weights/pallas_call | solution.py:543
  264.6 2.0 slice.52
  266.7 4.5 collective-permute-done.4
  277.7 3.5 collective-permute-done.8
  281.8 2.5 slice.53.refs_8_
  284.3 2.4 slice.54.refs_17_
  286.6 6.7 norm_back.3
  296.2 6.6 norm_back.2
  308.0 63.4 %recurrent_backward.1 = (bf16[1024,1536]{1,0:T(8,128)(2,1)}, bf16[768,1024]{1,0:T(8,128)(2,1)}, bf16[768,1024]{1,0:T(8,128)(2,1)}, bf16[768,1024]{1,0:T(8,128)(2...) custom-call(bf16[512,1536]{1,0:T(8,128)(2,1)} %copy-done.1, ...), custom_call_target="tpu_custom_call" | custom-call | tf_op jit(solution)/shard_map/recurrent_backward/pallas_call | solution.py:773
  371.4 12.1 %all-reduce.2.cloned.1.call-done = bf16[768,1536]{1,0:T(8,128)(2,1)} async-done(((bf16[768,1536]{1,0:T(8,128)(2,1)}), bf16[768,1536]{1,0:T(8,128)(2,1)}) %all-reduce.2.cloned.1.call-update) | async-done | bytes 2359312 | tf_op jit(solution)/shard_map/psum | solution.py:1180
  383.5 275.1 %ring_sum.1 = (bf16[768,2304]{1,0:T(8,128)(2,1)}, bf16[768,2304]{1,0:T(8,128)(2,1)}, bf16[768,1024]{1,0:T(8,128)(2,1)}, bf16[768,1024]{1,0:T(8,128)(2,1)}, bf16[...) custom-call(bf16[768,2304]{1,0:T(8,128)(2,1)} %get-tuple-element.113, ...), custom_call_target="tpu_custom_call" | custom-call | tf_op jit(solution)/shard_map/ring_sum/pallas_call | solution.py:1068
  660.8 2.1 fusion
  664.5 4.9 maximum_convert_fusion
  670.6 3.5 convert_element_type.58
  674.1 3.5 convert_element_type.59
  677.6 2.1 convert_element_type.54
  679.7 2.1 convert_element_type.55
  681.7 2.1 convert_element_type.56
  685.1 6.3 final.1
  (98 shorter events, 31.2 us)
Async XLA Ops:
  7.2 376.3 %all-reduce.2.cloned.1.call-start = ((), (), s32[]{:S(2)}) async-start(), calls=%async_computation | async-start | bytes 4718592 | tf_op jit(solution)/shard_map/psum | solution.py:1180
  7.2 104.9 %collective-permute-start.1 = (bf16[768,2304]{1,0:T(8,128)(2,1)}, bf16[768,2304]{1,0:T(8,128)(2,1)S(1)}, u32[]{:S(2)}, u32[]{:S(2)}) collective-permute-start(bf16[768,2304]{1,0:T(8,128)(2,1)} %wg0.4), channel_id=1, source_target_pairs={{0,2},{2,0},{1,3},{3,1},{4,6},{6,4},{5,7},{7,5},{8,10},{10,8},{9,1... | collective-permute-start | bytes 10616840 | tf_op jit(solution)/shard_map/ppermute | solution.py:25
  7.8 104.4 %collective-permute-start.2 = (bf16[768,2304]{1,0:T(8,128)(2,1)}, bf16[768,2304]{1,0:T(8,128)(2,1)}, u32[]{:S(2)}, u32[]{:S(2)}) collective-permute-start(bf16[768,2304]{1,0:T(8,128)(2,1)} %wu0.3), channel_id=1, source_target_pairs={{0,2},{2,0},{1,3},{3,1},{4,6},{6,4},{5,7},{7,5},{8,10},{10,8},{9,1... | collective-permute-start | bytes 10616840 | tf_op jit(solution)/shard_map/ppermute | solution.py:25
  7.8 104.3 %collective-permute-start.3 = (bf16[768,2304]{1,0:T(8,128)(2,1)}, bf16[768,2304]{1,0:T(8,128)(2,1)}, u32[]{:S(2)}, u32[]{:S(2)}) collective-permute-start(bf16[768,2304]{1,0:T(8,128)(2,1)} %wd0.3), channel_id=1, source_target_pairs={{0,2},{2,0},{1,3},{3,1},{4,6},{6,4},{5,7},{7,5},{8,10},{10,8},{9,1... | collective-permute-start | bytes 10616840 | tf_op jit(solution)/shard_map/ppermute | solution.py:25
  8.3 103.3 %collective-permute-start = (f32[768]{0:T(1024)}, f32[768]{0:T(1024)S(1)}, u32[]{:S(2)}, u32[]{:S(2)}) collective-permute-start(f32[768]{0:T(1024)} %param.31), channel_id=1, source_target_pairs={{0,2},{2,0},{1,3},{3,1},{4,6},{6,4},{5,7},{7,5},{8,10},{10,8},{9,1... | collective-permute-start | bytes 9224 | tf_op jit(solution)/shard_map/ppermute | solution.py:25
  108.9 2.7 copy-start.29
  264.6 6.6 copy-start.16
  266.6 4.6 collective-permute-start.4
  271.2 3.5 copy-start.15
  273.2 32.5 %collective-permute-start.5 = (bf16[768,1024]{1,0:T(8,128)(2,1)}, bf16[768,1024]{1,0:T(8,128)(2,1)S(1)}, u32[]{:S(2)}, u32[]{:S(2)}) collective-permute-start(bf16[768,1024]{1,0:T(8,128)(2,1)} %ow0.1), channel_id=1, source_target_pairs={{0,2},{2,0},{1,3},{3,1},{4,6},{6,4},{5,7},{7,5},{8,10},{10,8},{9,1... | collective-permute-start | bytes 4718600 | tf_op jit(solution)/shard_map/ppermute | solution.py:25
  274.6 31.1 %collective-permute-start.6 = (bf16[768,1024]{1,0:T(8,128)(2,1)S(1)}, bf16[768,1024]{1,0:T(8,128)(2,1)S(1)}, u32[]{:S(2)}, u32[]{:S(2)}) collective-permute-start(bf16[768,1024]{1,0:T(8,128)(2,1)S(1)} %copy-done.14), channel_id=1, source_target_pairs={{0,2},{2,0},{1,3},{3,1},{4,6},{6,4},{5,7},{7,5},{8,10},{10,8},{9,1... | collective-permute-start | bytes 4718600 | tf_op jit(solution)/shard_map/ppermute | solution.py:25
  274.7 31.0 %collective-permute-start.7 = (bf16[768,1024]{1,0:T(8,128)(2,1)S(1)}, bf16[768,1024]{1,0:T(8,128)(2,1)S(1)}, u32[]{:S(2)}, u32[]{:S(2)}) collective-permute-start(bf16[768,1024]{1,0:T(8,128)(2,1)S(1)} %copy-done.15), channel_id=1, source_target_pairs={{0,2},{2,0},{1,3},{3,1},{4,6},{6,4},{5,7},{7,5},{8,10},{10,8},{9,1... | collective-permute-start | bytes 4718600 | tf_op jit(solution)/shard_map/ppermute | solution.py:25
  275.1 6.1 collective-permute-start.8
  281.8 4.9 copy-start.4
  281.8 4.9 copy-start.10
  286.6 9.6 %copy-start.2 = (bf16[512,1536]{1,0:T(8,128)(2,1)S(1)}, bf16[512,1536]{1,0:T(8,128)(2,1)}, u32[]{:S(2)}) copy-start(bf16[512,1536]{1,0:T(8,128)(2,1)} %get-tuple-element.99.refs_0_.gn) | copy-start | bytes 4718596
  658.6 5.9 copy-start.19
  660.2 31.2 %collective-permute-start.9 = (f32[768]{0:T(1024)S(1)}, f32[768]{0:T(1024)S(1)}, u32[]{:S(2)}, u32[]{:S(2)}) collective-permute-start(f32[768]{0:T(1024)S(1)} %get-tuple-element.168), channel_id=1, source_target_pairs={{0,1},{1,0},{2,3},{3,2},{4,5},{5,4},{6,7},{7,6},{8,9},{9,8},{10,11... | collective-permute-start | bytes 9224 | tf_op jit(solution)/shard_map/ppermute | solution.py:25
  664.5 4.9 copy-start.28
  664.5 6.1 copy-start.18
  670.6 3.5 copy-start.17
  674.1 3.5 copy-start.25
  681.7 3.1 copy-start.8
  681.7 3.4 copy-start.9
  (17 other events, 25.2 us)
Sparse Core Ops, SparseCore 0:
  273.3 110.1 all-reduce.1

commit v3 on v2

--- a/solution.py
+++ b/solution.py
@@ -11,7 +11,6 @@
 D = 1536
 KCONV = 4
 LEN = 1024
-OFFLOAD = 1536
 EPS = 1e-06
 GATE_SCALE = 8.0
 TANH_COEF = math.sqrt(2.0 / math.pi)
@@ -94,9 +93,9 @@
 def rec_forward_kernel(
     chunk, count, cot_parts,
     tokens, cotangent, wr_h, wg_h, ow_h, gain_h, rw, iw, cw, cb, rb, ib, sp,
-    x_o, n1t_o, rec_o, gate_o, cl_o, r_o, i_o, st_o, br_o, mix_o, cot_o, far_o,
+    x_o, n1t_o, rec_o, gate_o, cl_o, r_o, i_o, st_o, br_o, mix_o, cot_o, far_o, wr_o, wg_o, ow_o,
     tok_b, mix_s, wr, wg, ow, gain, gw, halo, carry, recpad, pre,
-    tok_send, tok_recv, w_send, w_recv, w_own, cot_send, cot_recv, mix_send, mix_recv,
+    tok_send, tok_recv, w_send, w_recv, w_own, cot_send, cot_recv, mix_send, mix_recv, put,
 ):
     step = pl.program_id(0)
     width = wr_h.shape[1]
@@ -267,6 +266,17 @@
     def _():
         wait_weight(2)
 
+    def put_moves():
+        return [
+            pltpu.make_async_copy(held.at[1], out, put.at[n])
+            for n, (held, out) in enumerate(((wr, wr_o), (wg, wg_o), (ow, ow_o)))
+        ]
+
+    @pl.when(step == 0)
+    def _():
+        for move in put_moves():
+            move.start()
+
     branch = br_o[...]
     mix_o[:, :half] = dot_nt(branch, ow[0]).astype(BF16)
     mix_o[:, half:] = dot_nt(branch, ow[1]).astype(BF16)
@@ -293,6 +303,8 @@
             finish_send(token_moves(k))
         for n in range(4):
             weight_moves(n)[1].wait_send()
+        for move in put_moves():
+            move.wait()
 
 
 def rec_forward(tokens, cotangent, wr, wg, ow, gain, rw, iw, cw, cb, rb, ib, sp, chunk=256):
@@ -319,7 +331,8 @@
         + [whole((1, width))] * 4,
         out_specs=[row_block(wide), pl.BlockSpec((wide, chunk), lambda i: (0, i))]
         + [row_block(width)] * 7
-        + [row_block(wide), hbm, hbm],
+        + [row_block(wide)]
+        + [hbm] * 5,
         out_shape=[
             jax.ShapeDtypeStruct((length, wide), BF16),
             jax.ShapeDtypeStruct((wide, length), BF16),
@@ -327,7 +340,8 @@
             jax.ShapeDtypeStruct((length, wide), BF16),
             jax.ShapeDtypeStruct((2, half, cot_parts * chunk), BF16),
             jax.ShapeDtypeStruct((cot_parts * chunk, wide), BF16),
-        ],
+        ]
+        + [jax.ShapeDtypeStruct((half, width), BF16)] * 3,
         scratch_shapes=[
             pltpu.VMEM((count, 2, half, chunk), BF16),
             pltpu.VMEM((cot_parts, chunk, wide), BF16),
@@ -349,6 +363,7 @@
             dma((count, 2)),
             dma((cot_parts,)),
             dma((cot_parts,)),
+            dma((3,)),
         ],
         compiler_params=pltpu.CompilerParams(
             vmem_limit_bytes=60 * MIB, collective_id=2, has_side_effects=True
@@ -416,8 +431,13 @@
     srcs, refs = refs[:moved], refs[moved:]
     (res_o, n2t_o, cott_o, cot_o, out_o, gn2_o, hid_o, ga_o, gb_o), refs = refs[:9], refs[9:]
     dsts, (n2_s, out_acc, gn2_acc, send, recv) = refs[:moved], refs[moved:]
+    later = pl.ds(x.shape[0], x.shape[0])
+    if moved == 2:
+        views = [srcs[0].at[later, :], srcs[1].at[:, later]]
+    else:
+        views = [srcs[0].at[...]]
     finish = exchange(
-        srcs, dsts, send, recv, pl.program_id(0), lax.axis_index("rows"), lax.axis_index("cols")
+        views, dsts, send, recv, pl.program_id(0), lax.axis_index("rows"), lax.axis_index("cols")
     )
     step = pl.program_id(0)
     tokens, wide = x.shape
@@ -443,7 +463,7 @@
         n2t_o[...] = n2_s[...].T
 
     def tile_step(i, _):
-        rows = pl.ds(pl.multiple_of(i * tile, tile), tile)
+        rows = pl.ds(i * tile, tile)
         n0, n1 = n2_s[rows, :half], n2_s[rows, half:]
         c0, c1 = cot_o[rows, :half], cot_o[rows, half:]
         a = dot(n0, wg0[...]) + dot(n1, wg1[...])
@@ -462,7 +482,8 @@
         gn2_acc[rows, half:] += dot_nt(ga, wg1[...]) + dot_nt(gb, wu1[...])
         return 0
 
-    lax.fori_loop(0, tokens // tile, tile_step, 0)
+    for i in range(tokens // tile):
+        tile_step(i, 0)
 
     @pl.when(step == pl.num_programs(0) - 1)
     def _():
@@ -514,52 +535,8 @@
     )(x, mix, mix_far, cott, live, gain, keep, wg[0], wg[1], wu[0], wu[1], wd[0], wd[1], *srcs)
 
 
-def ffn_weights_kernel(parts, *refs):
-    n2t, cott, hid, ga, gb = (refs[i * parts : (i + 1) * parts] for i in range(5))
-    src, gg0, gg1, gu0, gu1, gd0, gd1, dst, send, recv = refs[5 * parts :]
-    finish = exchange(
-        [src], [dst], send, recv, pl.program_id(0), lax.axis_index("rows"), lax.axis_index("cols")
-    )
-    half = gg0.shape[0]
-    total = lambda pairs: sum(dot(left, right) for left, right in pairs).astype(BF16)
-    for left, right, out0, out1 in ((n2t, ga, gg0, gg1), (n2t, gb, gu0, gu1), (cott, hid, gd0, gd1)):
-        out0[...] = total([(a[:half], b[...]) for a, b in zip(left, right)])
-        out1[...] = total([(a[half:], b[...]) for a, b in zip(left, right)])
-
-    @pl.when(pl.program_id(0) == pl.num_programs(0) - 1)
-    def _():
-        finish()
-
-
-def ffn_weights(n2t, cott, hid, ga, gb, src, collective_id, block=256):
-    parts = len(n2t)
-    wide, tokens = n2t[0].shape
-    half, width = wide // 2, hid[0].shape[1]
-    whole = lambda shape: pl.BlockSpec(shape, lambda i: (0, 0), pipeline_mode=pl.Buffered(1))
-    mid = pl.BlockSpec((tokens, block), lambda i: (0, i))
-    grad = jax.ShapeDtypeStruct((half, width), BF16)
-    hbm = pl.BlockSpec(memory_space=pl.ANY)
-    sems = pltpu.SemaphoreType.DMA((1, 2))
-    return pl.pallas_call(
-        functools.partial(ffn_weights_kernel, parts),
-        grid=(width // block,),
-        in_specs=[whole((wide, tokens))] * (2 * parts) + [mid] * (3 * parts) + [hbm],
-        out_specs=[pl.BlockSpec((half, block), lambda i: (0, i))] * 6 + [hbm],
-        out_shape=[grad] * 6 + [jax.ShapeDtypeStruct(src.shape, src.dtype)],
-        scratch_shapes=[sems, sems],
-        compiler_params=pltpu.CompilerParams(
-            vmem_limit_bytes=60 * MIB, collective_id=collective_id, has_side_effects=True
-        ),
-        name="ffn_weights",
-    )(*n2t, *cott, *hid, *ga, *gb, src)
-
-
-def norm_back_kernel(gn, gn_far, res, cot, gain, g1_o, g1t_o, gain_o):
-    rows_all, wide = gn.shape
-
-    @pl.when(pl.program_id(0) == 0)
-    def _():
-        gain_o[...] = jnp.zeros_like(gain_o)
+def norm_back(gn, gn_far, res, cot, gain, g1_o, g1t_o, gain_o):
+    rows_all, wide = g1_o.shape
 
     def step(i, _):
         rows = pl.ds(pl.multiple_of(i * 16, 16), 16)
@@ -582,34 +559,234 @@
     g1t_o[...] = g1_o[...].T
 
 
-def norm_back(gn, gn_far, res, cot, gain, chunk=256):
-    tokens, wide = gn.shape
-    rows = pl.BlockSpec((chunk, wide), lambda i: (i, 0))
+def ffn_back_kernel(
+    n2t_a, n2t_b, cott_a, cott_b, hid_a, hid_b, ga_a, ga_b, gb_a, gb_b,
+    gn_a, gn_far_a, gn_b, res_a, res_b, cot_a, cot_b, gain,
+    gu_sum, gg0, gg1, gd0, gd1, g1_a, g1t_a, g1_b, g1t_b, gain_o,
+    gn_far_b, keep_s, give_s, got_s, send, recv, up_send, up_recv,
+):
+    step = pl.program_id(0)
+    last = pl.num_programs(0) - 1
+    core, chip = lax.axis_index("rows"), lax.axis_index("cols")
+    finish = exchange([gn_b.at[...]], [gn_far_b], send, recv, step, core, chip)
+    half, block = gg0.shape
+
+    def give(k):
+        return pltpu.make_async_remote_copy(
+            give_s.at[k], got_s.at[k], up_send.at[k], up_recv.at[k], device_id={"rows": 1 - core}
+        )
+
+    def join(k):
+        give(k).wait()
+        total = keep_s[k].astype(F32) + got_s[k].astype(F32)
+        gu_sum[:, pl.ds(pl.multiple_of(k * block, block), block)] = total.astype(BF16)
+
+    @pl.when(step == 0)
+    def _():
+        gain_o[...] = jnp.zeros_like(gain_o)
+        norm_back(gn_a, gn_far_a, res_a, cot_a, gain, g1_a, g1t_a, gain_o)
+
+    def product(left_a, left_b, right_a, right_b, top):
+        sl = slice(0, half) if top else slice(half, 2 * half)
+        return (dot(left_a[sl], right_a[...]) + dot(left_b[sl], right_b[...])).astype(BF16)
+
+    give_s[step] = product(n2t_a, n2t_b, gb_a, gb_b, False)
+    give(step).start()
+    keep_s[step] = product(n2t_a, n2t_b, gb_a, gb_b, True)
+    gg0[...] = product(n2t_a, n2t_b, ga_a, ga_b, True)
+    gg1[...] = product(n2t_a, n2t_b, ga_a, ga_b, False)
+    gd0[...] = product(cott_a, cott_b, hid_a, hid_b, True)
+    gd1[...] = product(cott_a, cott_b, hid_a, hid_b, False)
+
+    @pl.when(step > 0)
+    def _():
+        join(step - 1)
+
+    @pl.when(step == last)
+    def _():
+        finish()
+        norm_back(gn_b, gn_far_b, res_b, cot_b, gain, g1_b, g1t_b, gain_o)
+        join(step)
+
+
+def ffn_back(n2t, cott, hid, ga, gb, gn, gn_far_a, res, cot, gain, collective_id, block=256):
+    wide, tokens = n2t[0].shape
+    half, width = wide // 2, hid[0].shape[1]
+    count = width // block
+    whole = lambda shape: pl.BlockSpec(shape, lambda i: (0, 0), pipeline_mode=pl.Buffered(1))
+    mid = pl.BlockSpec((tokens, block), lambda i: (0, i))
+    grad = jax.ShapeDtypeStruct((half, width), BF16)
+    act, across = whole((tokens, wide)), whole((wide, tokens))
+    weight = pl.BlockSpec((half, block), lambda i: (0, i))
+    sems = pltpu.SemaphoreType.DMA((1, 2))
+    up_sems = pltpu.SemaphoreType.DMA((count,))
+    low = jax.ShapeDtypeStruct((tokens, wide), BF16)
+    turned = jax.ShapeDtypeStruct((wide, tokens), BF16)
+    blocks = pltpu.VMEM((count, half, block), BF16)
     return pl.pallas_call(
-        norm_back_kernel,
-        grid=(tokens // chunk,),
-        in_specs=[rows] * 4 + [pl.BlockSpec((1, wide), lambda i: (0, 0))],
-        out_specs=[
-            rows,
-            pl.BlockSpec((wide, chunk), lambda i: (0, i)),
-            pl.BlockSpec((8, wide), lambda i: (0, 0)),
+        ffn_back_kernel,
+        grid=(count,),
+        in_specs=[across] * 4 + [mid] * 6 + [act] * 7 + [whole((1, wide))],
+        out_specs=[whole((half, width))]
+        + [weight] * 4
+        + [act, across, act, across, whole((8, wide))],
+        out_shape=[grad] * 5 + [low, turned, low, turned, jax.ShapeDtypeStruct((8, wide), F32)],
+        scratch_shapes=[
+            pltpu.VMEM((tokens, wide), BF16), blocks, blocks, blocks, sems, sems, up_sems, up_sems,
         ],
-        out_shape=[
-            jax.ShapeDtypeStruct((tokens, wide), BF16),
-            jax.ShapeDtypeStruct((wide, tokens), BF16),
-            jax.ShapeDtypeStruct((8, wide), F32),
-        ],
-        compiler_params=pltpu.CompilerParams(vmem_limit_bytes=48 * MIB),
-        name="norm_back",
-    )(gn, gn_far, res, cot, gain)
+        compiler_params=pltpu.CompilerParams(
+            vmem_limit_bytes=60 * MIB, collective_id=collective_id, has_side_effects=True
+        ),
+        name="ffn_back",
+    )(*n2t, *cott, *hid, *ga, *gb, gn[0], gn_far_a, gn[1], *res, *cot, gain)
+
+
+def ring_place(n, at):
+    def index_of(place):
+        return lax.select(place < n // 2, 2 * place, 2 * (n - 1 - place) + 1)
+
+    me = lax.select(at % 2 == 0, at // 2, n - 1 - at // 2)
+    return me, (index_of(lax.rem(me + 1, n)), index_of(lax.rem(me + n - 1, n)))
+
+
+def ring_rows(n, me, total, way, s):
+    size = total // n
+    chunk = lax.rem(me + n - s, n) if way == 0 else lax.rem(me + s, n)
+    return pl.ds(pl.multiple_of(chunk * size, size), size)
+
+
+def ring_beside(n, own, out, own_b, ring_b, own_sem, rs_send, rs_recv, ag_send, ag_recv, put_sem):
+    me, nexts = ring_place(n, lax.axis_index("dp"))
+    wide = own.shape[1] // 2
+    cut = (wide // 128 + 1) // 2 * 128
+    groups = (pl.ds(0, cut), pl.ds(cut, wide - cut))
+    both = [(g, way) for g in range(2) for way in range(2)]
+    per = -(-n // 8)
+    per_gather = -(-(n - 2) // 6)
+    rows_of = lambda way, s: ring_rows(n, me, own.shape[0], way, s)
+    cols_of = lambda g, way: pl.ds(way * wide + g * cut, wide - cut if g else cut)
+
+    def own_copy(way, s):
+        return pltpu.make_async_copy(
+            own.at[rows_of(way, s), pl.ds(way * wide, wide)], own_b.at[way, s], own_sem.at[way, s]
+        )
+
+    def sum_copy(g, way, s):
+        return pltpu.make_async_remote_copy(
+            ring_b.at[way, s, :, groups[g]], ring_b.at[way, s + 1, :, groups[g]],
+            rs_send.at[g, way], rs_recv.at[g, way, s], device_id={"dp": nexts[way]},
+        )
+
+    def first_gather(g, way):
+        return pltpu.make_async_remote_copy(
+            ring_b.at[way, n - 1, :, groups[g]], out.at[rows_of(way, n - 1), cols_of(g, way)],
+            ag_send.at[g, way, 0], ag_recv.at[g, way, 0], device_id={"dp": nexts[way]},
+        )
+
+    def gather_copy(g, way, s):
+        there = out.at[rows_of(way, s - 1), cols_of(g, way)]
+        return pltpu.make_async_remote_copy(
+            there, there, ag_send.at[g, way, s], ag_recv.at[g, way, s], device_id={"dp": nexts[way]}
+        )
+
+    def put_copy(g, way):
+        return pltpu.make_async_copy(
+            ring_b.at[way, n - 1, :, groups[g]],
+            out.at[rows_of(way, n - 1), cols_of(g, way)],
+            put_sem.at[g, way],
+        )
+
+    def begin():
+        barrier = pltpu.get_barrier_semaphore()
+        for neighbour in nexts:
+            pl.semaphore_signal(barrier, inc=1, device_id={"dp": neighbour})
+
+        def load(s, _):
+            for way in range(2):
+                own_copy(way, s).start()
+            return 0
+
+        lax.fori_loop(0, n, load, 0)
+        pl.semaphore_wait(barrier, 2)
+
+    def tick(g, t):
+        def sum_step(s, _):
+            for way in range(2):
+                if g == 0:
+                    own_copy(way, s).wait()
+
+                @pl.when(s == 0)
+                def _():
+                    ring_b[way, s, :, groups[g]] = own_b[way, s, :, groups[g]]
+
+                @pl.when(s > 0)
+                def _():
+                    sum_copy(g, way, s - 1).wait_recv()
+                    total = ring_b[way, s, :, groups[g]].astype(F32) + own_b[
+                        way, s, :, groups[g]
+                    ].astype(F32)
+                    ring_b[way, s, :, groups[g]] = total.astype(BF16)
+
+                @pl.when(s < n - 1)
+                def _():
+                    sum_copy(g, way, s).start()
+
+                @pl.when(s == n - 1)
+                def _():
+                    first_gather(g, way).start()
+                    put_copy(g, way).start()
+            return 0
+
+        def gather_step(s, _):
+            for way in range(2):
+
+                @pl.when(s == 1)
+                def _():
+                    first_gather(g, way).wait_recv()
+
+                @pl.when(s > 1)
+                def _():
+                    gather_copy(g, way, s - 1).wait_recv()
+
+                gather_copy(g, way, s).start()
+            return 0
+
+        @pl.when(t < 8)
+        def _():
+            lax.fori_loop(t * per, jnp.minimum((t + 1) * per, n), sum_step, 0)
+
+        @pl.when(t >= 8)
+        def _():
+            start = 1 + (t - 8) * per_gather
+            lax.fori_loop(start, jnp.minimum(start + per_gather, n - 1), gather_step, 0)
+
+    def end():
+        for g, way in both:
+            gather_copy(g, way, n - 2).wait_recv()
+            put_copy(g, way).wait()
+            first_gather(g, way).wait_send()
+            pltpu.make_async_remote_copy(
+                ring_b.at[way, pl.ds(0, n - 1), :, groups[g]],
+                ring_b.at[way, pl.ds(1, n - 1), :, groups[g]],
+                rs_send.at[g, way], rs_recv.at[g, way, 0], device_id={"dp": nexts[way]},
+            ).wait_send()
+
+        def drain(s, _):
+            for g, way in both:
+                gather_copy(g, way, s).wait_send()
+            return 0
+
+        lax.fori_loop(1, n - 1, drain, 0)
+
+    return begin, tick, end
 
 
 def rec_backward_kernel(
-    tile,
-    g1a, g1b, g1ta, g1tb, n1t, st, gate, r_in, i_in, cl, rec, br, ow0, ow1, wr0, wr1, wg0, wg1, gw, cw, sp,
-    x, gain, gain_a, gain_b,
-    gn1_o, go0, go1, gr0, gr1, gg0, gg1, ggw, sums, stat, gains0, gains1,
-    acc, gb_s, gc_s, ggp_s, grp_s, gip_s, grec_s, gain_s,
+    tile, n,
+    g1a, g1b, g1ta, g1tb, n1t, st, gate, r_in, i_in, cl, rec, br, ow0, ow1, wr0, wr1, wg0, wg1, rw, iw, cw, sp,
+    x, gain, gain_two, up,
+    gn1_o, go0, go1, gr0, gr1, gg0, gg1, ggw, sums, stat, gains0, gains1, up_o,
+    acc, gb_s, gc_s, ggp_s, grp_s, gip_s, grec_s, gain_s, *ring_refs
 ):
     step = pl.program_id(0)
     tokens, block = gb_s.shape
@@ -619,19 +796,30 @@
     tiles = tokens // tile
     subs = tile // 8
 
+    begin, tick, end = ring_beside(n, up, up_o, *ring_refs)
+
     @pl.when(step == 0)
     def _():
+        begin()
         acc[...] = jnp.zeros_like(acc)
 
+    beat = lambda at: tick(at % 2, step * 3 + at // 2)
+    beat(0)
     mid = tokens // 2
     gb_s[:mid] = dot(g1a[:, :half], ow0[...]) + dot(g1a[:, half:], ow1[...])
     gb_s[mid:] = dot(g1b[:, :half], ow0[...]) + dot(g1b[:, half:], ow1[...])
+    beat(1)
     go0[...] = (dot(g1ta[:half], br[:mid]) + dot(g1tb[:half], br[mid:])).astype(BF16)
     go1[...] = (dot(g1ta[half:], br[:mid]) + dot(g1tb[half:], br[mid:])).astype(BF16)
+    beat(2)
     sums[...] = jnp.zeros_like(sums)
     row = lax.broadcasted_iota(jnp.int32, (8, 128), 0)
 
     def back_step(j, held):
+        @pl.when(j == tiles // 2)
+        def _():
+            beat(3)
+
         i = tiles - 1 - j
         base = pl.multiple_of(i * tile, tile)
         rows = pl.ds(base, tile)
@@ -686,12 +874,13 @@
 
     zero = jnp.zeros((1, 128), F32)
     lax.fori_loop(0, tiles, back_step, tuple((zero, zero) for _ in range(heads)))
+    beat(4)
     for h in range(heads):
         sl = slice(h * 128, (h + 1) * 128)
         low = cl[:, sl]
         ggw[h, :, 0:128] = dot_tn(low, grp_s[:, sl]).astype(BF16)
         ggw[h, :, 128:256] = dot_tn(low, gip_s[:, sl]).astype(BF16)
-        gc_s[:, sl] += dot_nt(grp_s[:, sl], gw[h, :, 0:128]) + dot_nt(gip_s[:, sl], gw[h, :, 128:256])
+        gc_s[:, sl] += dot_nt(grp_s[:, sl], rw[h]) + dot_nt(gip_s[:, sl], iw[h])
 
     def conv_step(j, held):
         i = tiles - 1 - j
@@ -722,6 +911,7 @@
         return tuple(out)
 
     lax.fori_loop(0, tiles, conv_step, tuple(jnp.zeros((8, 128), F32) for _ in range(heads)))
+    beat(5)
     grad_rec = grec_s[...]
     grad_gate = ggp_s[...]
     gr0[...] = dot(n1t[:half], grad_rec).astype(BF16)
@@ -734,8 +924,15 @@
     @pl.when(step == pl.num_programs(0) - 1)
     def _():
         gain_s[...] = jnp.zeros_like(gain_s)
+        for g in range(2):
+            tick(g, 12)
 
         def stat_step(i, _):
+            @pl.when(i == tokens // 32)
+            def _():
+                for g in range(2):
+                    tick(g, 13)
+
             rows = pl.ds(pl.multiple_of(i * 16, 16), 16)
             part = acc[rows, :]
             gn1_o[rows, :] = part.astype(BF16)
@@ -750,37 +947,44 @@
             return 0
 
         lax.fori_loop(0, tokens // 16, stat_step, 0)
-        both = gain_a[...] + gain_b[...]
+        both = gain_two[...]
         for out, sl in ((gains0, slice(0, half)), (gains1, slice(half, wide))):
             out[...] = jnp.zeros_like(out)
             out[0:8, :] = gain_s[:, sl]
             out[8:16, :] = both[:, sl]
+        end()
 
 
 def rec_backward(
-    g1, g1t, n1t, st, gate, r, g, cl, rec, br, ow, wr, wg, gw, cw, sp, x, gain, gain_a, gain_b, block=256, tile=32
+    g1, g1t, n1t, st, gate, r, g, cl, rec, br, ow, wr, wg, rw, iw, cw, sp, x, gain, gain_two, up, n, block=256, tile=64
 ):
     wide, tokens = n1t.shape
     half, width = wr[0].shape
     heads = block // 128
     mid = tokens // 2
+    rows = up.shape[0]
+    up = jnp.pad(up, ((0, -rows % (16 * n)), (0, 0)))
+    slots = pltpu.VMEM((2, n, up.shape[0] // n, up.shape[1] // 2), BF16)
+    dma = pltpu.SemaphoreType.DMA
+    hbm = pl.BlockSpec(memory_space=pl.ANY)
     whole = lambda shape: pl.BlockSpec(shape, lambda i: (0, 0), pipeline_mode=pl.Buffered(1))
     act = pl.BlockSpec((tokens, block), lambda i: (0, i))
     weight = pl.BlockSpec((half, block), lambda i: (0, i))
     thin = lambda n: pl.BlockSpec((n, block), lambda i: (0, i))
     gate_block = pl.BlockSpec((heads, 128, 256), lambda i: (i, 0, 0))
     grad = jax.ShapeDtypeStruct((half, width), BF16)
-    return pl.pallas_call(
-        functools.partial(rec_backward_kernel, tile),
+    outs = pl.pallas_call(
+        functools.partial(rec_backward_kernel, tile, n),
         grid=(width // block,),
         in_specs=[whole((mid, wide))] * 2 + [whole((wide, mid))] * 2 + [whole((wide, tokens))]
         + [act] * 7
         + [weight] * 6
-        + [gate_block, thin(KCONV), thin(1)]
-        + [whole((tokens, wide)), whole((1, wide)), whole((8, wide)), whole((8, wide))],
+        + [pl.BlockSpec((heads, 128, 128), lambda i: (i, 0, 0))] * 2
+        + [thin(KCONV), thin(1)]
+        + [whole((tokens, wide)), whole((1, wide)), whole((8, wide)), hbm],
         out_specs=[whole((tokens, wide))]
         + [weight] * 6
-        + [gate_block, thin(64), whole((tokens, 128)), whole((64, half)), whole((64, half))],
+        + [gate_block, thin(64), whole((tokens, 128)), whole((64, half)), whole((64, half)), hbm],
         out_shape=[jax.ShapeDtypeStruct((tokens, wide), BF16)]
         + [grad] * 6
         + [
@@ -789,6 +993,7 @@
             jax.ShapeDtypeStruct((tokens, 128), F32),
             jax.ShapeDtypeStruct((64, half), F32),
             jax.ShapeDtypeStruct((64, half), F32),
+            jax.ShapeDtypeStruct(up.shape, BF16),
         ],
         scratch_shapes=[
             pltpu.VMEM((tokens, wide), F32),
@@ -799,13 +1004,18 @@
             pltpu.VMEM((tokens, block), BF16),
             pltpu.VMEM((tokens, block), BF16),
             pltpu.VMEM((8, wide), F32),
+            slots, slots,
+            dma((2, n)), dma((2, 2)), dma((2, 2, n)), dma((2, 2, n)), dma((2, 2, n)), dma((2, 2)),
         ],
-        compiler_params=pltpu.CompilerParams(vmem_limit_bytes=60 * MIB),
+        compiler_params=pltpu.CompilerParams(
+            vmem_limit_bytes=62 * MIB, collective_id=6, has_side_effects=True
+        ),
         name="recurrent_backward",
     )(
         g1[0], g1[1], g1t[0], g1t[1], n1t, st, gate, r, g, cl, rec, br,
-        ow[0], ow[1], wr[0], wr[1], wg[0], wg[1], gw, cw, sp, x, gain, gain_a, gain_b,
+        ow[0], ow[1], wr[0], wr[1], wg[0], wg[1], rw, iw, cw, sp, x, gain, gain_two, up,
     )
+    return (*outs[:-1], outs[-1][:rows])
 
 
 def ring_kernel(n, count, *refs):
@@ -821,14 +1031,7 @@
     core = lax.axis_index("rows")
     chip = lax.axis_index("cols")
 
-    def place_of(index):
-        return lax.select(index % 2 == 0, index // 2, n - 1 - index // 2)
-
-    def index_of(place):
-        return lax.select(place < n // 2, 2 * place, 2 * (n - 1 - place) + 1)
-
-    me = place_of(at)
-    nexts = (index_of(lax.rem(me + 1, n)), index_of(lax.rem(me + n - 1, n)))
+    me, nexts = ring_place(n, at)
     barrier = pltpu.get_barrier_semaphore()
     for neighbour in nexts:
         pl.semaphore_signal(barrier, inc=1, device_id={"dp": neighbour})
@@ -894,12 +1097,8 @@
             moves[1].start()
             moves[3].start()
 
-    def chunk_of(way, s):
-        return lax.rem(me + n - s, n) if way == 0 else lax.rem(me + s, n)
-
     def rows_of(k, way, s):
-        size = own[k].shape[0] // n
-        return pl.ds(pl.multiple_of(chunk_of(way, s) * size, size), size)
+        return ring_rows(n, me, own[k].shape[0], way, s)
 
     def cols_of(k, way):
         wide = own[k].shape[1] // 2
@@ -1135,9 +1334,6 @@
     half = tokens.shape[0]
     wide = 2 * half
 
-    def over_rows(own, other):
-        return (own.astype(F32) + swap(other, "rows").astype(F32)).astype(BF16)
-
     both = lambda weight: (weight, swap(weight, "rows"))
 
     positions = jnp.arange(LEN, dtype=jnp.int32)
@@ -1146,52 +1342,43 @@
     part = LEN // 2
 
     sp = jax.nn.softplus(-decay_param)[None, :]
-    (x, n1t, rec, gate, cl, r, g, st, br, mixed, cot_a, far_a) = rec_forward(
+    (x, n1t, rec, gate, cl, r, g, st, br, mixed, cot_a, far_a, wr_far, wg_far, ow_far) = rec_forward(
         tokens, cotangent, rec_weight, gate_weight, out_weight, mix_gain[:, None],
         recur_weight, input_weight, conv_weight, conv_bias[None, :], recur_bias[None, :],
         input_bias[None, :], sp,
     )
-    wr = both(rec_weight)
-    wg = both(gate_weight)
-    ow = both(out_weight)
+    wr = (rec_weight, wr_far)
+    wg = (gate_weight, wg_far)
+    ow = (out_weight, ow_far)
     fg = both(ffn_gate)
     fu = both(ffn_up)
     fd = both(ffn_down)
     gain_two = jnp.concatenate(both(ffn_gain))[None, :]
     gain_one = jnp.concatenate(both(mix_gain))[None, :]
     keep = diag.astype(F32).reshape(1, 1)
-    gw = jnp.concatenate([recur_weight, input_weight], axis=2)
 
     half_shape = (part, 2 * half)
     res_a, n2t_a, cott_a, ctok_a, out_a, gn2_a, hid_a, ga_a, gb_a, far_b, cot_b = ffn(
         0, part, x, mixed, far_a, cot_a, live_core, gain_two, keep, fg, fu, fd,
-        [mixed[part:], cotangent[:, part:]], [half_shape, (2, half, part)], 3,
+        [mixed, cotangent], [half_shape, (2, half, part)], 3,
     )
     res_b, n2t_b, cott_b, ctok_b, out_b, gn2_b, hid_b, ga_b, gb_b, gn2_far_a = ffn(
         1, part, x, mixed, far_b, cot_b, live_core, gain_two, keep, fg, fu, fd,
         [gn2_a], [half_shape], 4,
     )
-    gg0, gg1, gu0, gu1, gd0, gd1, gn2_far_b = ffn_weights(
-        [n2t_a, n2t_b], [cott_a, cott_b], [hid_a, hid_b], [ga_a, ga_b], [gb_a, gb_b], gn2_b, 5
+    up_sum, gg0, gg1, gd0, gd1, g1_a, g1t_a, g1_b, g1t_b, grad_gain_two = ffn_back(
+        [n2t_a, n2t_b], [cott_a, cott_b], [hid_a, hid_b], [ga_a, ga_b], [gb_a, gb_b],
+        [gn2_a, gn2_b], gn2_far_a, [res_a, res_b], [ctok_a, ctok_b], gain_two, 5,
     )
-    g1_a, g1t_a, gain_a = norm_back(gn2_a, gn2_far_a, res_a, ctok_a, gain_two)
-    g1_b, g1t_b, gain_b = norm_back(gn2_b, gn2_far_b, res_b, ctok_b, gain_two)
-    cut = OFFLOAD
-    sum_gate = lax.psum(over_rows(gg0[:, :cut], gg1[:, :cut]), "dp")
-    gn1_part, go0, go1, gr0, gr1, gt0, gt1, ggw, sums, stat, gains0, gains1 = rec_backward(
-        [g1_a, g1_b], [g1t_a, g1t_b], n1t, st, gate, r, g, cl, rec, br, ow, wr, wg, gw,
-        conv_weight, sp, x, gain_one, gain_a, gain_b,
+    gn1_part, go0, go1, gr0, gr1, gt0, gt1, ggw, sums, stat, gains0, gains1, sum_up = rec_backward(
+        [g1_a, g1_b], [g1t_a, g1t_b], n1t, st, gate, r, g, cl, rec, br, ow, wr, wg, recur_weight,
+        input_weight, conv_weight, sp, x, gain_one, grad_gain_two, up_sum, dp,
     )
-    sum_gate, gu0 = lax.optimization_barrier((sum_gate, gu0))
     gates = ggw.reshape(-1, 256)
-    own = [gu0, gd0, go0, gr0, gt0, gates, sums, gains0]
-    other = [gu1, gd1, go1, gr1, gt1, gates, sums, gains1]
-    if cut < gg0.shape[1]:
-        own.append(gg0[:, cut:])
-        other.append(gg1[:, cut:])
+    own = [gd0, gg0, go0, gr0, gt0, gates, sums, gains0]
+    other = [gd1, gg1, go1, gr1, gt1, gates, sums, gains1]
     total, moved = ring_sum(dp, own, other, [gn1_part, out_a, out_b, stat, g1_a, g1_b])
-    sum_up, sum_down, sum_out, sum_rec, sum_gatew, gates, sums, gains = total[:8]
-    sum_gate = jnp.concatenate([sum_gate] + total[8:], axis=1)
+    sum_down, sum_gate, sum_out, sum_rec, sum_gatew, gates, sums, gains = total
     result, grad_tokens = final(*moved, tokens, mix_gain[:, None], live_chip[None, :])
     gates = gates.astype(F32).reshape(ggw.shape)
     vec = jnp.sum(sums.reshape(8, 8, -1), axis=1)

time: 699 us -> 645 us (0.923)
  local copies, waits for them, and re-layouts: 32 us -> 9.63 us
  waiting for transfers between devices: 20.1 us -> 0.02 us
  between operations: 14.3 us -> 0.79 us
    pallas_call x4 -> x2, Pallas kernels: 119 us -> 149 us  [the longest x1 92.5 us: rec_backward(): pl.pallas_call(functools.partial(rec_backward_kernel, tile, n), grid=(wid...]
    pallas_call x1, Pallas kernels: 275 us -> 251 us  [ring_sum(): pl.pallas_call(functools.partial(ring_kernel, n, count), in_specs=[hbm] *...]
    psum x1 -> x0, waiting for transfers between devices: 12.1 us -> none  [body(): sum_gate = lax.psum(over_rows(gg0[:, :cut], gg1[:, :cut]), 'dp')]
    slice x5 -> x0, local copies, waits for them, and re-layouts: 11.5 us -> none  [the longest x1 2.66 us: body(): mixed[part:]]
    unnamed x60 -> x26, local copies, waits for them, and re-layouts: 12.4 us -> 1.59 us
    ppermute x10 -> x6, waiting for transfers between devices: 8.02 us -> 0.02 us  [swap(): return lax.ppermute(value, axis, [(0, 1), (1, 0)])]
  transfers between devices with their start and end apart: 11 -> 6, of which waited for: 3 -> 0; matrix products, arithmetic and copies ran while one was open for 6% -> 5% of each run, Pallas kernels for 25% -> 15%
where the time goes in v3:
time: 645 us
  Pallas kernels  608 us (94%)
  other arithmetic  24.5 us (4%)
  local copies, waits for them, and re-layouts  9.63 us (1%)
    pallas_call x1, Pallas kernels, ring_sum(): pl.pallas_call(functools.partial(ring_kernel, n, count), in_specs=[hbm] *...  251 us
    pallas_call x2, Pallas kernels, ffn(): pl.pallas_call(functools.partial(ffn_kernel, tile, len(srcs)), grid=(widt...  109 us
    pallas_call x1, Pallas kernels, rec_forward(): pl.pallas_call(functools.partial(rec_forward_kernel, chunk, count, cot_pa...  92.9 us
    pallas_call x1, Pallas kernels, rec_backward(): pl.pallas_call(functools.partial(rec_backward_kernel, tile, n), grid=(wid...  92.5 us
    pallas_call x1, Pallas kernels, ffn_back(): pl.pallas_call(ffn_back_kernel, grid=(count,), in_specs=[across] * 4 + [m...  56.3 us
  transfers between devices with their start and end apart: 6, of which 0 were waited for; matrix products, arithmetic and copies ran while one was open for 5% of the time, Pallas kernels for 15%

profile of v3, /device:TPU:0, one launch (start us, length us, event | category | flops | bytes accessed | tf_op | source)
XLA Modules:
  0.0 645.0 jit_solution(13074323720896496462)
XLA Ops:
  2.2 1.3 fusion.2
  3.5 1.2 compare_convert_fusion.1.live
  4.8 1.3 compare_select_fusion
  6.1 0.7 compare_convert_fusion.live
  6.7 1.6 broadcast_in_dim.31.gain_h.gain
  8.3 92.9 %recurrent_forward.1 = (bf16[1024,1536]{1,0:T(8,128)(2,1)}, bf16[1536,1024]{1,0:T(8,128)(2,1)}, f32[1024,1024]{1,0:T(8,128)}, f32[1024,1024]{1,0:T(8,128)}, bf16...) custom-call(bf16[768,1024]{1,0:T(8,128)(2,1)} %tokens.3, ...), custom_call_target="tpu_custom_call" | custom-call | tf_op jit(solution)/shard_map/recurrent_forward/pallas_call | solution.py:325
  102.4 62.2 %ffn_0.1 = (f32[512,1536]{1,0:T(8,128)}, bf16[1536,512]{1,0:T(8,128)(2,1)}, bf16[1536,512]{1,0:T(8,128)(2,1)}, bf16[512,1536]{1,0:T(8,128)(2,1)}, bf16[512,1536]...) custom-call(bf16[1024,1536]{1,0:T(8,128)(2,1)} %get-tuple-element.90, ...), custom_call_target="tpu_custom_call" | custom-call | tf_op jit(solution)/shard_map/ffn_0/pallas_call | solution.py:511
  164.7 46.3 %ffn_1.1 = (f32[512,1536]{1,0:T(8,128)}, bf16[1536,512]{1,0:T(8,128)(2,1)}, bf16[1536,512]{1,0:T(8,128)(2,1)}, bf16[512,1536]{1,0:T(8,128)(2,1)}, bf16[512,1536]...) custom-call(bf16[1024,1536]{1,0:T(8,128)(2,1)} %get-tuple-element.90, ...), custom_call_target="tpu_custom_call" | custom-call | tf_op jit(solution)/shard_map/ffn_1/pallas_call | solution.py:511
  211.0 56.3 %ffn_back.1 = (bf16[768,2304]{1,0:T(8,128)(2,1)}, bf16[768,2304]{1,0:T(8,128)(2,1)}, bf16[768,2304]{1,0:T(8,128)(2,1)}, bf16[768,2304]{1,0:T(8,128)(2,1)}, bf16[...) custom-call(bf16[1536,512]{1,0:T(8,128)(2,1)} %get-tuple-element.94., ...), custom_call_target="tpu_custom_call" | custom-call | tf_op jit(solution)/shard_map/ffn_back/pallas_call | solution.py:626
  267.3 92.5 %recurrent_backward.1 = (bf16[1024,1536]{1,0:T(8,128)(2,1)}, bf16[768,1024]{1,0:T(8,128)(2,1)}, bf16[768,1024]{1,0:T(8,128)(2,1)}, bf16[768,1024]{1,0:T(8,128)(2...) custom-call(bf16[512,1536]{1,0:T(8,128)(2,1)} %get-tuple-element.115, ...), custom_call_target="tpu_custom_call" | custom-call | tf_op jit(solution)/shard_map/recurrent_backward/pallas_call | solution.py:976
  359.8 251.1 %ring_sum.1 = (bf16[768,2304]{1,0:T(8,128)(2,1)}, bf16[768,2304]{1,0:T(8,128)(2,1)}, bf16[768,1024]{1,0:T(8,128)(2,1)}, bf16[768,1024]{1,0:T(8,128)(2,1)}, bf16[...) custom-call(bf16[768,2304]{1,0:T(8,128)(2,1)} %get-tuple-element.113, ...), custom_call_target="tpu_custom_call" | custom-call | tf_op jit(solution)/shard_map/ring_sum/pallas_call | solution.py:1267
  611.0 0.9 bitcast_reduce_fusion.1
  612.4 0.9 collective-permute-start.5
  613.4 2.1 fusion
  616.1 0.6 negate_multiply_fusion
  616.8 0.6 slice.42
  617.4 5.6 convert_element_type.45
  623.0 3.5 convert_element_type.47
  626.5 2.1 convert_element_type.42
  628.5 2.1 convert_element_type.43
  630.6 2.1 convert_element_type.44
  632.7 1.1 copy-done.4
  633.8 3.9 convert_element_type.46
  638.1 6.3 final.1
  (44 shorter events, 5.2 us)
Async XLA Ops:
  0.7 101.8 %collective-permute-start.1 = (bf16[768,2304]{1,0:T(8,128)(2,1)}, bf16[768,2304]{1,0:T(8,128)(2,1)}, u32[]{:S(2)}, u32[]{:S(2)}) collective-permute-start(bf16[768,2304]{1,0:T(8,128)(2,1)} %wg0.4), channel_id=1, source_target_pairs={{0,2},{2,0},{1,3},{3,1},{4,6},{6,4},{5,7},{7,5},{8,10},{10,8},{9,1... | collective-permute-start | bytes 10616840 | tf_op jit(solution)/shard_map/ppermute | solution.py:24
  1.2 101.3 %collective-permute-start.2 = (bf16[768,2304]{1,0:T(8,128)(2,1)}, bf16[768,2304]{1,0:T(8,128)(2,1)}, u32[]{:S(2)}, u32[]{:S(2)}) collective-permute-start(bf16[768,2304]{1,0:T(8,128)(2,1)} %wu0.3), channel_id=1, source_target_pairs={{0,2},{2,0},{1,3},{3,1},{4,6},{6,4},{5,7},{7,5},{8,10},{10,8},{9,1... | collective-permute-start | bytes 10616840 | tf_op jit(solution)/shard_map/ppermute | solution.py:24
  1.3 101.2 %collective-permute-start.3 = (bf16[768,2304]{1,0:T(8,128)(2,1)}, bf16[768,2304]{1,0:T(8,128)(2,1)}, u32[]{:S(2)}, u32[]{:S(2)}) collective-permute-start(bf16[768,2304]{1,0:T(8,128)(2,1)} %wd0.3), channel_id=1, source_target_pairs={{0,2},{2,0},{1,3},{3,1},{4,6},{6,4},{5,7},{7,5},{8,10},{10,8},{9,1... | collective-permute-start | bytes 10616840 | tf_op jit(solution)/shard_map/ppermute | solution.py:24
  1.7 99.5 %collective-permute-start = (f32[768]{0:T(1024)}, f32[768]{0:T(1024)S(1)}, u32[]{:S(2)}, u32[]{:S(2)}) collective-permute-start(f32[768]{0:T(1024)} %param.31), channel_id=1, source_target_pairs={{0,2},{2,0},{1,3},{3,1},{4,6},{6,4},{5,7},{7,5},{8,10},{10,8},{9,1... | collective-permute-start | bytes 9224 | tf_op jit(solution)/shard_map/ppermute | solution.py:24
  1.8 100.1 %collective-permute-start.4 = (f32[768]{0:T(1024)}, f32[768]{0:T(1024)S(1)}, u32[]{:S(2)}, u32[]{:S(2)}) collective-permute-start(f32[768]{0:T(1024)} %param.20), channel_id=1, source_target_pairs={{0,2},{2,0},{1,3},{3,1},{4,6},{6,4},{5,7},{7,5},{8,10},{10,8},{9,1... | collective-permute-start | bytes 9224 | tf_op jit(solution)/shard_map/ppermute | solution.py:24
  8.3 92.9 %copy-start.12 = (f32[768]{0:T(1024)S(1)}, f32[768]{0:T(1024)}, u32[]{:S(2)}) copy-start(f32[768]{0:T(1024)} %param.31) | copy-start | bytes 9220
  8.3 93.5 %copy-start.10 = (f32[768]{0:T(1024)S(1)}, f32[768]{0:T(1024)}, u32[]{:S(2)}) copy-start(f32[768]{0:T(1024)} %param.20) | copy-start | bytes 9220
  610.9 4.5 copy-start.9
  610.9 5.2 copy-start.11
  612.4 32.0 %collective-permute-start.5 = (f32[768]{0:T(1024)S(1)}, f32[768]{0:T(1024)S(1)}, u32[]{:S(2)}, u32[]{:S(2)}) collective-permute-start(f32[768]{0:T(1024)S(1)} %get-tuple-element.164), channel_id=1, source_target_pairs={{0,1},{1,0},{2,3},{3,2},{4,5},{5,4},{6,7},{7,6},{8,9},{9,8},{10,11... | collective-permute-start | bytes 9224 | tf_op jit(solution)/shard_map/ppermute | solution.py:24
  617.4 5.6 copy-start.5
  623.0 3.5 copy-start.8
  626.5 2.1 copy-start.7
  628.5 2.1 copy-start.6
  630.6 3.1 copy-start.4
  633.7 3.9 copy-start
  633.7 3.9 copy-start.1
  633.7 3.9 copy-start.2
  633.7 4.4 copy-start.3

commit v4 on v3

--- a/solution.py
+++ b/solution.py
@@ -312,7 +312,7 @@
     width = wr.shape[1]
     heads = width // 128
     count = length // chunk
-    cot_parts = count // 2
+    cot_parts = 1
     wide = 2 * half
     row_block = lambda cols: pl.BlockSpec((chunk, cols), lambda i: (i, 0))
     whole = lambda shape: pl.BlockSpec(
@@ -372,100 +372,116 @@
     )(tokens, cotangent, wr, wg, ow, gain, rw, iw, cw, cb, rb, ib, sp)
 
 
-def exchange(srcs, dsts, send, recv, at, core, chip):
-    def moves(m):
-        src, dst = srcs[m], dsts[m]
-        if len(dst.shape) == 2:
-            return (
-                pltpu.make_async_remote_copy(src, dst, send.at[m, 0], recv.at[m, 0], device_id={"cols": 1 - chip}),
-            )
-        slot = lax.select(core == chip, 0, 1)
-        there = dst.at[slot]
+def ffn_kernel(
+    count, blocks,
+    x, mix, live, gain, keep, wg0, wg1, wu0, wu1, wd0, wd1, mixed, cotangent, far_first, cot_first,
+    out_o, gu_sum, gg0, gg1, gd0, gd1, g1_o, g1t_o, gain_o,
+    far_s, ct_s, ctok_s, n2_s, n2t_s, hid_s, ga_s, gb_s, out_acc, gn_acc, gn_s, gn_far,
+    keep_s, give_s, got_s,
+    far_send, far_recv, ct_send, ct_recv, gn_send, gn_recv, up_send, up_recv, free_sem,
+):
+    step = pl.program_id(0)
+    core, chip = lax.axis_index("rows"), lax.axis_index("cols")
+    chunk, wide = n2_s.shape
+    half, block = gg0.shape
+    first_part = count * blocks
+    slot = lax.select(core == chip, 0, 1)
+    beside = {"cols": 1 - chip}
+
+    def far_move(c):
+        return pltpu.make_async_remote_copy(
+            mixed.at[pl.ds(c * chunk, chunk), :], far_s.at[c], far_send.at[c], far_recv.at[c], device_id=beside
+        )
+
+    def far_load():
+        return pltpu.make_async_copy(far_first, far_s.at[0], far_recv.at[0])
+
+    def cot_moves(c):
+        src = cotangent.at[:, pl.ds(c * chunk, chunk)]
+        there = ct_s.at[slot, :, pl.ds(c * chunk, chunk)]
         return (
-            pltpu.make_async_copy(src, there, recv.at[m, slot]),
+            pltpu.make_async_copy(src, there, ct_recv.at[c, slot]),
             pltpu.make_async_remote_copy(
-                src, there, send.at[m, 0], recv.at[m, slot], device_id={"rows": 1 - core}
+                src, there, ct_send.at[c, 0], ct_recv.at[c, slot], device_id={"rows": 1 - core}
             ),
             pltpu.make_async_remote_copy(
-                src, there, send.at[m, 1], recv.at[m, slot], device_id={"rows": chip, "cols": 1 - chip}
+                src, there, ct_send.at[c, 1], ct_recv.at[c, slot],
+                device_id={"rows": chip, "cols": 1 - chip},
             ),
         )
 
-    @pl.when(at == 0)
-    def _():
+    def cot_load(s):
+        return pltpu.make_async_copy(
+            cot_first.at[s], ct_s.at[s, :, pl.ds(0, chunk)], ct_recv.at[0, s]
+        )
+
+    def gn_move(c):
+        return pltpu.make_async_remote_copy(
+            gn_s.at[c], gn_far.at[c], gn_send.at[c], gn_recv.at[c], device_id=beside
+        )
+
+    def send_part(c):
+        far_move(c).start()
+        moves = cot_moves(c)
+        moves[2].start()
+
+        @pl.when(core == chip)
+        def _():
+            moves[0].start()
+
+        @pl.when(core != chip)
+        def _():
+            moves[1].start()
+
+    @pl.when(step == 0)
+    def _():
+        far_load().start()
+        for s in range(2):
+            cot_load(s).start()
         group_barrier(core, chip)
-        for m in range(len(srcs)):
-            move = moves(m)
-            move[-1].start()
-            if len(move) > 1:
-
-                @pl.when(core == chip)
-                def _():
-                    move[0].start()
-
-                @pl.when(core != chip)
-                def _():
-                    move[1].start()
-
-    def finish():
-        for m in range(len(srcs)):
-            move = moves(m)
-            if len(move) == 1:
-                move[0].wait()
-                continue
-            for s in range(2):
-                pltpu.make_async_copy(srcs[m], dsts[m].at[s], recv.at[m, s]).wait()
-            move[2].wait_send()
-
-            @pl.when(core != chip)
-            def _():
-                move[1].wait_send()
-
-    return finish
-
-
-def ffn_kernel(
-    tile, moved,
-    x, mix, mix_far, ct, live, gain, keep, wg0, wg1, wu0, wu1, wd0, wd1, *refs
-):
-    srcs, refs = refs[:moved], refs[moved:]
-    (res_o, n2t_o, cott_o, cot_o, out_o, gn2_o, hid_o, ga_o, gb_o), refs = refs[:9], refs[9:]
-    dsts, (n2_s, out_acc, gn2_acc, send, recv) = refs[:moved], refs[moved:]
-    later = pl.ds(x.shape[0], x.shape[0])
-    if moved == 2:
-        views = [srcs[0].at[later, :], srcs[1].at[:, later]]
-    else:
-        views = [srcs[0].at[...]]
-    finish = exchange(
-        views, dsts, send, recv, pl.program_id(0), lax.axis_index("rows"), lax.axis_index("cols")
-    )
-    step = pl.program_id(0)
-    tokens, wide = x.shape
-    half = wide // 2
-
-    @pl.when(step == 0)
-    def _():
-        out_acc[...] = jnp.zeros_like(out_acc)
-        gn2_acc[...] = jnp.zeros_like(gn2_acc)
-        cott_o[:half] = ct[0] * live[...]
-        cott_o[half:] = ct[1] * live[...]
-        cot_o[...] = cott_o[...].T
-
-        def norm_step(i, _):
+        for c in range(1, count):
+            send_part(c)
+        gain_o[...] = jnp.zeros_like(gain_o)
+
+    def turned_cot(c):
+        cols = pl.ds(pl.multiple_of(c * chunk, chunk), chunk)
+        for s in range(2):
+            ctok_s[:, s * half : (s + 1) * half] = ct_s[s, :, cols].T
+
+    def norm_forward(c):
+        cols = pl.ds(pl.multiple_of(c * chunk, chunk), chunk)
+        pltpu.make_async_copy(far_first, far_s.at[c], far_recv.at[c]).wait()
+        for s in range(2):
+            pltpu.make_async_copy(
+                cot_first.at[s], ct_s.at[s, :, cols], ct_recv.at[c, s]
+            ).wait()
+            ct_s[s, :, cols] = ct_s[s, :, cols] * live[:, cols]
+        turned_cot(c)
+        gn_acc[...] = jnp.zeros_like(gn_acc)
+
+        def rows_step(i, _):
             rows = pl.ds(pl.multiple_of(i * 16, 16), 16)
-            res = x[rows, :].astype(F32) + (mix[rows, :].astype(F32) + mix_far[rows, :].astype(F32))
-            res_o[rows, :] = res
+            res = x[rows, :].astype(F32) + (mix[rows, :].astype(F32) + far_s[c, rows, :].astype(F32))
+            out_acc[rows, :] = keep[...] * res
             scale = lax.rsqrt(jnp.sum(res * res, axis=1, keepdims=True) / wide + EPS)
             n2_s[rows, :] = (res * scale * gain[...]).astype(BF16)
             return 0
 
-        lax.fori_loop(0, tokens // 16, norm_step, 0)
-        n2t_o[...] = n2_s[...].T
-
-    def tile_step(i, _):
-        rows = pl.ds(i * tile, tile)
-        n0, n1 = n2_s[rows, :half], n2_s[rows, half:]
-        c0, c1 = cot_o[rows, :half], cot_o[rows, half:]
+        lax.fori_loop(0, chunk // 16, rows_step, 0)
+        n2t_s[:, cols] = n2_s[...].T
+
+    @pl.when(step < first_part)
+    def _():
+        c = step // blocks
+        blk = step % blocks
+        rows = pl.ds(pl.multiple_of(c * chunk, chunk), chunk)
+
+        @pl.when(blk == 0)
+        def _():
+            norm_forward(c)
+
+        n0, n1 = n2_s[:, :half], n2_s[:, half:]
+        c0, c1 = ctok_s[:, :half], ctok_s[:, half:]
         a = dot(n0, wg0[...]) + dot(n1, wg1[...])
         b = dot(n0, wu0[...]) + dot(n1, wu1[...])
         gh = dot(c0, wd0[...]) + dot(c1, wd1[...])
@@ -473,172 +489,171 @@
         hidden = (act * b).astype(BF16)
         ga = (gh * b * slope).astype(BF16)
         gb = (gh * act).astype(BF16)
-        hid_o[rows, :] = hidden
-        ga_o[rows, :] = ga
-        gb_o[rows, :] = gb
-        out_acc[rows, :half] += dot_nt(hidden, wd0[...])
-        out_acc[rows, half:] += dot_nt(hidden, wd1[...])
-        gn2_acc[rows, :half] += dot_nt(ga, wg0[...]) + dot_nt(gb, wu0[...])
-        gn2_acc[rows, half:] += dot_nt(ga, wg1[...]) + dot_nt(gb, wu1[...])
-        return 0
-
-    for i in range(tokens // tile):
-        tile_step(i, 0)
-
-    @pl.when(step == pl.num_programs(0) - 1)
-    def _():
-        out_o[...] = (out_acc[...] + keep[...] * res_o[...]).astype(BF16)
-        gn2_o[...] = gn2_acc[...].astype(BF16)
-        finish()
-
-
-def ffn(part, tokens, x, mix, mix_far, cott, live, gain, keep, wg, wu, wd, srcs, dsts, collective_id, block=256, tile=256):
-    wide = x.shape[1]
+        hid_s[blk, rows, :] = hidden
+        ga_s[blk, rows, :] = ga
+        gb_s[blk, rows, :] = gb
+        out_acc[:, :half] += dot_nt(hidden, wd0[...])
+        out_acc[:, half:] += dot_nt(hidden, wd1[...])
+        gn_acc[:, :half] += dot_nt(ga, wg0[...]) + dot_nt(gb, wu0[...])
+        gn_acc[:, half:] += dot_nt(ga, wg1[...]) + dot_nt(gb, wu1[...])
+
+        @pl.when(blk == blocks - 1)
+        def _():
+            out_o[...] = out_acc[...].astype(BF16)
+            gn_s[c] = gn_acc[...].astype(BF16)
+            gn_move(c).start()
+
+    def norm_back(c):
+        turned_cot(c)
+        gn_move(c).wait_recv()
+
+        def rows_step(i, _):
+            rows = pl.ds(pl.multiple_of(i * 16, 16), 16)
+            grad = gn_s[c, rows, :].astype(F32) + gn_far[c, rows, :].astype(F32)
+            held = x[rows, :].astype(F32) + (mix[rows, :].astype(F32) + far_s[c, rows, :].astype(F32))
+            scale = lax.rsqrt(jnp.sum(held * held, axis=1, keepdims=True) / wide + EPS)
+            product = grad * held
+            by_gain = product * scale
+            gain_o[...] += by_gain[0:8] + by_gain[8:16]
+            inner = jnp.sum(product * gain[...], axis=1, keepdims=True)
+            grad_one = (
+                ctok_s[rows, :].astype(F32)
+                + scale * (grad * gain[...])
+                - held * (scale * scale * scale * inner / wide)
+            )
+            g1_o[rows, :] = grad_one.astype(BF16)
+            return 0
+
+        lax.fori_loop(0, chunk // 16, rows_step, 0)
+        g1t_o[...] = g1_o[...].T
+
+    def give(k):
+        at = k % 2
+        return pltpu.make_async_remote_copy(
+            give_s.at[at], got_s.at[at], up_send.at[at], up_recv.at[at], device_id={"rows": 1 - core}
+        )
+
+    k = step - first_part
+
+    @pl.when(jnp.logical_and(k > 0, k <= blocks))
+    def _():
+        give(k - 1).wait()
+        total = keep_s[(k - 1) % 2].astype(F32) + got_s[(k - 1) % 2].astype(F32)
+        gu_sum[...] = total.astype(BF16)
+
+        @pl.when(k - 1 < blocks - 2)
+        def _():
+            pl.semaphore_signal(free_sem, inc=1, device_id={"rows": 1 - core})
+
+    @pl.when(jnp.logical_and(k >= 0, k < blocks))
+    def _():
+        up, down, gate = gb_s[k], hid_s[k], ga_s[k]
+        give_s[k % 2] = dot(n2t_s[half:], up).astype(BF16)
+
+        @pl.when(k >= 2)
+        def _():
+            pl.semaphore_wait(free_sem, 1)
+
+        give(k).start()
+        keep_s[k % 2] = dot(n2t_s[:half], up).astype(BF16)
+        gg0[...] = dot(n2t_s[:half], gate).astype(BF16)
+        gg1[...] = dot(n2t_s[half:], gate).astype(BF16)
+        gd0[...] = dot(ct_s[0], down).astype(BF16)
+        gd1[...] = dot(ct_s[1], down).astype(BF16)
+
+    for c in range(count):
+
+        @pl.when(k == (2 * c + 1 if c < count - 1 else blocks))
+        def _():
+            norm_back(c)
+
+    @pl.when(k == blocks)
+    def _():
+        for c in range(count):
+            gn_move(c).wait_send()
+        for c in range(1, count):
+            far_move(c).wait_send()
+            moves = cot_moves(c)
+            moves[2].wait_send()
+
+            @pl.when(core != chip)
+            def _():
+                moves[1].wait_send()
+
+
+def ffn(x, mix, live, gain, keep, wg, wu, wd, cotangent, far_first, cot_first, chunk=256, block=256):
+    tokens, wide = x.shape
     half, width = wg[0].shape
-    whole = lambda shape, at=(0, 0): pl.BlockSpec(
-        shape, lambda i: at, pipeline_mode=pl.Buffered(1)
+    count, blocks = tokens // chunk, width // block
+    first_part = count * blocks
+    whole = lambda shape: pl.BlockSpec(
+        shape, lambda i: (0,) * len(shape), pipeline_mode=pl.Buffered(1)
     )
     hbm = pl.BlockSpec(memory_space=pl.ANY)
-    rows = whole((tokens, wide), (part, 0))
-    act = whole((tokens, wide))
-    across = whole((wide, tokens))
-    weight = pl.BlockSpec((half, block), lambda i: (0, i))
-    mid = pl.BlockSpec((tokens, block), lambda i: (0, i))
+
+    def back_chunk(i):
+        return jnp.clip((i - first_part) // 2, 0, count - 1)
+
+    def chunk_at(i):
+        return jnp.where(i < first_part, i // blocks, back_chunk(i))
+
+    rows = pl.BlockSpec((chunk, wide), lambda i: (chunk_at(i), 0))
+    weight = pl.BlockSpec(
+        (half, block), lambda i: (0, jnp.where(i < first_part, i % blocks, blocks - 1))
+    )
+    grad_at = lambda late: pl.BlockSpec(
+        (half, block), lambda i: (0, jnp.clip(i - first_part - late, 0, blocks - 1))
+    )
+    grad = jax.ShapeDtypeStruct((half, width), BF16)
     low = jax.ShapeDtypeStruct((tokens, wide), BF16)
-    turned = jax.ShapeDtypeStruct((wide, tokens), BF16)
-    hidden = jax.ShapeDtypeStruct((tokens, width), BF16)
-    sems = pltpu.SemaphoreType.DMA((len(srcs), 2))
+    part = pltpu.VMEM((count, chunk, wide), BF16)
+    middle = pltpu.VMEM((blocks, tokens, block), BF16)
+    pair = pltpu.VMEM((2, half, block), BF16)
+    dma = pltpu.SemaphoreType.DMA
     return pl.pallas_call(
-        functools.partial(ffn_kernel, tile, len(srcs)),
-        grid=(width // block,),
-        in_specs=[rows, rows, act, whole((2, half, tokens), (0, 0, 0)), whole((1, tokens), (0, part))]
-        + [whole((1, wide)), whole((1, 1))]
+        functools.partial(ffn_kernel, count, blocks),
+        grid=(first_part + blocks + 1,),
+        in_specs=[rows, rows, whole((1, tokens)), whole((1, wide)), whole((1, 1))]
         + [weight] * 6
-        + [hbm] * len(srcs),
-        out_specs=[act, across, across, act, act, act, mid, mid, mid] + [hbm] * len(srcs),
-        out_shape=[
-            jax.ShapeDtypeStruct((tokens, wide), F32),
-            turned, turned, low, low, low, hidden, hidden, hidden,
+        + [hbm] * 4,
+        out_specs=[
+            pl.BlockSpec((chunk, wide), lambda i: (jnp.minimum(i // blocks, count - 1), 0)),
+            grad_at(1),
         ]
-        + [jax.ShapeDtypeStruct(shape, BF16) for shape in dsts],
+        + [grad_at(0)] * 4
+        + [
+            pl.BlockSpec((chunk, wide), lambda i: (back_chunk(i), 0)),
+            pl.BlockSpec((wide, chunk), lambda i: (0, back_chunk(i))),
+            whole((8, wide)),
+        ],
+        out_shape=[low]
+        + [grad] * 5
+        + [low, jax.ShapeDtypeStruct((wide, tokens), BF16), jax.ShapeDtypeStruct((8, wide), F32)],
         scratch_shapes=[
-            pltpu.VMEM((tokens, wide), BF16),
-            pltpu.VMEM((tokens, wide), F32),
-            pltpu.VMEM((tokens, wide), F32),
-            sems,
-            sems,
+            part,
+            pltpu.VMEM((2, half, tokens), BF16),
+            pltpu.VMEM((chunk, wide), BF16),
+            pltpu.VMEM((chunk, wide), BF16),
+            pltpu.VMEM((wide, tokens), BF16),
+            middle, middle, middle,
+            pltpu.VMEM((chunk, wide), F32),
+            pltpu.VMEM((chunk, wide), F32),
+            part, part,
+            pair, pair, pair,
+            dma((count,)), dma((count,)),
+            dma((count, 2)), dma((count, 2)),
+            dma((count,)), dma((count,)),
+            dma((2,)), dma((2,)),
+            pltpu.SemaphoreType.REGULAR,
         ],
         compiler_params=pltpu.CompilerParams(
-            vmem_limit_bytes=60 * MIB, collective_id=collective_id, has_side_effects=True
+            vmem_limit_bytes=62 * MIB, collective_id=3, has_side_effects=True
         ),
-        name=f"ffn_{part}",
-    )(x, mix, mix_far, cott, live, gain, keep, wg[0], wg[1], wu[0], wu[1], wd[0], wd[1], *srcs)
-
-
-def norm_back(gn, gn_far, res, cot, gain, g1_o, g1t_o, gain_o):
-    rows_all, wide = g1_o.shape
-
-    def step(i, _):
-        rows = pl.ds(pl.multiple_of(i * 16, 16), 16)
-        grad = gn[rows, :].astype(F32) + gn_far[rows, :].astype(F32)
-        held = res[rows, :]
-        scale = lax.rsqrt(jnp.sum(held * held, axis=1, keepdims=True) / wide + EPS)
-        product = grad * held
-        by_gain = product * scale
-        gain_o[...] += by_gain[0:8] + by_gain[8:16]
-        inner = jnp.sum(product * gain[...], axis=1, keepdims=True)
-        grad_one = (
-            cot[rows, :].astype(F32)
-            + scale * (grad * gain[...])
-            - held * (scale * scale * scale * inner / wide)
-        )
-        g1_o[rows, :] = grad_one.astype(BF16)
-        return 0
-
-    lax.fori_loop(0, rows_all // 16, step, 0)
-    g1t_o[...] = g1_o[...].T
-
-
-def ffn_back_kernel(
-    n2t_a, n2t_b, cott_a, cott_b, hid_a, hid_b, ga_a, ga_b, gb_a, gb_b,
-    gn_a, gn_far_a, gn_b, res_a, res_b, cot_a, cot_b, gain,
-    gu_sum, gg0, gg1, gd0, gd1, g1_a, g1t_a, g1_b, g1t_b, gain_o,
-    gn_far_b, keep_s, give_s, got_s, send, recv, up_send, up_recv,
-):
-    step = pl.program_id(0)
-    last = pl.num_programs(0) - 1
-    core, chip = lax.axis_index("rows"), lax.axis_index("cols")
-    finish = exchange([gn_b.at[...]], [gn_far_b], send, recv, step, core, chip)
-    half, block = gg0.shape
-
-    def give(k):
-        return pltpu.make_async_remote_copy(
-            give_s.at[k], got_s.at[k], up_send.at[k], up_recv.at[k], device_id={"rows": 1 - core}
-        )
-
-    def join(k):
-        give(k).wait()
-        total = keep_s[k].astype(F32) + got_s[k].astype(F32)
-        gu_sum[:, pl.ds(pl.multiple_of(k * block, block), block)] = total.astype(BF16)
-
-    @pl.when(step == 0)
-    def _():
-        gain_o[...] = jnp.zeros_like(gain_o)
-        norm_back(gn_a, gn_far_a, res_a, cot_a, gain, g1_a, g1t_a, gain_o)
-
-    def product(left_a, left_b, right_a, right_b, top):
-        sl = slice(0, half) if top else slice(half, 2 * half)
-        return (dot(left_a[sl], right_a[...]) + dot(left_b[sl], right_b[...])).astype(BF16)
-
-    give_s[step] = product(n2t_a, n2t_b, gb_a, gb_b, False)
-    give(step).start()
-    keep_s[step] = product(n2t_a, n2t_b, gb_a, gb_b, True)
-    gg0[...] = product(n2t_a, n2t_b, ga_a, ga_b, True)
-    gg1[...] = product(n2t_a, n2t_b, ga_a, ga_b, False)
-    gd0[...] = product(cott_a, cott_b, hid_a, hid_b, True)
-    gd1[...] = product(cott_a, cott_b, hid_a, hid_b, False)
-
-    @pl.when(step > 0)
-    def _():
-        join(step - 1)
-
-    @pl.when(step == last)
-    def _():
-        finish()
-        norm_back(gn_b, gn_far_b, res_b, cot_b, gain, g1_b, g1t_b, gain_o)
-        join(step)
-
-
-def ffn_back(n2t, cott, hid, ga, gb, gn, gn_far_a, res, cot, gain, collective_id, block=256):
-    wide, tokens = n2t[0].shape
-    half, width = wide // 2, hid[0].shape[1]
-    count = width // block
-    whole = lambda shape: pl.BlockSpec(shape, lambda i: (0, 0), pipeline_mode=pl.Buffered(1))
-    mid = pl.BlockSpec((tokens, block), lambda i: (0, i))
-    grad = jax.ShapeDtypeStruct((half, width), BF16)
-    act, across = whole((tokens, wide)), whole((wide, tokens))
-    weight = pl.BlockSpec((half, block), lambda i: (0, i))
-    sems = pltpu.SemaphoreType.DMA((1, 2))
-    up_sems = pltpu.SemaphoreType.DMA((count,))
-    low = jax.ShapeDtypeStruct((tokens, wide), BF16)
-    turned = jax.ShapeDtypeStruct((wide, tokens), BF16)
-    blocks = pltpu.VMEM((count, half, block), BF16)
-    return pl.pallas_call(
-        ffn_back_kernel,
-        grid=(count,),
-        in_specs=[across] * 4 + [mid] * 6 + [act] * 7 + [whole((1, wide))],
-        out_specs=[whole((half, width))]
-        + [weight] * 4
-        + [act, across, act, across, whole((8, wide))],
-        out_shape=[grad] * 5 + [low, turned, low, turned, jax.ShapeDtypeStruct((8, wide), F32)],
-        scratch_shapes=[
-            pltpu.VMEM((tokens, wide), BF16), blocks, blocks, blocks, sems, sems, up_sems, up_sems,
-        ],
-        compiler_params=pltpu.CompilerParams(
-            vmem_limit_bytes=60 * MIB, collective_id=collective_id, has_side_effects=True
-        ),
-        name="ffn_back",
-    )(*n2t, *cott, *hid, *ga, *gb, gn[0], gn_far_a, gn[1], *res, *cot, gain)
+        name="ffn",
+    )(
+        x, mix, live, gain, keep, wg[0], wg[1], wu[0], wu[1], wd[0], wd[1],
+        mix, cotangent, far_first, cot_first,
+    )
 
 
 def ring_place(n, at):
@@ -783,7 +798,7 @@
 
 def rec_backward_kernel(
     tile, n,
-    g1a, g1b, g1ta, g1tb, n1t, st, gate, r_in, i_in, cl, rec, br, ow0, ow1, wr0, wr1, wg0, wg1, rw, iw, cw, sp,
+    g1, g1t, n1t, st, gate, r_in, i_in, cl, rec, br, ow0, ow1, wr0, wr1, wg0, wg1, rw, iw, cw, sp,
     x, gain, gain_two, up,
     gn1_o, go0, go1, gr0, gr1, gg0, gg1, ggw, sums, stat, gains0, gains1, up_o,
     acc, gb_s, gc_s, ggp_s, grp_s, gip_s, grec_s, gain_s, *ring_refs
@@ -805,12 +820,10 @@
 
     beat = lambda at: tick(at % 2, step * 3 + at // 2)
     beat(0)
-    mid = tokens // 2
-    gb_s[:mid] = dot(g1a[:, :half], ow0[...]) + dot(g1a[:, half:], ow1[...])
-    gb_s[mid:] = dot(g1b[:, :half], ow0[...]) + dot(g1b[:, half:], ow1[...])
+    gb_s[...] = dot(g1[:, :half], ow0[...]) + dot(g1[:, half:], ow1[...])
     beat(1)
-    go0[...] = (dot(g1ta[:half], br[:mid]) + dot(g1tb[:half], br[mid:])).astype(BF16)
-    go1[...] = (dot(g1ta[half:], br[:mid]) + dot(g1tb[half:], br[mid:])).astype(BF16)
+    go0[...] = dot(g1t[:half], br[...]).astype(BF16)
+    go1[...] = dot(g1t[half:], br[...]).astype(BF16)
     beat(2)
     sums[...] = jnp.zeros_like(sums)
     row = lax.broadcasted_iota(jnp.int32, (8, 128), 0)
@@ -961,7 +974,6 @@
     wide, tokens = n1t.shape
     half, width = wr[0].shape
     heads = block // 128
-    mid = tokens // 2
     rows = up.shape[0]
     up = jnp.pad(up, ((0, -rows % (16 * n)), (0, 0)))
     slots = pltpu.VMEM((2, n, up.shape[0] // n, up.shape[1] // 2), BF16)
@@ -976,7 +988,7 @@
     outs = pl.pallas_call(
         functools.partial(rec_backward_kernel, tile, n),
         grid=(width // block,),
-        in_specs=[whole((mid, wide))] * 2 + [whole((wide, mid))] * 2 + [whole((wide, tokens))]
+        in_specs=[whole((tokens, wide))] + [whole((wide, tokens))] * 2
         + [act] * 7
         + [weight] * 6
         + [pl.BlockSpec((heads, 128, 128), lambda i: (i, 0, 0))] * 2
@@ -1012,7 +1024,7 @@
         ),
         name="recurrent_backward",
     )(
-        g1[0], g1[1], g1t[0], g1t[1], n1t, st, gate, r, g, cl, rec, br,
+        g1, g1t, n1t, st, gate, r, g, cl, rec, br,
         ow[0], ow[1], wr[0], wr[1], wg[0], wg[1], rw, iw, cw, sp, x, gain, gain_two, up,
     )
     return (*outs[:-1], outs[-1][:rows])
@@ -1020,7 +1032,7 @@
 
 def ring_kernel(n, count, *refs):
     own, other, refs = refs[:count], refs[count : 2 * count], refs[2 * count :]
-    (gn1, out_a, out_b, stat, g1_a, g1_b), refs = refs[:6], refs[6:]
+    (gn1, out, stat, g1), refs = refs[:4], refs[4:]
     outs, refs = refs[:count], refs[count:]
     (gn1_p, out_p, stat_p, g1_p), scratch = refs[:4], refs[4:]
     piece_send, piece_recv = scratch[-2:]
@@ -1040,16 +1052,14 @@
     pl.semaphore_wait(barrier, 5)
 
     half = gn1_p.shape[2]
-    part = out_a.shape[0]
     first, second = slice(0, half), slice(half, 2 * half)
     everything = slice(None)
     pieces = [
         (gn1, gn1_p, slice(None), first, second),
-        (out_a, out_p, slice(0, part), first, second),
-        (out_b, out_p, slice(part, 2 * part), first, second),
+        (out, out_p, slice(None), first, second),
         (stat, stat_p, slice(None), everything, everything),
     ]
-    singles = [(g1_a, slice(0, part)), (g1_b, slice(part, 2 * part))]
+    singles = [(g1, slice(None))]
     diag = core == chip
 
     def piece_moves(m):
@@ -1277,7 +1287,7 @@
         ],
         scratch_shapes=slots * 3
         + [sems, pair, sems, pair] + [sems] * 3 + [pair]
-        + [pltpu.SemaphoreType.DMA((6, 2))] * 2,
+        + [pltpu.SemaphoreType.DMA((4, 2))] * 2,
         compiler_params=pltpu.CompilerParams(
             collective_id=0, has_side_effects=True, vmem_limit_bytes=60 * MIB
         ),
@@ -1339,7 +1349,6 @@
     positions = jnp.arange(LEN, dtype=jnp.int32)
     live_core = (positions < lengths[at_row]).astype(BF16)[None, :]
     live_chip = (positions < lengths[at_col]).astype(F32)
-    part = LEN // 2
 
     sp = jax.nn.softplus(-decay_param)[None, :]
     (x, n1t, rec, gate, cl, r, g, st, br, mixed, cot_a, far_a, wr_far, wg_far, ow_far) = rec_forward(
@@ -1357,27 +1366,17 @@
     gain_one = jnp.concatenate(both(mix_gain))[None, :]
     keep = diag.astype(F32).reshape(1, 1)
 
-    half_shape = (part, 2 * half)
-    res_a, n2t_a, cott_a, ctok_a, out_a, gn2_a, hid_a, ga_a, gb_a, far_b, cot_b = ffn(
-        0, part, x, mixed, far_a, cot_a, live_core, gain_two, keep, fg, fu, fd,
-        [mixed, cotangent], [half_shape, (2, half, part)], 3,
-    )
-    res_b, n2t_b, cott_b, ctok_b, out_b, gn2_b, hid_b, ga_b, gb_b, gn2_far_a = ffn(
-        1, part, x, mixed, far_b, cot_b, live_core, gain_two, keep, fg, fu, fd,
-        [gn2_a], [half_shape], 4,
-    )
-    up_sum, gg0, gg1, gd0, gd1, g1_a, g1t_a, g1_b, g1t_b, grad_gain_two = ffn_back(
-        [n2t_a, n2t_b], [cott_a, cott_b], [hid_a, hid_b], [ga_a, ga_b], [gb_a, gb_b],
-        [gn2_a, gn2_b], gn2_far_a, [res_a, res_b], [ctok_a, ctok_b], gain_two, 5,
+    out, up_sum, gg0, gg1, gd0, gd1, g1, g1t, grad_gain_two = ffn(
+        x, mixed, live_core, gain_two, keep, fg, fu, fd, cotangent, far_a, cot_a
     )
     gn1_part, go0, go1, gr0, gr1, gt0, gt1, ggw, sums, stat, gains0, gains1, sum_up = rec_backward(
-        [g1_a, g1_b], [g1t_a, g1t_b], n1t, st, gate, r, g, cl, rec, br, ow, wr, wg, recur_weight,
+        g1, g1t, n1t, st, gate, r, g, cl, rec, br, ow, wr, wg, recur_weight,
         input_weight, conv_weight, sp, x, gain_one, grad_gain_two, up_sum, dp,
     )
     gates = ggw.reshape(-1, 256)
     own = [gd0, gg0, go0, gr0, gt0, gates, sums, gains0]
     other = [gd1, gg1, go1, gr1, gt1, gates, sums, gains1]
-    total, moved = ring_sum(dp, own, other, [gn1_part, out_a, out_b, stat, g1_a, g1_b])
+    total, moved = ring_sum(dp, own, other, [gn1_part, out, stat, g1])
     sum_down, sum_gate, sum_out, sum_rec, sum_gatew, gates, sums, gains = total
     result, grad_tokens = final(*moved, tokens, mix_gain[:, None], live_chip[None, :])
     gates = gates.astype(F32).reshape(ggw.shape)

time: 645 us -> 611 us (0.947)
  Pallas kernels: 608 us -> 572 us
    pallas_call x1, Pallas kernels: 92.9 us -> 67.5 us  [rec_forward(): pl.pallas_call(functools.partial(rec_forward_kernel, chunk, count, cot_pa...]
    pallas_call x3 -> x1, Pallas kernels: 165 us -> 155 us  [ffn(): pl.pallas_call(functools.partial(ffn_kernel, count, blocks), grid=(first_...]
  transfers between devices with their start and end apart: 6 -> 6, of which waited for: 0 -> 0; matrix products, arithmetic and copies ran while one was open for 5% -> 5% of each run, Pallas kernels for 15% -> 12%
where the time goes in v4:
time: 611 us
  Pallas kernels  572 us (94%)
  other arithmetic  25.4 us (4%)
  local copies, waits for them, and re-layouts  9.63 us (2%)
    pallas_call x1, Pallas kernels, ring_sum(): pl.pallas_call(functools.partial(ring_kernel, n, count), in_specs=[hbm] *...  251 us
    pallas_call x1, Pallas kernels, ffn(): pl.pallas_call(functools.partial(ffn_kernel, count, blocks), grid=(first_...  155 us
    pallas_call x1, Pallas kernels, rec_backward(): pl.pallas_call(functools.partial(rec_backward_kernel, tile, n), grid=(wid...  92.3 us
    pallas_call x1, Pallas kernels, rec_forward(): pl.pallas_call(functools.partial(rec_forward_kernel, chunk, count, cot_pa...  67.5 us
  transfers between devices with their start and end apart: 6, of which 0 were waited for; matrix products, arithmetic and copies ran while one was open for 5% of the time, Pallas kernels for 12%

profile of v4, /device:TPU:0, one launch (start us, length us, event | category | flops | bytes accessed | tf_op | source)
XLA Modules:
  0.0 610.8 jit_solution(16763229572585139637)
XLA Ops:
  2.2 1.3 fusion.2
  3.5 1.2 compare_convert_fusion.1.live
  4.8 1.3 compare_select_fusion
  6.1 0.7 compare_convert_fusion.live
  6.7 1.6 broadcast_in_dim.31.gain_h.gain
  8.3 67.5 %recurrent_forward.1 = (bf16[1024,1536]{1,0:T(8,128)(2,1)}, bf16[1536,1024]{1,0:T(8,128)(2,1)}, f32[1024,1024]{1,0:T(8,128)}, f32[1024,1024]{1,0:T(8,128)}, bf16...) custom-call(bf16[768,1024]{1,0:T(8,128)(2,1)} %tokens.3, ...), custom_call_target="tpu_custom_call" | custom-call | tf_op jit(solution)/shard_map/recurrent_forward/pallas_call | solution.py:325
  77.1 154.5 %ffn.1 = (bf16[1024,1536]{1,0:T(8,128)(2,1)}, bf16[768,2304]{1,0:T(8,128)(2,1)}, bf16[768,2304]{1,0:T(8,128)(2,1)}, bf16[768,2304]{1,0:T(8,128)(2,1)}, bf16[768,...) custom-call(bf16[1024,1536]{1,0:T(8,128)(2,1)} %get-tuple-element.68, ...), custom_call_target="tpu_custom_call" | custom-call | tf_op jit(solution)/shard_map/ffn/pallas_call | solution.py:613
  231.6 92.3 %recurrent_backward.1 = (bf16[1024,1536]{1,0:T(8,128)(2,1)}, bf16[768,1024]{1,0:T(8,128)(2,1)}, bf16[768,1024]{1,0:T(8,128)(2,1)}, bf16[768,1024]{1,0:T(8,128)(2...) custom-call(bf16[1024,1536]{1,0:T(8,128)(2,1)} %get-tuple-element.74, ...), custom_call_target="tpu_custom_call" | custom-call | tf_op jit(solution)/shard_map/recurrent_backward/pallas_call | solution.py:988
  324.0 251.2 %ring_sum.1 = (bf16[768,2304]{1,0:T(8,128)(2,1)}, bf16[768,2304]{1,0:T(8,128)(2,1)}, bf16[768,1024]{1,0:T(8,128)(2,1)}, bf16[768,1024]{1,0:T(8,128)(2,1)}, bf16[...) custom-call(bf16[768,2304]{1,0:T(8,128)(2,1)} %get-tuple-element.72., ...), custom_call_target="tpu_custom_call" | custom-call | tf_op jit(solution)/shard_map/ring_sum/pallas_call | solution.py:1277
  575.1 0.8 bitcast_reduce_fusion.1
  575.9 0.6 slice_reduce_fusion
  576.6 1.6 collective-permute-start.5
  578.2 2.1 fusion
  580.3 1.0 bitcast_reduce_fusion
  581.9 0.6 negate_multiply_fusion
  582.5 0.6 slice.42
  583.2 5.6 convert_element_type.45
  588.8 3.5 convert_element_type.47
  592.3 2.1 convert_element_type.42
  594.3 2.1 convert_element_type.43
  596.4 2.1 convert_element_type.44
  598.5 1.1 copy-done.4
  599.5 3.9 convert_element_type.46
  603.9 6.3 %final.1 = (bf16[768,1024]{1,0:T(8,128)(2,1)}, bf16[768,1024]{1,0:T(8,128)(2,1)}) custom-call(bf16[2,1024,768]{2,1,0:T(8,128)(2,1)} %get-tuple-element.104.gn, bf16[2,1024,768]{2,1,0:T(8,128)(2,1)} %get-tuple-element.105.out, f32[2,1024,128]{2,1,0:T(8,128)S(1)} %copy-done.3, bf16[1024,768]{1,0:T(8,128)(2,1)S(1)} %copy-done.2, bf16[768,1024]{1,0:T(8,128)(2,1)S(1)} %copy-done, ...), custom_call_target="tpu_custom_call" | custom-call | tf_op jit(solution)/shard_map/final/pallas_call | solution.py:1319
  (40 shorter events, 4.5 us)
Async XLA Ops:
  0.7 76.4 %collective-permute-start.1 = (bf16[768,2304]{1,0:T(8,128)(2,1)}, bf16[768,2304]{1,0:T(8,128)(2,1)}, u32[]{:S(2)}, u32[]{:S(2)}) collective-permute-start(bf16[768,2304]{1,0:T(8,128)(2,1)} %wg0.2), channel_id=1, source_target_pairs={{0,2},{2,0},{1,3},{3,1},{4,6},{6,4},{5,7},{7,5},{8,10},{10,8},{9,1... | collective-permute-start | bytes 10616840 | tf_op jit(solution)/shard_map/ppermute | solution.py:24
  1.2 75.9 %collective-permute-start.2 = (bf16[768,2304]{1,0:T(8,128)(2,1)}, bf16[768,2304]{1,0:T(8,128)(2,1)}, u32[]{:S(2)}, u32[]{:S(2)}) collective-permute-start(bf16[768,2304]{1,0:T(8,128)(2,1)} %wu0.1), channel_id=1, source_target_pairs={{0,2},{2,0},{1,3},{3,1},{4,6},{6,4},{5,7},{7,5},{8,10},{10,8},{9,1... | collective-permute-start | bytes 10616840 | tf_op jit(solution)/shard_map/ppermute | solution.py:24
  1.3 75.8 %collective-permute-start.3 = (bf16[768,2304]{1,0:T(8,128)(2,1)}, bf16[768,2304]{1,0:T(8,128)(2,1)}, u32[]{:S(2)}, u32[]{:S(2)}) collective-permute-start(bf16[768,2304]{1,0:T(8,128)(2,1)} %wd0.1), channel_id=1, source_target_pairs={{0,2},{2,0},{1,3},{3,1},{4,6},{6,4},{5,7},{7,5},{8,10},{10,8},{9,1... | collective-permute-start | bytes 10616840 | tf_op jit(solution)/shard_map/ppermute | solution.py:24
  1.7 74.1 %collective-permute-start = (f32[768]{0:T(1024)}, f32[768]{0:T(1024)S(1)}, u32[]{:S(2)}, u32[]{:S(2)}) collective-permute-start(f32[768]{0:T(1024)} %param.31), channel_id=1, source_target_pairs={{0,2},{2,0},{1,3},{3,1},{4,6},{6,4},{5,7},{7,5},{8,10},{10,8},{9,1... | collective-permute-start | bytes 9224 | tf_op jit(solution)/shard_map/ppermute | solution.py:24
  1.8 74.7 %collective-permute-start.4 = (f32[768]{0:T(1024)}, f32[768]{0:T(1024)S(1)}, u32[]{:S(2)}, u32[]{:S(2)}) collective-permute-start(f32[768]{0:T(1024)} %param.20), channel_id=1, source_target_pairs={{0,2},{2,0},{1,3},{3,1},{4,6},{6,4},{5,7},{7,5},{8,10},{10,8},{9,1... | collective-permute-start | bytes 9224 | tf_op jit(solution)/shard_map/ppermute | solution.py:24
  8.3 67.5 %copy-start.11 = (f32[768]{0:T(1024)S(1)}, f32[768]{0:T(1024)}, u32[]{:S(2)}) copy-start(f32[768]{0:T(1024)} %param.31) | copy-start | bytes 9220
  8.3 68.1 %copy-start.9 = (f32[768]{0:T(1024)S(1)}, f32[768]{0:T(1024)}, u32[]{:S(2)}) copy-start(f32[768]{0:T(1024)} %param.20) | copy-start | bytes 9220
  323.9 258.0 %copy-start.10 = (f32[1024]{0:T(1024)S(1)}, f32[1024]{0:T(1024)}, u32[]{:S(2)}) copy-start(f32[1024]{0:T(1024)} %param.29) | copy-start | bytes 12292
  576.6 33.7 %collective-permute-start.5 = (f32[768]{0:T(1024)S(1)}, f32[768]{0:T(1024)S(1)}, u32[]{:S(2)}, u32[]{:S(2)}) collective-permute-start(f32[768]{0:T(1024)S(1)} %get-tuple-element.120), channel_id=1, source_target_pairs={{0,1},{1,0},{2,3},{3,2},{4,5},{5,4},{6,7},{7,6},{8,9},{9,8},{10,11... | collective-permute-start | bytes 9224 | tf_op jit(solution)/shard_map/ppermute | solution.py:24
  583.2 5.6 copy-start.5
  588.8 3.5 copy-start.8
  592.3 2.1 copy-start.7
  594.3 2.1 copy-start.6
  596.4 3.1 copy-start.4
  599.5 3.9 copy-start
  599.5 3.9 copy-start.1
  599.5 3.9 copy-start.2
  599.5 4.4 copy-start.3

commit v5 on v4

--- a/solution.py
+++ b/solution.py
@@ -11,6 +11,10 @@
 D = 1536
 KCONV = 4
 LEN = 1024
+BLOCK = 256
+SEND_STEPS = (0, 8, 17)
+GN_STEPS = (0, 6, 11)
+BESIDE = 3
 EPS = 1e-06
 GATE_SCALE = 8.0
 TANH_COEF = math.sqrt(2.0 / math.pi)
@@ -372,10 +376,25 @@
     )(tokens, cotangent, wr, wg, ow, gain, rw, iw, cw, cb, rb, ib, sp)
 
 
+def norm_back_rows(rows, grad, held, cot, gain, gain_o, g1_o):
+    wide = held.shape[1]
+    scale = lax.rsqrt(jnp.sum(held * held, axis=1, keepdims=True) / wide + EPS)
+    product = grad * held
+    by_gain = product * scale
+    gain_o[...] += by_gain[0:8] + by_gain[8:16]
+    inner = jnp.sum(product * gain[...], axis=1, keepdims=True)
+    grad_one = (
+        cot.astype(F32)
+        + scale * (grad * gain[...])
+        - held * (scale * scale * scale * inner / wide)
+    )
+    g1_o[rows, :] = grad_one.astype(BF16)
+
+
 def ffn_kernel(
     count, blocks,
-    x, mix, live, gain, keep, wg0, wg1, wu0, wu1, wd0, wd1, mixed, cotangent, far_first, cot_first,
-    out_o, gu_sum, gg0, gg1, gd0, gd1, g1_o, g1t_o, gain_o,
+    x, mix, lengths, gain, keep, wg0, wg1, wu0, wu1, wd0, wd1, mixed, cotangent, far_first, cot_first,
+    out_o, gu_sum, gg_sum, gg0, gg1, gd0, gd1, g1_o, g1t_o, gain_o, gn_last, far_last, cot_last,
     far_s, ct_s, ctok_s, n2_s, n2t_s, hid_s, ga_s, gb_s, out_acc, gn_acc, gn_s, gn_far,
     keep_s, give_s, got_s,
     far_send, far_recv, ct_send, ct_recv, gn_send, gn_recv, up_send, up_recv, free_sem,
@@ -439,9 +458,13 @@
         for s in range(2):
             cot_load(s).start()
         group_barrier(core, chip)
-        for c in range(1, count):
-            send_part(c)
         gain_o[...] = jnp.zeros_like(gain_o)
+
+    for c, at in enumerate(SEND_STEPS):
+
+        @pl.when(step == at)
+        def _():
+            send_part(c + 1)
 
     def turned_cot(c):
         cols = pl.ds(pl.multiple_of(c * chunk, chunk), chunk)
@@ -450,12 +473,14 @@
 
     def norm_forward(c):
         cols = pl.ds(pl.multiple_of(c * chunk, chunk), chunk)
+        slots = c * chunk + lax.broadcasted_iota(jnp.int32, (1, chunk), 1)
+        live = (slots < lengths[core]).astype(F32).astype(BF16)
         pltpu.make_async_copy(far_first, far_s.at[c], far_recv.at[c]).wait()
         for s in range(2):
             pltpu.make_async_copy(
                 cot_first.at[s], ct_s.at[s, :, cols], ct_recv.at[c, s]
             ).wait()
-            ct_s[s, :, cols] = ct_s[s, :, cols] * live[:, cols]
+            ct_s[s, :, cols] = ct_s[s, :, cols] * live
         turned_cot(c)
         gn_acc[...] = jnp.zeros_like(gn_acc)
 
@@ -501,6 +526,17 @@
         def _():
             out_o[...] = out_acc[...].astype(BF16)
             gn_s[c] = gn_acc[...].astype(BF16)
+
+        @pl.when(step == first_part - 1)
+        def _():
+            gn_last[...] = gn_s[count - 1]
+            far_last[...] = far_s[count - 1]
+            cot_last[...] = ctok_s[...]
+
+    for c, at in enumerate(GN_STEPS):
+
+        @pl.when(step == first_part - blocks + at)
+        def _():
             gn_move(c).start()
 
     def norm_back(c):
@@ -511,65 +547,64 @@
             rows = pl.ds(pl.multiple_of(i * 16, 16), 16)
             grad = gn_s[c, rows, :].astype(F32) + gn_far[c, rows, :].astype(F32)
             held = x[rows, :].astype(F32) + (mix[rows, :].astype(F32) + far_s[c, rows, :].astype(F32))
-            scale = lax.rsqrt(jnp.sum(held * held, axis=1, keepdims=True) / wide + EPS)
-            product = grad * held
-            by_gain = product * scale
-            gain_o[...] += by_gain[0:8] + by_gain[8:16]
-            inner = jnp.sum(product * gain[...], axis=1, keepdims=True)
-            grad_one = (
-                ctok_s[rows, :].astype(F32)
-                + scale * (grad * gain[...])
-                - held * (scale * scale * scale * inner / wide)
-            )
-            g1_o[rows, :] = grad_one.astype(BF16)
+            norm_back_rows(rows, grad, held, ctok_s[rows, :], gain, gain_o, g1_o)
             return 0
 
         lax.fori_loop(0, chunk // 16, rows_step, 0)
         g1t_o[...] = g1_o[...].T
 
-    def give(k):
+    def give(a, k):
         at = k % 2
         return pltpu.make_async_remote_copy(
-            give_s.at[at], got_s.at[at], up_send.at[at], up_recv.at[at], device_id={"rows": 1 - core}
+            give_s.at[a, at], got_s.at[a, at], up_send.at[a, at], up_recv.at[a, at],
+            device_id={"rows": 1 - core},
         )
 
     k = step - first_part
-
-    @pl.when(jnp.logical_and(k > 0, k <= blocks))
+    shared = ((gb_s, gu_sum, blocks), (ga_s, gg_sum, BESIDE))
+    for a, (_, total_o, many) in enumerate(shared):
+
+        @pl.when(jnp.logical_and(k > 0, k <= many))
+        def _():
+            give(a, k - 1).wait()
+            at = (k - 1) % 2
+            total_o[...] = (keep_s[a, at].astype(F32) + got_s[a, at].astype(F32)).astype(BF16)
+
+            @pl.when(k - 1 < many - 2)
+            def _():
+                pl.semaphore_signal(free_sem.at[a], inc=1, device_id={"rows": 1 - core})
+
+        @pl.when(jnp.logical_and(k >= 0, k < many))
+        def _():
+            grad = shared[a][0][k]
+            give_s[a, k % 2] = dot(n2t_s[half:], grad).astype(BF16)
+
+            @pl.when(k >= 2)
+            def _():
+                pl.semaphore_wait(free_sem.at[a], 1)
+
+            give(a, k).start()
+            keep_s[a, k % 2] = dot(n2t_s[:half], grad).astype(BF16)
+
+    @pl.when(jnp.logical_and(k >= BESIDE, k < blocks))
     def _():
-        give(k - 1).wait()
-        total = keep_s[(k - 1) % 2].astype(F32) + got_s[(k - 1) % 2].astype(F32)
-        gu_sum[...] = total.astype(BF16)
-
-        @pl.when(k - 1 < blocks - 2)
-        def _():
-            pl.semaphore_signal(free_sem, inc=1, device_id={"rows": 1 - core})
+        gg0[...] = dot(n2t_s[:half], ga_s[k]).astype(BF16)
+        gg1[...] = dot(n2t_s[half:], ga_s[k]).astype(BF16)
 
     @pl.when(jnp.logical_and(k >= 0, k < blocks))
     def _():
-        up, down, gate = gb_s[k], hid_s[k], ga_s[k]
-        give_s[k % 2] = dot(n2t_s[half:], up).astype(BF16)
-
-        @pl.when(k >= 2)
-        def _():
-            pl.semaphore_wait(free_sem, 1)
-
-        give(k).start()
-        keep_s[k % 2] = dot(n2t_s[:half], up).astype(BF16)
-        gg0[...] = dot(n2t_s[:half], gate).astype(BF16)
-        gg1[...] = dot(n2t_s[half:], gate).astype(BF16)
-        gd0[...] = dot(ct_s[0], down).astype(BF16)
-        gd1[...] = dot(ct_s[1], down).astype(BF16)
-
-    for c in range(count):
-
-        @pl.when(k == (2 * c + 1 if c < count - 1 else blocks))
+        gd0[...] = dot(ct_s[0], hid_s[k]).astype(BF16)
+        gd1[...] = dot(ct_s[1], hid_s[k]).astype(BF16)
+
+    for c in range(count - 1):
+
+        @pl.when(k == 3 * (c + 1))
         def _():
             norm_back(c)
 
     @pl.when(k == blocks)
     def _():
-        for c in range(count):
+        for c in range(count - 1):
             gn_move(c).wait_send()
         for c in range(1, count):
             far_move(c).wait_send()
@@ -581,7 +616,7 @@
                 moves[1].wait_send()
 
 
-def ffn(x, mix, live, gain, keep, wg, wu, wd, cotangent, far_first, cot_first, chunk=256, block=256):
+def ffn(x, mix, lengths, gain, keep, wg, wu, wd, cotangent, far_first, cot_first, chunk=256, block=BLOCK):
     tokens, wide = x.shape
     half, width = wg[0].shape
     count, blocks = tokens // chunk, width // block
@@ -592,7 +627,7 @@
     hbm = pl.BlockSpec(memory_space=pl.ANY)
 
     def back_chunk(i):
-        return jnp.clip((i - first_part) // 2, 0, count - 1)
+        return jnp.clip((i - first_part - 1) // 3, 0, count - 2)
 
     def chunk_at(i):
         return jnp.where(i < first_part, i // blocks, back_chunk(i))
@@ -601,34 +636,44 @@
     weight = pl.BlockSpec(
         (half, block), lambda i: (0, jnp.where(i < first_part, i % blocks, blocks - 1))
     )
-    grad_at = lambda late: pl.BlockSpec(
-        (half, block), lambda i: (0, jnp.clip(i - first_part - late, 0, blocks - 1))
+    grad_at = lambda late, many: pl.BlockSpec(
+        (half, block), lambda i: (0, jnp.clip(i - first_part - late, 0, many - 1))
     )
-    grad = jax.ShapeDtypeStruct((half, width), BF16)
+    grad = lambda many: jax.ShapeDtypeStruct((half, many * block), BF16)
     low = jax.ShapeDtypeStruct((tokens, wide), BF16)
     part = pltpu.VMEM((count, chunk, wide), BF16)
     middle = pltpu.VMEM((blocks, tokens, block), BF16)
-    pair = pltpu.VMEM((2, half, block), BF16)
+    pair = pltpu.VMEM((2, 2, half, block), BF16)
     dma = pltpu.SemaphoreType.DMA
     return pl.pallas_call(
         functools.partial(ffn_kernel, count, blocks),
         grid=(first_part + blocks + 1,),
-        in_specs=[rows, rows, whole((1, tokens)), whole((1, wide)), whole((1, 1))]
+        in_specs=[rows, rows, pl.BlockSpec(memory_space=pltpu.SMEM), whole((1, wide)), whole((1, 1))]
         + [weight] * 6
         + [hbm] * 4,
         out_specs=[
             pl.BlockSpec((chunk, wide), lambda i: (jnp.minimum(i // blocks, count - 1), 0)),
-            grad_at(1),
+            grad_at(1, blocks),
+            grad_at(1, BESIDE),
         ]
-        + [grad_at(0)] * 4
+        + [grad_at(BESIDE, blocks - BESIDE)] * 2
+        + [grad_at(0, blocks)] * 2
         + [
             pl.BlockSpec((chunk, wide), lambda i: (back_chunk(i), 0)),
             pl.BlockSpec((wide, chunk), lambda i: (0, back_chunk(i))),
             whole((8, wide)),
-        ],
+        ]
+        + [whole((chunk, wide))] * 3,
         out_shape=[low]
-        + [grad] * 5
-        + [low, jax.ShapeDtypeStruct((wide, tokens), BF16), jax.ShapeDtypeStruct((8, wide), F32)],
+        + [grad(blocks), grad(BESIDE)]
+        + [grad(blocks - BESIDE)] * 2
+        + [grad(blocks)] * 2
+        + [
+            jax.ShapeDtypeStruct((tokens - chunk, wide), BF16),
+            jax.ShapeDtypeStruct((wide, tokens - chunk), BF16),
+            jax.ShapeDtypeStruct((8, wide), F32),
+        ]
+        + [jax.ShapeDtypeStruct((chunk, wide), BF16)] * 3,
         scratch_shapes=[
             part,
             pltpu.VMEM((2, half, tokens), BF16),
@@ -643,15 +688,15 @@
             dma((count,)), dma((count,)),
             dma((count, 2)), dma((count, 2)),
             dma((count,)), dma((count,)),
-            dma((2,)), dma((2,)),
-            pltpu.SemaphoreType.REGULAR,
+            dma((2, 2)), dma((2, 2)),
+            pltpu.SemaphoreType.REGULAR((2,)),
         ],
         compiler_params=pltpu.CompilerParams(
             vmem_limit_bytes=62 * MIB, collective_id=3, has_side_effects=True
         ),
         name="ffn",
     )(
-        x, mix, live, gain, keep, wg[0], wg[1], wu[0], wu[1], wd[0], wd[1],
+        x, mix, lengths, gain, keep, wg[0], wg[1], wu[0], wu[1], wd[0], wd[1],
         mix, cotangent, far_first, cot_first,
     )
 
@@ -670,21 +715,30 @@
     return pl.ds(pl.multiple_of(chunk * size, size), size)
 
 
-def ring_beside(n, own, out, own_b, ring_b, own_sem, rs_send, rs_recv, ag_send, ag_recv, put_sem):
+def ring_beside(n, owns, out, own_b, ring_b, own_sem, rs_send, rs_recv, ag_send, ag_recv, put_sem):
     me, nexts = ring_place(n, lax.axis_index("dp"))
-    wide = own.shape[1] // 2
+    wide = out.shape[1] // 2
     cut = (wide // 128 + 1) // 2 * 128
     groups = (pl.ds(0, cut), pl.ds(cut, wide - cut))
     both = [(g, way) for g in range(2) for way in range(2)]
     per = -(-n // 8)
     per_gather = -(-(n - 2) // 6)
-    rows_of = lambda way, s: ring_rows(n, me, own.shape[0], way, s)
+    rows_of = lambda way, s: ring_rows(n, me, out.shape[0], way, s)
     cols_of = lambda g, way: pl.ds(way * wide + g * cut, wide - cut if g else cut)
 
-    def own_copy(way, s):
-        return pltpu.make_async_copy(
-            own.at[rows_of(way, s), pl.ds(way * wide, wide)], own_b.at[way, s], own_sem.at[way, s]
-        )
+    def own_copies(way, s):
+        moves, at = [], 0
+        for m, own in enumerate(owns):
+            size = own.shape[1] // 2
+            moves.append(
+                pltpu.make_async_copy(
+                    own.at[rows_of(way, s), pl.ds(way * size, size)],
+                    own_b.at[way, s % 2, :, pl.ds(at, size)],
+                    own_sem.at[m, way, s % 2],
+                )
+            )
+            at += size
+        return moves
 
     def sum_copy(g, way, s):
         return pltpu.make_async_remote_copy(
@@ -711,69 +765,85 @@
             put_sem.at[g, way],
         )
 
-    def begin():
+    def begin(chip):
         barrier = pltpu.get_barrier_semaphore()
         for neighbour in nexts:
             pl.semaphore_signal(barrier, inc=1, device_id={"dp": neighbour})
-
-        def load(s, _):
+        pl.semaphore_signal(barrier, inc=1, device_id={"cols": 1 - chip})
+        for s in range(2):
             for way in range(2):
-                own_copy(way, s).start()
-            return 0
-
-        lax.fori_loop(0, n, load, 0)
-        pl.semaphore_wait(barrier, 2)
+                for move in own_copies(way, s):
+                    move.start()
+        pl.semaphore_wait(barrier, 3)
+
+    def sum_step(g, s):
+        for way in range(2):
+            if g == 0:
+                for move in own_copies(way, s):
+                    move.wait()
+
+            @pl.when(s == 0)
+            def _():
+                ring_b[way, s, :, groups[g]] = own_b[way, s % 2, :, groups[g]]
+
+            @pl.when(s > 0)
+            def _():
+                sum_copy(g, way, s - 1).wait_recv()
+                total = ring_b[way, s, :, groups[g]].astype(F32) + own_b[
+                    way, s % 2, :, groups[g]
+                ].astype(F32)
+                ring_b[way, s, :, groups[g]] = total.astype(BF16)
+
+            @pl.when(s < n - 1)
+            def _():
+                sum_copy(g, way, s).start()
+
+            @pl.when(s == n - 1)
+            def _():
+                first_gather(g, way).start()
+                put_copy(g, way).start()
+
+            if g == 1:
+
+                @pl.when(s < n - 2)
+                def _():
+                    for move in own_copies(way, s + 2):
+                        move.start()
+
+    def gather_step(g, s):
+        for way in range(2):
+
+            @pl.when(s == 1)
+            def _():
+                first_gather(g, way).wait_recv()
+
+            @pl.when(s > 1)
+            def _():
+                gather_copy(g, way, s - 1).wait_recv()
+
+            gather_copy(g, way, s).start()
 
     def tick(g, t):
-        def sum_step(s, _):
-            for way in range(2):
-                if g == 0:
-                    own_copy(way, s).wait()
-
-                @pl.when(s == 0)
-                def _():
-                    ring_b[way, s, :, groups[g]] = own_b[way, s, :, groups[g]]
-
-                @pl.when(s > 0)
-                def _():
-                    sum_copy(g, way, s - 1).wait_recv()
-                    total = ring_b[way, s, :, groups[g]].astype(F32) + own_b[
-                        way, s, :, groups[g]
-                    ].astype(F32)
-                    ring_b[way, s, :, groups[g]] = total.astype(BF16)
-
-                @pl.when(s < n - 1)
-                def _():
-                    sum_copy(g, way, s).start()
-
-                @pl.when(s == n - 1)
-                def _():
-                    first_gather(g, way).start()
-                    put_copy(g, way).start()
-            return 0
-
-        def gather_step(s, _):
-            for way in range(2):
-
-                @pl.when(s == 1)
-                def _():
-                    first_gather(g, way).wait_recv()
-
-                @pl.when(s > 1)
-                def _():
-                    gather_copy(g, way, s - 1).wait_recv()
-
-                gather_copy(g, way, s).start()
-            return 0
+        if per > 1 and g == 0:
+            return
+        turns = (0, 1) if per > 1 else (g,)
+
+        def run(step):
+            def once(s, _):
+                for turn in turns:
+                    step(turn, s)
+                return 0
+
+            return once
 
         @pl.when(t < 8)
         def _():
-            lax.fori_loop(t * per, jnp.minimum((t + 1) * per, n), sum_step, 0)
+            lax.fori_loop(t * per, jnp.minimum((t + 1) * per, n), run(sum_step), 0)
 
         @pl.when(t >= 8)
         def _():
             start = 1 + (t - 8) * per_gather
-            lax.fori_loop(start, jnp.minimum(start + per_gather, n - 1), gather_step, 0)
+            lax.fori_loop(start, jnp.minimum(start + per_gather, n - 1), run(gather_step), 0)
 
     def end():
         for g, way in both:
@@ -798,10 +868,11 @@
 
 def rec_backward_kernel(
     tile, n,
-    g1, g1t, n1t, st, gate, r_in, i_in, cl, rec, br, ow0, ow1, wr0, wr1, wg0, wg1, rw, iw, cw, sp,
-    x, gain, gain_two, up,
-    gn1_o, go0, go1, gr0, gr1, gg0, gg1, ggw, sums, stat, gains0, gains1, up_o,
-    acc, gb_s, gc_s, ggp_s, grp_s, gip_s, grec_s, gain_s, *ring_refs
+    n1t, st, gate, r_in, i_in, cl, rec, br, ow0, ow1, wr0, wr1, wg0, wg1, rw, iw, cw, sp,
+    x, gain, gain_second, gain_two, up, gate_own, g1_head, g1t_head, mixed, gn_last, far_last, cot_last,
+    gn1_o, go0, go1, gr0, gr1, gg0, gg1, ggw, small0, small1, stat, up_o, g1_last,
+    acc, gb_s, gc_s, ggp_s, grp_s, gip_s, grec_s, gain_s, sums, g1, g1t, gain_b,
+    gn_s, gn_far, mix_s, far_s, cot_s, load_sem, gn_send, gn_recv, put_last, *ring_refs
 ):
     step = pl.program_id(0)
     tokens, block = gb_s.shape
@@ -811,14 +882,61 @@
     tiles = tokens // tile
     subs = tile // 8
 
-    begin, tick, end = ring_beside(n, up, up_o, *ring_refs)
+    begin, tick, end = ring_beside(n, (up, gate_own), up_o, *ring_refs)
+
+    chunk = gn_s.shape[0]
+    head = tokens - chunk
+    chip = lax.axis_index("cols")
+    gn_move = pltpu.make_async_remote_copy(
+        gn_last, gn_far, gn_send.at[0], gn_recv.at[0], device_id={"cols": 1 - chip}
+    )
+    last_put = pltpu.make_async_copy(g1.at[pl.ds(head, chunk), :], g1_last, put_last.at[0])
+    beat = lambda at: tick(at % 2, 3 + step * 3 + at // 2)
 
     @pl.when(step == 0)
     def _():
-        begin()
+        loads = [
+            pltpu.make_async_copy(src, dst, load_sem.at[m])
+            for m, (src, dst) in enumerate(
+                (
+                    (mixed.at[pl.ds(head, chunk), :], mix_s),
+                    (far_last, far_s),
+                    (cot_last, cot_s),
+                    (gn_last, gn_s),
+                    (g1_head, g1.at[pl.ds(0, head), :]),
+                    (g1t_head, g1t.at[:, pl.ds(0, head)]),
+                )
+            )
+        ]
+        for move in loads:
+            move.start()
+        begin(chip)
+        gn_move.start()
         acc[...] = jnp.zeros_like(acc)
-
-    beat = lambda at: tick(at % 2, step * 3 + at // 2)
+        small0[...] = jnp.zeros_like(small0)
+        small1[...] = jnp.zeros_like(small1)
+        gain_b[...] = gain_two[...]
+        for t in range(3):
+            for g in range(2):
+                tick(g, t)
+        for move in loads:
+            move.wait()
+        gn_move.wait()
+
+        def rows_step(i, _):
+            base = pl.multiple_of(i * 16, 16)
+            rows = pl.ds(base, 16)
+            grad = gn_s[rows, :].astype(F32) + gn_far[rows, :].astype(F32)
+            held = x[pl.ds(head + base, 16), :].astype(F32) + (
+                mix_s[rows, :].astype(F32) + far_s[rows, :].astype(F32)
+            )
+            norm_back_rows(pl.ds(head + base, 16), grad, held, cot_s[rows, :], gain_second, gain_b, g1)
+            return 0
+
+        lax.fori_loop(0, chunk // 16, rows_step, 0)
+        g1t[:, head:] = g1[head:, :].T
+        last_put.start()
+
     beat(0)
     gb_s[...] = dot(g1[:, :half], ow0[...]) + dot(g1[:, half:], ow1[...])
     beat(1)
@@ -925,6 +1043,16 @@
 
     lax.fori_loop(0, tiles, conv_step, tuple(jnp.zeros((8, 128), F32) for _ in range(heads)))
     beat(5)
+    all_heads = small0.shape[0] // 8
+    head_row = lax.broadcasted_iota(jnp.int32, (all_heads, 128), 0)
+    for n in range(8):
+        vector = jnp.sum(sums[n * 8 : n * 8 + 8, :], axis=0, keepdims=True)
+        for h in range(heads):
+            at = slice(n * all_heads, (n + 1) * all_heads)
+            mine = vector[:, h * 128 : (h + 1) * 128]
+            tile_now = jnp.where(head_row == step * heads + h, mine, small0[at, 0:128])
+            small0[at, 0:128] = tile_now
+            small1[at, 0:128] = tile_now
     grad_rec = grec_s[...]
     grad_gate = ggp_s[...]
     gr0[...] = dot(n1t[:half], grad_rec).astype(BF16)
@@ -937,46 +1065,45 @@
     @pl.when(step == pl.num_programs(0) - 1)
     def _():
         gain_s[...] = jnp.zeros_like(gain_s)
-        for g in range(2):
-            tick(g, 12)
 
         def stat_step(i, _):
-            @pl.when(i == tokens // 32)
-            def _():
-                for g in range(2):
-                    tick(g, 13)
-
-            rows = pl.ds(pl.multiple_of(i * 16, 16), 16)
+            rows = pl.ds(pl.multiple_of(i * 32, 32), 32)
             part = acc[rows, :]
             gn1_o[rows, :] = part.astype(BF16)
             held = x[rows, :].astype(F32)
             scale = lax.rsqrt(jnp.sum(held * held, axis=1, keepdims=True) / wide + EPS)
             product = part * held
             by_gain = product * scale
-            gain_s[...] += by_gain[0:8] + by_gain[8:16]
+            gain_s[...] += (by_gain[0:8] + by_gain[8:16]) + (by_gain[16:24] + by_gain[24:32])
             inner = jnp.sum(product * gain[...], axis=1, keepdims=True)
-            stat[rows, 0:64] = jnp.broadcast_to(inner, (16, 64))
-            stat[rows, 64:128] = jnp.broadcast_to(scale, (16, 64))
+            stat[rows, 0:64] = jnp.broadcast_to(inner, (32, 64))
+            stat[rows, 64:128] = jnp.broadcast_to(scale, (32, 64))
             return 0
 
-        lax.fori_loop(0, tokens // 16, stat_step, 0)
-        both = gain_two[...]
-        for out, sl in ((gains0, slice(0, half)), (gains1, slice(half, wide))):
-            out[...] = jnp.zeros_like(out)
-            out[0:8, :] = gain_s[:, sl]
-            out[8:16, :] = both[:, sl]
+        lax.fori_loop(0, tokens // 32, stat_step, 0)
+        for n, held in enumerate((gain_s, gain_b)):
+            vector = jnp.sum(held[...], axis=0, keepdims=True)
+            for m in range(half // 128):
+                at = n * 8 + m
+                small0[at : at + 1, 128:] = vector[:, m * 128 : (m + 1) * 128]
+                small1[at : at + 1, 128:] = vector[:, half + m * 128 : half + (m + 1) * 128]
+        last_put.wait()
         end()
 
 
 def rec_backward(
-    g1, g1t, n1t, st, gate, r, g, cl, rec, br, ow, wr, wg, rw, iw, cw, sp, x, gain, gain_two, up, n, block=256, tile=64
+    n1t, st, gate, r, g, cl, rec, br, ow, wr, wg, rw, iw, cw, sp, x, gain, gain_second, gain_two,
+    up, gate_own, lasts, n, block=256, tile=64
 ):
     wide, tokens = n1t.shape
     half, width = wr[0].shape
     heads = block // 128
     rows = up.shape[0]
-    up = jnp.pad(up, ((0, -rows % (16 * n)), (0, 0)))
-    slots = pltpu.VMEM((2, n, up.shape[0] // n, up.shape[1] // 2), BF16)
+    up, gate_own = (jnp.pad(a, ((0, -rows % (16 * n)), (0, 0))) for a in (up, gate_own))
+    side = (up.shape[0], up.shape[1] + gate_own.shape[1])
+    small = (8 * (width // 128), 256)
+    chunk = lasts[-1].shape[0]
+    slots = lambda many: pltpu.VMEM((2, many, side[0] // n, side[1] // 2), BF16)
     dma = pltpu.SemaphoreType.DMA
     hbm = pl.BlockSpec(memory_space=pl.ANY)
     whole = lambda shape: pl.BlockSpec(shape, lambda i: (0, 0), pipeline_mode=pl.Buffered(1))
@@ -988,24 +1115,25 @@
     outs = pl.pallas_call(
         functools.partial(rec_backward_kernel, tile, n),
         grid=(width // block,),
-        in_specs=[whole((tokens, wide))] + [whole((wide, tokens))] * 2
+        in_specs=[whole((wide, tokens))]
         + [act] * 7
         + [weight] * 6
         + [pl.BlockSpec((heads, 128, 128), lambda i: (i, 0, 0))] * 2
         + [thin(KCONV), thin(1)]
-        + [whole((tokens, wide)), whole((1, wide)), whole((8, wide)), hbm],
+        + [whole((tokens, wide)), whole((1, wide)), whole((1, wide)), whole((8, wide))]
+        + [hbm] * 8,
         out_specs=[whole((tokens, wide))]
         + [weight] * 6
-        + [gate_block, thin(64), whole((tokens, 128)), whole((64, half)), whole((64, half)), hbm],
+        + [gate_block, whole(small), whole(small), whole((tokens, 128)), hbm, hbm],
         out_shape=[jax.ShapeDtypeStruct((tokens, wide), BF16)]
         + [grad] * 6
         + [
             jax.ShapeDtypeStruct((width // 128, 128, 256), BF16),
-            jax.ShapeDtypeStruct((64, width), F32),
+            jax.ShapeDtypeStruct(small, F32),
+            jax.ShapeDtypeStruct(small, F32),
             jax.ShapeDtypeStruct((tokens, 128), F32),
-            jax.ShapeDtypeStruct((64, half), F32),
-            jax.ShapeDtypeStruct((64, half), F32),
-            jax.ShapeDtypeStruct(up.shape, BF16),
+            jax.ShapeDtypeStruct(side, BF16),
+            jax.ShapeDtypeStruct((chunk, wide), BF16),
         ],
         scratch_shapes=[
             pltpu.VMEM((tokens, wide), F32),
@@ -1016,23 +1144,32 @@
             pltpu.VMEM((tokens, block), BF16),
             pltpu.VMEM((tokens, block), BF16),
             pltpu.VMEM((8, wide), F32),
-            slots, slots,
-            dma((2, n)), dma((2, 2)), dma((2, 2, n)), dma((2, 2, n)), dma((2, 2, n)), dma((2, 2)),
+            pltpu.VMEM((64, block), F32),
+            pltpu.VMEM((tokens, wide), BF16),
+            pltpu.VMEM((wide, tokens), BF16),
+            pltpu.VMEM((8, wide), F32),
+        ]
+        + [pltpu.VMEM((chunk, wide), BF16)] * 5
+        + [
+            dma((6,)), dma((1,)), dma((1,)), dma((1,)),
+            slots(2), slots(n),
+            dma((2, 2, 2)), dma((2, 2)), dma((2, 2, n)), dma((2, 2, n)), dma((2, 2, n)), dma((2, 2)),
         ],
         compiler_params=pltpu.CompilerParams(
             vmem_limit_bytes=62 * MIB, collective_id=6, has_side_effects=True
         ),
         name="recurrent_backward",
     )(
-        g1, g1t, n1t, st, gate, r, g, cl, rec, br,
-        ow[0], ow[1], wr[0], wr[1], wg[0], wg[1], rw, iw, cw, sp, x, gain, gain_two, up,
+        n1t, st, gate, r, g, cl, rec, br,
+        ow[0], ow[1], wr[0], wr[1], wg[0], wg[1], rw, iw, cw, sp, x, gain, gain_second, gain_two,
+        up, gate_own, *lasts,
     )
-    return (*outs[:-1], outs[-1][:rows])
+    return (*outs[:-2], outs[-2][:rows], outs[-1])
 
 
 def ring_kernel(n, count, *refs):
     own, other, refs = refs[:count], refs[count : 2 * count], refs[2 * count :]
-    (gn1, out, stat, g1), refs = refs[:4], refs[4:]
+    (gn1, out, stat, g1_head, g1_last), refs = refs[:5], refs[5:]
     outs, refs = refs[:count], refs[count:]
     (gn1_p, out_p, stat_p, g1_p), scratch = refs[:4], refs[4:]
     piece_send, piece_recv = scratch[-2:]
@@ -1059,7 +1196,8 @@
         (out, out_p, slice(None), first, second),
         (stat, stat_p, slice(None), everything, everything),
     ]
-    singles = [(g1, slice(None))]
+    head = g1_head.shape[0]
+    singles = [(g1_head, slice(0, head)), (g1_last, slice(head, gn1.shape[0]))]
     diag = core == chip
 
     def piece_moves(m):
@@ -1287,7 +1425,7 @@
         ],
         scratch_shapes=slots * 3
         + [sems, pair, sems, pair] + [sems] * 3 + [pair]
-        + [pltpu.SemaphoreType.DMA((4, 2))] * 2,
+        + [pltpu.SemaphoreType.DMA((5, 2))] * 2,
         compiler_params=pltpu.CompilerParams(
             collective_id=0, has_side_effects=True, vmem_limit_bytes=60 * MIB
         ),
@@ -1296,10 +1434,16 @@
     return [a[:r] for a, r in zip(outs, rows)], outs[count:]
 
 
-def final_kernel(gn, out, stat, g1, tokens, gain, live, result_o, grad_o):
+def final_kernel(
+    gn, out, stat, g1, tokens, gain, lengths, beside, down, gate, out_w, rec_w, gate_w,
+    result_o, grad_o, up_o, gate_o, down_o, out_w_o, rec_w_o, gate_w_o,
+):
     wide = 2 * tokens.shape[0]
     low = lambda ref: ref[0].astype(F32) + ref[1].astype(F32)
-    result_o[...] = (low(out).T * live[...]).astype(BF16)
+    chunk = tokens.shape[1]
+    slots = pl.program_id(0) * chunk + lax.broadcasted_iota(jnp.int32, (1, chunk), 1)
+    live = (slots < lengths[lax.axis_index("cols")]).astype(F32)
+    result_o[...] = (low(out).T * live).astype(BF16)
     grad = low(gn).T
     held = tokens[...].astype(F32)
     inner = (stat[0] + stat[1]).T[0:1, :]
@@ -1309,28 +1453,43 @@
         + (scale * gain[...]) * grad
         - held * (scale * scale * scale * inner / wide)
     ).astype(BF16)
-
-
-def final(gn, out, stat, g1, tokens, gain, live, chunk=256):
+    side = beside.shape[1] // 2
+    up_half = up_o.shape[1] // 2
+    gate_half = side - up_half
+    for way in range(2):
+        at = way * side
+        up_o[:, way * up_half : (way + 1) * up_half] = beside[:, at : at + up_half].astype(F32)
+        gate_o[:, way * gate_half : (way + 1) * gate_half] = beside[:, at + up_half : at + side].astype(F32)
+    gate_o[:, 2 * gate_half :] = gate[...].astype(F32)
+    for src, dst in ((down, down_o), (out_w, out_w_o), (rec_w, rec_w_o), (gate_w, gate_w_o)):
+        dst[...] = src[...].astype(F32)
+
+
+def final(gn, out, stat, g1, tokens, gain, lengths, beside, down, gate, out_w, rec_w, gate_w, steps=8):
     half, length = tokens.shape
+    chunk, size = length // steps, half // steps
     pair = lambda cols: pl.BlockSpec((2, chunk, cols), lambda i: (0, i, 0))
     across = pl.BlockSpec((half, chunk), lambda i: (0, i))
+    rows = lambda cols: pl.BlockSpec((size, cols), lambda i: (i, 0))
     shape = jax.ShapeDtypeStruct((half, length), BF16)
+    ffn_wide, wide = down.shape[1], out_w.shape[1]
+    grads = [ffn_wide] * 3 + [wide] * 3
     return pl.pallas_call(
         final_kernel,
-        grid=(length // chunk,),
+        grid=(steps,),
         in_specs=[
             pair(half), pair(half), pair(128),
             pl.BlockSpec((chunk, half), lambda i: (i, 0)),
             across,
             pl.BlockSpec((half, 1), lambda i: (0, 0)),
-            pl.BlockSpec((1, chunk), lambda i: (0, i)),
-        ],
-        out_specs=[across, across],
-        out_shape=[shape, shape],
-        compiler_params=pltpu.CompilerParams(vmem_limit_bytes=48 * MIB),
+            pl.BlockSpec(memory_space=pltpu.SMEM),
+        ]
+        + [rows(a.shape[1]) for a in (beside, down, gate, out_w, rec_w, gate_w)],
+        out_specs=[across, across] + [rows(cols) for cols in grads],
+        out_shape=[shape, shape] + [jax.ShapeDtypeStruct((half, cols), F32) for cols in grads],
+        compiler_params=pltpu.CompilerParams(vmem_limit_bytes=56 * MIB),
         name="final",
-    )(gn, out, stat, g1, tokens, gain, live)
+    )(gn, out, stat, g1, tokens, gain, lengths, beside, down, gate, out_w, rec_w, gate_w)
 
 
 def body(
@@ -1345,10 +1504,6 @@
     wide = 2 * half
 
     both = lambda weight: (weight, swap(weight, "rows"))
-
-    positions = jnp.arange(LEN, dtype=jnp.int32)
-    live_core = (positions < lengths[at_row]).astype(BF16)[None, :]
-    live_chip = (positions < lengths[at_col]).astype(F32)
 
     sp = jax.nn.softplus(-decay_param)[None, :]
     (x, n1t, rec, gate, cl, r, g, st, br, mixed, cot_a, far_a, wr_far, wg_far, ow_far) = rec_forward(
@@ -1366,30 +1521,35 @@
     gain_one = jnp.concatenate(both(mix_gain))[None, :]
     keep = diag.astype(F32).reshape(1, 1)
 
-    out, up_sum, gg0, gg1, gd0, gd1, g1, g1t, grad_gain_two = ffn(
-        x, mixed, live_core, gain_two, keep, fg, fu, fd, cotangent, far_a, cot_a
+    out, up_own, gate_own, gg0, gg1, gd0, gd1, g1_head, g1t_head, grad_gain_two, *lasts = ffn(
+        x, mixed, lengths, gain_two, keep, fg, fu, fd, cotangent, far_a, cot_a
     )
-    gn1_part, go0, go1, gr0, gr1, gt0, gt1, ggw, sums, stat, gains0, gains1, sum_up = rec_backward(
-        g1, g1t, n1t, st, gate, r, g, cl, rec, br, ow, wr, wg, recur_weight,
-        input_weight, conv_weight, sp, x, gain_one, grad_gain_two, up_sum, dp,
+    gn1_part, go0, go1, gr0, gr1, gt0, gt1, ggw, small0, small1, stat, beside, g1_last = rec_backward(
+        n1t, st, gate, r, g, cl, rec, br, ow, wr, wg, recur_weight, input_weight, conv_weight, sp,
+        x, gain_one, gain_two, grad_gain_two, up_own, gate_own, [g1_head, g1t_head, mixed, *lasts], dp,
     )
     gates = ggw.reshape(-1, 256)
-    own = [gd0, gg0, go0, gr0, gt0, gates, sums, gains0]
-    other = [gd1, gg1, go1, gr1, gt1, gates, sums, gains1]
-    total, moved = ring_sum(dp, own, other, [gn1_part, out, stat, g1])
-    sum_down, sum_gate, sum_out, sum_rec, sum_gatew, gates, sums, gains = total
-    result, grad_tokens = final(*moved, tokens, mix_gain[:, None], live_chip[None, :])
+    total, moved = ring_sum(
+        dp,
+        [gd0, gg0, go0, gr0, gt0, gates, small0],
+        [gd1, gg1, go1, gr1, gt1, gates, small1],
+        [gn1_part, out, stat, g1_head, g1_last],
+    )
+    gates, small = total[5:]
+    result, grad_tokens, sum_up, sum_gate, sum_down, sum_out, sum_rec, sum_gatew = final(
+        *moved, tokens, mix_gain[:, None], lengths, beside, *total[:5]
+    )
     gates = gates.astype(F32).reshape(ggw.shape)
-    vec = jnp.sum(sums.reshape(8, 8, -1), axis=1)
-    gains = jnp.sum(gains[:16].reshape(2, 8, half), axis=1)
+    vec = small[:, :128].reshape(8, -1)
+    gains = small[:16, 128:].reshape(2, -1)[:, :half]
     grad_gain_one = gains[0] + swap(gains[0], "cols")
     grad_decay = vec[2] * -jax.nn.sigmoid(-decay_param)
     return (
         result,
         grad_tokens,
         grad_gain_one,
-        sum_rec.astype(F32),
-        sum_gatew.astype(F32),
+        sum_rec,
+        sum_gatew,
         vec[3:7],
         vec[7],
         gates[:, :, :128],
@@ -1397,11 +1557,11 @@
         gates[:, :, 128:],
         vec[1],
         grad_decay,
-        sum_out.astype(F32),
+        sum_out,
         gains[1],
-        sum_gate.astype(F32),
-        sum_up.astype(F32),
-        sum_down.astype(F32),
+        sum_gate,
+        sum_up,
+        sum_down,
     )
 
 

time: 611 us -> 595 us (0.974)
  other arithmetic: 25.4 us -> 3.2 us
  Pallas kernels: 572 us -> 579 us
    pallas_call x1, Pallas kernels: 251 us -> 224 us  [ring_sum(): pl.pallas_call(functools.partial(ring_kernel, n, count), in_specs=[hbm] *...]
    pallas_call x1, Pallas kernels: 92.3 us -> 114 us  [rec_backward(): pl.pallas_call(functools.partial(rec_backward_kernel, tile, n), grid=(wid...]
    convert_element_type x8 -> x0, other arithmetic: 21.1 us -> none  [the longest x1 5.63 us: body(): sum_gate.astype(F32)]
    pallas_call x1, Pallas kernels: 6.3 us -> 20.7 us  [final(): pl.pallas_call(final_kernel, grid=(steps,), in_specs=[pair(half), pair(ha...]
  transfers between devices with their start and end apart: 6 -> 6, of which waited for: 0 -> 0; matrix products, arithmetic and copies ran while one was open for 5% -> 1% of each run, Pallas kernels for 12% -> 15%
where the time goes in v5:
time: 595 us
  Pallas kernels  579 us (97%)
  local copies, waits for them, and re-layouts  8.86 us (1%)
    pallas_call x1, Pallas kernels, ring_sum(): pl.pallas_call(functools.partial(ring_kernel, n, count), in_specs=[hbm] *...  224 us
    pallas_call x1, Pallas kernels, ffn(): pl.pallas_call(functools.partial(ffn_kernel, count, blocks), grid=(first_...  154 us
    pallas_call x1, Pallas kernels, rec_backward(): pl.pallas_call(functools.partial(rec_backward_kernel, tile, n), grid=(wid...  114 us
    pallas_call x1, Pallas kernels, rec_forward(): pl.pallas_call(functools.partial(rec_forward_kernel, chunk, count, cot_pa...  67.3 us
    pallas_call x1, Pallas kernels, final(): pl.pallas_call(final_kernel, grid=(steps,), in_specs=[pair(half), pair(ha...  20.7 us
  transfers between devices with their start and end apart: 6, of which 0 were waited for; matrix products, arithmetic and copies ran while one was open for 1% of the time, Pallas kernels for 15%

profile of v5, /device:TPU:0, one launch (start us, length us, event | category | flops | bytes accessed | tf_op | source)
XLA Modules:
  0.0 594.7 jit_solution(17274827471980232796)
XLA Ops:
  0.7 0.5 collective-permute-start.1
  1.2 0.1 collective-permute-start.2
  1.3 0.4 collective-permute-start.3
  1.7 0.1 collective-permute-start
  1.8 0.4 collective-permute-start.4
  2.2 1.3 compare_select_fusion
  3.5 1.6 broadcast_in_dim.29.gain_h.gain
  5.1 67.3 %recurrent_forward.1 = (bf16[1024,1536]{1,0:T(8,128)(2,1)}, bf16[1536,1024]{1,0:T(8,128)(2,1)}, f32[1024,1024]{1,0:T(8,128)}, f32[1024,1024]{1,0:T(8,128)}, bf16...) custom-call(bf16[768,1024]{1,0:T(8,128)(2,1)} %tokens.3, ...), custom_call_target="tpu_custom_call" | custom-call | tf_op jit(solution)/shard_map/recurrent_forward/pallas_call | solution.py:329
  72.5 0.6 broadcast_in_dim.27.gain.gain_second
  73.1 0.6 broadcast_in_dim.28.gain
  73.7 154.0 %ffn.1 = (bf16[1024,1536]{1,0:T(8,128)(2,1)}, bf16[768,2304]{1,0:T(8,128)(2,1)}, bf16[768,768]{1,0:T(8,128)(2,1)}, bf16[768,1536]{1,0:T(8,128)(2,1)}, bf16[768,1...) custom-call(bf16[1024,1536]{1,0:T(8,128)(2,1)} %get-tuple-element.77, ...), custom_call_target="tpu_custom_call" | custom-call | tf_op jit(solution)/shard_map/ffn/pallas_call | solution.py:648
  227.7 113.5 %recurrent_backward.1 = (bf16[1024,1536]{1,0:T(8,128)(2,1)}, bf16[768,1024]{1,0:T(8,128)(2,1)}, bf16[768,1024]{1,0:T(8,128)(2,1)}, bf16[768,1024]{1,0:T(8,128)(2...) custom-call(bf16[1536,1024]{1,0:T(8,128)(2,1)} %get-tuple-element.83, ...), custom_call_target="tpu_custom_call" | custom-call | tf_op jit(solution)/shard_map/recurrent_backward/pallas_call | solution.py:1115
  341.2 0.0 copy-start.1
  341.2 223.7 %ring_sum.1 = (bf16[768,2304]{1,0:T(8,128)(2,1)}, bf16[768,1536]{1,0:T(8,128)(2,1)}, bf16[768,1024]{1,0:T(8,128)(2,1)}, bf16[768,1024]{1,0:T(8,128)(2,1)}, bf16[...) custom-call(bf16[768,2304]{1,0:T(8,128)(2,1)} %get-tuple-element.81., ...), custom_call_target="tpu_custom_call" | custom-call | tf_op jit(solution)/shard_map/ring_sum/pallas_call | solution.py:1415
  564.9 0.7 slice.47
  565.6 1.3 slice_bitcast_fusion
  566.9 0.6 slice_reduce_fusion
  567.5 1.2 collective-permute-start.5
  568.6 2.1 fusion
  570.7 1.3 bitcast_multiply_fusion
  572.0 0.7 slice.49
  572.7 0.6 slice.50
  573.4 20.7 %final.1 = (bf16[768,1024]{1,0:T(8,128)(2,1)}, bf16[768,1024]{1,0:T(8,128)(2,1)}, f32[768,2304]{1,0:T(8,128)}, f32[768,2304]{1,0:T(8,128)}, f32[768,2304]{1,0:T(...) custom-call(bf16[2,1024,768]{2,1,0:T(8,128)(2,1)} %get-tuple-element.117.gn, ...), custom_call_target="tpu_custom_call" | custom-call | tf_op jit(solution)/shard_map/final/pallas_call | solution.py:1477
  594.1 0.6 add.11
  (14 shorter events, 0.1 us)
Async XLA Ops:
  0.7 73.0 %collective-permute-start.1 = (bf16[768,2304]{1,0:T(8,128)(2,1)}, bf16[768,2304]{1,0:T(8,128)(2,1)}, u32[]{:S(2)}, u32[]{:S(2)}) collective-permute-start(bf16[768,2304]{1,0:T(8,128)(2,1)} %wg0.2), channel_id=1, source_target_pairs={{0,2},{2,0},{1,3},{3,1},{4,6},{6,4},{5,7},{7,5},{8,10},{10,8},{9,1... | collective-permute-start | bytes 10616840 | tf_op jit(solution)/shard_map/ppermute | solution.py:28
  1.2 72.5 %collective-permute-start.2 = (bf16[768,2304]{1,0:T(8,128)(2,1)}, bf16[768,2304]{1,0:T(8,128)(2,1)}, u32[]{:S(2)}, u32[]{:S(2)}) collective-permute-start(bf16[768,2304]{1,0:T(8,128)(2,1)} %wu0.1), channel_id=1, source_target_pairs={{0,2},{2,0},{1,3},{3,1},{4,6},{6,4},{5,7},{7,5},{8,10},{10,8},{9,1... | collective-permute-start | bytes 10616840 | tf_op jit(solution)/shard_map/ppermute | solution.py:28
  1.3 72.4 %collective-permute-start.3 = (bf16[768,2304]{1,0:T(8,128)(2,1)}, bf16[768,2304]{1,0:T(8,128)(2,1)}, u32[]{:S(2)}, u32[]{:S(2)}) collective-permute-start(bf16[768,2304]{1,0:T(8,128)(2,1)} %wd0.1), channel_id=1, source_target_pairs={{0,2},{2,0},{1,3},{3,1},{4,6},{6,4},{5,7},{7,5},{8,10},{10,8},{9,1... | collective-permute-start | bytes 10616840 | tf_op jit(solution)/shard_map/ppermute | solution.py:28
  1.7 70.7 %collective-permute-start = (f32[768]{0:T(1024)}, f32[768]{0:T(1024)S(1)}, u32[]{:S(2)}, u32[]{:S(2)}) collective-permute-start(f32[768]{0:T(1024)} %param.31), channel_id=1, source_target_pairs={{0,2},{2,0},{1,3},{3,1},{4,6},{6,4},{5,7},{7,5},{8,10},{10,8},{9,1... | collective-permute-start | bytes 9224 | tf_op jit(solution)/shard_map/ppermute | solution.py:28
  1.8 71.3 %collective-permute-start.4 = (f32[768]{0:T(1024)}, f32[768]{0:T(1024)S(1)}, u32[]{:S(2)}, u32[]{:S(2)}) collective-permute-start(f32[768]{0:T(1024)} %param.20), channel_id=1, source_target_pairs={{0,2},{2,0},{1,3},{3,1},{4,6},{6,4},{5,7},{7,5},{8,10},{10,8},{9,1... | collective-permute-start | bytes 9224 | tf_op jit(solution)/shard_map/ppermute | solution.py:28
  5.1 67.3 %copy-start.2 = (f32[768]{0:T(1024)S(1)}, f32[768]{0:T(1024)}, u32[]{:S(2)}) copy-start(f32[768]{0:T(1024)} %param.31) | copy-start | bytes 9220
  5.1 68.0 %copy-start = (f32[768]{0:T(1024)S(1)}, f32[768]{0:T(1024)}, u32[]{:S(2)}) copy-start(f32[768]{0:T(1024)} %param.20) | copy-start | bytes 9220
  341.2 229.5 %copy-start.1 = (f32[1024]{0:T(1024)S(1)}, f32[1024]{0:T(1024)}, u32[]{:S(2)}) copy-start(f32[1024]{0:T(1024)} %param.29) | copy-start | bytes 12292
  567.5 26.6 %collective-permute-start.5 = (f32[768]{0:T(1024)S(1)}, f32[768]{0:T(1024)S(1)}, u32[]{:S(2)}, u32[]{:S(2)}) collective-permute-start(f32[768]{0:T(1024)S(1)} %get-tuple-element.138), channel_id=1, source_target_pairs={{0,1},{1,0},{2,3},{3,2},{4,5},{5,4},{6,7},{7,6},{8,9},{9,8},{10,11... | collective-permute-start | bytes 9224 | tf_op jit(solution)/shard_map/ppermute | solution.py:28

commit v6 on v5

--- a/solution.py
+++ b/solution.py
@@ -576,25 +576,27 @@
 
         @pl.when(jnp.logical_and(k >= 0, k < many))
         def _():
-            grad = shared[a][0][k]
-            give_s[a, k % 2] = dot(n2t_s[half:], grad).astype(BF16)
+            product = dot(n2t_s[...], shared[a][0][k]).astype(BF16)
+            give_s[a, k % 2] = product[half:]
 
             @pl.when(k >= 2)
             def _():
                 pl.semaphore_wait(free_sem.at[a], 1)
 
             give(a, k).start()
-            keep_s[a, k % 2] = dot(n2t_s[:half], grad).astype(BF16)
+            keep_s[a, k % 2] = product[:half]
 
     @pl.when(jnp.logical_and(k >= BESIDE, k < blocks))
     def _():
-        gg0[...] = dot(n2t_s[:half], ga_s[k]).astype(BF16)
-        gg1[...] = dot(n2t_s[half:], ga_s[k]).astype(BF16)
+        product = dot(n2t_s[...], ga_s[k]).astype(BF16)
+        gg0[...] = product[:half]
+        gg1[...] = product[half:]
 
     @pl.when(jnp.logical_and(k >= 0, k < blocks))
     def _():
-        gd0[...] = dot(ct_s[0], hid_s[k]).astype(BF16)
-        gd1[...] = dot(ct_s[1], hid_s[k]).astype(BF16)
+        product = dot(ct_s[...].reshape(2 * half, ct_s.shape[2]), hid_s[k]).astype(BF16)
+        gd0[...] = product[:half]
+        gd1[...] = product[half:]
 
     for c in range(count - 1):
 
@@ -940,8 +942,9 @@
     beat(0)
     gb_s[...] = dot(g1[:, :half], ow0[...]) + dot(g1[:, half:], ow1[...])
     beat(1)
-    go0[...] = dot(g1t[:half], br[...]).astype(BF16)
-    go1[...] = dot(g1t[half:], br[...]).astype(BF16)
+    product = dot(g1t[...], br[...]).astype(BF16)
+    go0[...] = product[:half]
+    go1[...] = product[half:]
     beat(2)
     sums[...] = jnp.zeros_like(sums)
     row = lax.broadcasted_iota(jnp.int32, (8, 128), 0)
@@ -1055,10 +1058,12 @@
             small1[at, 0:128] = tile_now
     grad_rec = grec_s[...]
     grad_gate = ggp_s[...]
-    gr0[...] = dot(n1t[:half], grad_rec).astype(BF16)
-    gr1[...] = dot(n1t[half:], grad_rec).astype(BF16)
-    gg0[...] = dot(n1t[:half], grad_gate).astype(BF16)
-    gg1[...] = dot(n1t[half:], grad_gate).astype(BF16)
+    product = dot(n1t[...], grad_rec).astype(BF16)
+    gr0[...] = product[:half]
+    gr1[...] = product[half:]
+    product = dot(n1t[...], grad_gate).astype(BF16)
+    gg0[...] = product[:half]
+    gg1[...] = product[half:]
     acc[:, :half] += dot_nt(grad_rec, wr0[...]) + dot_nt(grad_gate, wg0[...])
     acc[:, half:] += dot_nt(grad_rec, wr1[...]) + dot_nt(grad_gate, wg1[...])
 

time: 595 us -> 584 us (0.982)
  Pallas kernels: 579 us -> 568 us
    pallas_call x1, Pallas kernels: 154 us -> 144 us  [ffn(): pl.pallas_call(functools.partial(ffn_kernel, count, blocks), grid=(first_...]
  transfers between devices with their start and end apart: 6 -> 6, of which waited for: 0 -> 0; matrix products, arithmetic and copies ran while one was open for 1% -> 2% of each run, Pallas kernels for 15% -> 15%
where the time goes in v6:
time: 584 us
  Pallas kernels  568 us (97%)
  local copies, waits for them, and re-layouts  8.86 us (2%)
    pallas_call x1, Pallas kernels, ring_sum(): pl.pallas_call(functools.partial(ring_kernel, n, count), in_specs=[hbm] *...  224 us
    pallas_call x1, Pallas kernels, ffn(): pl.pallas_call(functools.partial(ffn_kernel, count, blocks), grid=(first_...  144 us
    pallas_call x1, Pallas kernels, rec_backward(): pl.pallas_call(functools.partial(rec_backward_kernel, tile, n), grid=(wid...  112 us
    pallas_call x1, Pallas kernels, rec_forward(): pl.pallas_call(functools.partial(rec_forward_kernel, chunk, count, cot_pa...  67.3 us
    pallas_call x1, Pallas kernels, final(): pl.pallas_call(final_kernel, grid=(steps,), in_specs=[pair(half), pair(ha...  20.7 us
  transfers between devices with their start and end apart: 6, of which 0 were waited for; matrix products, arithmetic and copies ran while one was open for 2% of the time, Pallas kernels for 15%

profile of v6, /device:TPU:0, one launch (start us, length us, event | category | flops | bytes accessed | tf_op | source)
XLA Modules:
  0.0 583.7 jit_solution(13850432801489772874)
XLA Ops:
  0.7 0.5 collective-permute-start.1
  1.2 0.1 collective-permute-start.2
  1.3 0.4 collective-permute-start.3
  1.7 0.1 collective-permute-start
  1.8 0.4 collective-permute-start.4
  2.2 1.3 compare_select_fusion
  3.5 1.6 broadcast_in_dim.29.gain_h.gain
  5.1 67.3 %recurrent_forward.1 = (bf16[1024,1536]{1,0:T(8,128)(2,1)}, bf16[1536,1024]{1,0:T(8,128)(2,1)}, f32[1024,1024]{1,0:T(8,128)}, f32[1024,1024]{1,0:T(8,128)}, bf16...) custom-call(bf16[768,1024]{1,0:T(8,128)(2,1)} %tokens.3, ...), custom_call_target="tpu_custom_call" | custom-call | tf_op jit(solution)/shard_map/recurrent_forward/pallas_call | solution.py:329
  72.5 0.6 broadcast_in_dim.27.gain.gain_second
  73.1 0.6 broadcast_in_dim.28.gain
  73.7 144.3 %ffn.1 = (bf16[1024,1536]{1,0:T(8,128)(2,1)}, bf16[768,2304]{1,0:T(8,128)(2,1)}, bf16[768,768]{1,0:T(8,128)(2,1)}, bf16[768,1536]{1,0:T(8,128)(2,1)}, bf16[768,1...) custom-call(bf16[1024,1536]{1,0:T(8,128)(2,1)} %get-tuple-element.77, ...), custom_call_target="tpu_custom_call" | custom-call | tf_op jit(solution)/shard_map/ffn/pallas_call | solution.py:650
  218.0 112.2 %recurrent_backward.1 = (bf16[1024,1536]{1,0:T(8,128)(2,1)}, bf16[768,1024]{1,0:T(8,128)(2,1)}, bf16[768,1024]{1,0:T(8,128)(2,1)}, bf16[768,1024]{1,0:T(8,128)(2...) custom-call(bf16[1536,1024]{1,0:T(8,128)(2,1)} %get-tuple-element.83, ...), custom_call_target="tpu_custom_call" | custom-call | tf_op jit(solution)/shard_map/recurrent_backward/pallas_call | solution.py:1120
  330.2 0.0 copy-start.1
  330.2 223.6 %ring_sum.1 = (bf16[768,2304]{1,0:T(8,128)(2,1)}, bf16[768,1536]{1,0:T(8,128)(2,1)}, bf16[768,1024]{1,0:T(8,128)(2,1)}, bf16[768,1024]{1,0:T(8,128)(2,1)}, bf16[...) custom-call(bf16[768,2304]{1,0:T(8,128)(2,1)} %get-tuple-element.81., ...), custom_call_target="tpu_custom_call" | custom-call | tf_op jit(solution)/shard_map/ring_sum/pallas_call | solution.py:1420
  553.8 0.7 slice.47
  554.5 1.3 slice_bitcast_fusion
  555.8 0.6 slice_reduce_fusion
  556.4 1.2 collective-permute-start.5
  557.6 2.1 fusion
  559.7 1.3 bitcast_multiply_fusion
  561.0 0.7 slice.49
  561.7 0.6 slice.50
  562.3 20.7 %final.1 = (bf16[768,1024]{1,0:T(8,128)(2,1)}, bf16[768,1024]{1,0:T(8,128)(2,1)}, f32[768,2304]{1,0:T(8,128)}, f32[768,2304]{1,0:T(8,128)}, f32[768,2304]{1,0:T(...) custom-call(bf16[2,1024,768]{2,1,0:T(8,128)(2,1)} %get-tuple-element.117.gn, ...), custom_call_target="tpu_custom_call" | custom-call | tf_op jit(solution)/shard_map/final/pallas_call | solution.py:1482
  583.1 0.6 add.11
  (14 shorter events, 0.1 us)
Async XLA Ops:
  0.7 73.0 %collective-permute-start.1 = (bf16[768,2304]{1,0:T(8,128)(2,1)}, bf16[768,2304]{1,0:T(8,128)(2,1)}, u32[]{:S(2)}, u32[]{:S(2)}) collective-permute-start(bf16[768,2304]{1,0:T(8,128)(2,1)} %wg0.2), channel_id=1, source_target_pairs={{0,2},{2,0},{1,3},{3,1},{4,6},{6,4},{5,7},{7,5},{8,10},{10,8},{9,1... | collective-permute-start | bytes 10616840 | tf_op jit(solution)/shard_map/ppermute | solution.py:28
  1.2 72.5 %collective-permute-start.2 = (bf16[768,2304]{1,0:T(8,128)(2,1)}, bf16[768,2304]{1,0:T(8,128)(2,1)}, u32[]{:S(2)}, u32[]{:S(2)}) collective-permute-start(bf16[768,2304]{1,0:T(8,128)(2,1)} %wu0.1), channel_id=1, source_target_pairs={{0,2},{2,0},{1,3},{3,1},{4,6},{6,4},{5,7},{7,5},{8,10},{10,8},{9,1... | collective-permute-start | bytes 10616840 | tf_op jit(solution)/shard_map/ppermute | solution.py:28
  1.3 72.4 %collective-permute-start.3 = (bf16[768,2304]{1,0:T(8,128)(2,1)}, bf16[768,2304]{1,0:T(8,128)(2,1)}, u32[]{:S(2)}, u32[]{:S(2)}) collective-permute-start(bf16[768,2304]{1,0:T(8,128)(2,1)} %wd0.1), channel_id=1, source_target_pairs={{0,2},{2,0},{1,3},{3,1},{4,6},{6,4},{5,7},{7,5},{8,10},{10,8},{9,1... | collective-permute-start | bytes 10616840 | tf_op jit(solution)/shard_map/ppermute | solution.py:28
  1.7 70.7 %collective-permute-start = (f32[768]{0:T(1024)}, f32[768]{0:T(1024)S(1)}, u32[]{:S(2)}, u32[]{:S(2)}) collective-permute-start(f32[768]{0:T(1024)} %param.31), channel_id=1, source_target_pairs={{0,2},{2,0},{1,3},{3,1},{4,6},{6,4},{5,7},{7,5},{8,10},{10,8},{9,1... | collective-permute-start | bytes 9224 | tf_op jit(solution)/shard_map/ppermute | solution.py:28
  1.8 71.3 %collective-permute-start.4 = (f32[768]{0:T(1024)}, f32[768]{0:T(1024)S(1)}, u32[]{:S(2)}, u32[]{:S(2)}) collective-permute-start(f32[768]{0:T(1024)} %param.20), channel_id=1, source_target_pairs={{0,2},{2,0},{1,3},{3,1},{4,6},{6,4},{5,7},{7,5},{8,10},{10,8},{9,1... | collective-permute-start | bytes 9224 | tf_op jit(solution)/shard_map/ppermute | solution.py:28
  5.1 67.3 %copy-start.2 = (f32[768]{0:T(1024)S(1)}, f32[768]{0:T(1024)}, u32[]{:S(2)}) copy-start(f32[768]{0:T(1024)} %param.31) | copy-start | bytes 9220
  5.1 68.0 %copy-start = (f32[768]{0:T(1024)S(1)}, f32[768]{0:T(1024)}, u32[]{:S(2)}) copy-start(f32[768]{0:T(1024)} %param.20) | copy-start | bytes 9220
  330.2 229.5 %copy-start.1 = (f32[1024]{0:T(1024)S(1)}, f32[1024]{0:T(1024)}, u32[]{:S(2)}) copy-start(f32[1024]{0:T(1024)} %param.29) | copy-start | bytes 12292
  556.4 26.7 %collective-permute-start.5 = (f32[768]{0:T(1024)S(1)}, f32[768]{0:T(1024)S(1)}, u32[]{:S(2)}, u32[]{:S(2)}) collective-permute-start(f32[768]{0:T(1024)S(1)} %get-tuple-element.138), channel_id=1, source_target_pairs={{0,1},{1,0},{2,3},{3,2},{4,5},{5,4},{6,7},{7,6},{8,9},{9,8},{10,11... | collective-permute-start | bytes 9224 | tf_op jit(solution)/shard_map/ppermute | solution.py:28

commit v7 on v6

--- a/solution.py
+++ b/solution.py
@@ -1440,8 +1440,8 @@
 
 
 def final_kernel(
-    gn, out, stat, g1, tokens, gain, lengths, beside, down, gate, out_w, rec_w, gate_w,
-    result_o, grad_o, up_o, gate_o, down_o, out_w_o, rec_w_o, gate_w_o,
+    gn, out, stat, g1, tokens, gain, lengths, beside, down, gate, out_w, rec_w, gate_w, blocks,
+    result_o, grad_o, up_o, gate_o, down_o, out_w_o, rec_w_o, gate_w_o, recur_o, input_o,
 ):
     wide = 2 * tokens.shape[0]
     low = lambda ref: ref[0].astype(F32) + ref[1].astype(F32)
@@ -1468,9 +1468,12 @@
     gate_o[:, 2 * gate_half :] = gate[...].astype(F32)
     for src, dst in ((down, down_o), (out_w, out_w_o), (rec_w, rec_w_o), (gate_w, gate_w_o)):
         dst[...] = src[...].astype(F32)
-
-
-def final(gn, out, stat, g1, tokens, gain, lengths, beside, down, gate, out_w, rec_w, gate_w, steps=8):
+    both = blocks[...].astype(F32).reshape(recur_o.shape[0], 128, 256)
+    recur_o[...] = both[:, :, :128]
+    input_o[...] = both[:, :, 128:]
+
+
+def final(gn, out, stat, g1, tokens, gain, lengths, beside, down, gate, out_w, rec_w, gate_w, blocks, steps=8):
     half, length = tokens.shape
     chunk, size = length // steps, half // steps
     pair = lambda cols: pl.BlockSpec((2, chunk, cols), lambda i: (0, i, 0))
@@ -1479,6 +1482,7 @@
     shape = jax.ShapeDtypeStruct((half, length), BF16)
     ffn_wide, wide = down.shape[1], out_w.shape[1]
     grads = [ffn_wide] * 3 + [wide] * 3
+    heads = blocks.shape[0] // 128
     return pl.pallas_call(
         final_kernel,
         grid=(steps,),
@@ -1489,12 +1493,16 @@
             pl.BlockSpec((half, 1), lambda i: (0, 0)),
             pl.BlockSpec(memory_space=pltpu.SMEM),
         ]
-        + [rows(a.shape[1]) for a in (beside, down, gate, out_w, rec_w, gate_w)],
-        out_specs=[across, across] + [rows(cols) for cols in grads],
-        out_shape=[shape, shape] + [jax.ShapeDtypeStruct((half, cols), F32) for cols in grads],
+        + [rows(a.shape[1]) for a in (beside, down, gate, out_w, rec_w, gate_w)]
+        + [pl.BlockSpec((blocks.shape[0] // steps, 256), lambda i: (i, 0))],
+        out_specs=[across, across]
+        + [rows(cols) for cols in grads]
+        + [pl.BlockSpec((heads // steps, 128, 128), lambda i: (i, 0, 0))] * 2,
+        out_shape=[shape, shape] + [jax.ShapeDtypeStruct((half, cols), F32) for cols in grads]
+        + [jax.ShapeDtypeStruct((heads, 128, 128), F32)] * 2,
         compiler_params=pltpu.CompilerParams(vmem_limit_bytes=56 * MIB),
         name="final",
-    )(gn, out, stat, g1, tokens, gain, lengths, beside, down, gate, out_w, rec_w, gate_w)
+    )(gn, out, stat, g1, tokens, gain, lengths, beside, down, gate, out_w, rec_w, gate_w, blocks)
 
 
 def body(
@@ -1540,11 +1548,10 @@
         [gd1, gg1, go1, gr1, gt1, gates, small1],
         [gn1_part, out, stat, g1_head, g1_last],
     )
-    gates, small = total[5:]
-    result, grad_tokens, sum_up, sum_gate, sum_down, sum_out, sum_rec, sum_gatew = final(
-        *moved, tokens, mix_gain[:, None], lengths, beside, *total[:5]
+    small = total[6]
+    result, grad_tokens, sum_up, sum_gate, sum_down, sum_out, sum_rec, sum_gatew, grad_recur, grad_input = final(
+        *moved, tokens, mix_gain[:, None], lengths, beside, *total[:6]
     )
-    gates = gates.astype(F32).reshape(ggw.shape)
     vec = small[:, :128].reshape(8, -1)
     gains = small[:16, 128:].reshape(2, -1)[:, :half]
     grad_gain_one = gains[0] + swap(gains[0], "cols")
@@ -1557,9 +1564,9 @@
         sum_gatew,
         vec[3:7],
         vec[7],
-        gates[:, :, :128],
+        grad_recur,
         vec[0],
-        gates[:, :, 128:],
+        grad_input,
         vec[1],
         grad_decay,
         sum_out,

time: 584 us -> 582 us (level)
  transfers between devices with their start and end apart: 6 -> 6, of which waited for: 0 -> 0; matrix products, arithmetic and copies ran while one was open for 2% -> 1% of each run, Pallas kernels for 15% -> 15%
where the time goes in v7:
time: 582 us
  Pallas kernels  568 us (98%)
  local copies, waits for them, and re-layouts  6.76 us (1%)
    pallas_call x1, Pallas kernels, ring_sum(): pl.pallas_call(functools.partial(ring_kernel, n, count), in_specs=[hbm] *...  224 us
    pallas_call x1, Pallas kernels, ffn(): pl.pallas_call(functools.partial(ffn_kernel, count, blocks), grid=(first_...  144 us
    pallas_call x1, Pallas kernels, rec_backward(): pl.pallas_call(functools.partial(rec_backward_kernel, tile, n), grid=(wid...  112 us
    pallas_call x1, Pallas kernels, rec_forward(): pl.pallas_call(functools.partial(rec_forward_kernel, chunk, count, cot_pa...  67.3 us
    pallas_call x1, Pallas kernels, final(): pl.pallas_call(final_kernel, grid=(steps,), in_specs=[pair(half), pair(ha...  21 us
  transfers between devices with their start and end apart: 6, of which 0 were waited for; matrix products, arithmetic and copies ran while one was open for 1% of the time, Pallas kernels for 15%

profile of v7, /device:TPU:0, one launch (start us, length us, event | category | flops | bytes accessed | tf_op | source)
XLA Modules:
  0.0 581.8 jit_solution(6741805192837739178)
XLA Ops:
  0.7 0.5 collective-permute-start.1
  1.2 0.1 collective-permute-start.2
  1.3 0.4 collective-permute-start.3
  1.7 0.1 collective-permute-start
  1.8 0.4 collective-permute-start.4
  2.2 1.3 compare_select_fusion
  3.5 1.6 broadcast_in_dim.29.gain_h.gain
  5.1 67.3 %recurrent_forward.1 = (bf16[1024,1536]{1,0:T(8,128)(2,1)}, bf16[1536,1024]{1,0:T(8,128)(2,1)}, f32[1024,1024]{1,0:T(8,128)}, f32[1024,1024]{1,0:T(8,128)}, bf16...) custom-call(bf16[768,1024]{1,0:T(8,128)(2,1)} %tokens.3, ...), custom_call_target="tpu_custom_call" | custom-call | tf_op jit(solution)/shard_map/recurrent_forward/pallas_call | solution.py:329
  72.5 0.6 broadcast_in_dim.27.gain.gain_second
  73.1 0.0 collective-permute-done.4
  73.1 0.6 broadcast_in_dim.28.gain
  73.7 144.3 %ffn.1 = (bf16[1024,1536]{1,0:T(8,128)(2,1)}, bf16[768,2304]{1,0:T(8,128)(2,1)}, bf16[768,768]{1,0:T(8,128)(2,1)}, bf16[768,1536]{1,0:T(8,128)(2,1)}, bf16[768,1...) custom-call(bf16[1024,1536]{1,0:T(8,128)(2,1)} %get-tuple-element.79, ...), custom_call_target="tpu_custom_call" | custom-call | tf_op jit(solution)/shard_map/ffn/pallas_call | solution.py:650
  218.0 112.2 %recurrent_backward.1 = (bf16[1024,1536]{1,0:T(8,128)(2,1)}, bf16[768,1024]{1,0:T(8,128)(2,1)}, bf16[768,1024]{1,0:T(8,128)(2,1)}, bf16[768,1024]{1,0:T(8,128)(2...) custom-call(bf16[1536,1024]{1,0:T(8,128)(2,1)} %get-tuple-element.85, ...), custom_call_target="tpu_custom_call" | custom-call | tf_op jit(solution)/shard_map/recurrent_backward/pallas_call | solution.py:1120
  330.2 0.0 copy-start.1
  330.3 223.6 %ring_sum.1 = (bf16[768,2304]{1,0:T(8,128)(2,1)}, bf16[768,1536]{1,0:T(8,128)(2,1)}, bf16[768,1024]{1,0:T(8,128)(2,1)}, bf16[768,1024]{1,0:T(8,128)(2,1)}, bf16[...) custom-call(bf16[768,2304]{1,0:T(8,128)(2,1)} %get-tuple-element.83., ...), custom_call_target="tpu_custom_call" | custom-call | tf_op jit(solution)/shard_map/ring_sum/pallas_call | solution.py:1420
  553.8 0.7 slice.41
  554.5 1.3 slice_bitcast_fusion
  555.8 0.6 slice_reduce_fusion
  556.4 1.2 collective-permute-start.5
  557.6 1.3 bitcast_multiply_fusion
  558.9 0.7 slice.43
  559.6 0.6 slice.44
  560.2 21.0 %final.1 = (bf16[768,1024]{1,0:T(8,128)(2,1)}, bf16[768,1024]{1,0:T(8,128)(2,1)}, f32[768,2304]{1,0:T(8,128)}, f32[768,2304]{1,0:T(8,128)}, f32[768,2304]{1,0:T(...) custom-call(bf16[2,1024,768]{2,1,0:T(8,128)(2,1)} %get-tuple-element, ...), custom_call_target="tpu_custom_call" | custom-call | tf_op jit(solution)/shard_map/final/pallas_call | solution.py:1486
  581.2 0.6 add.11
  (13 shorter events, 0.0 us)
Async XLA Ops:
  0.7 73.0 %collective-permute-start.1 = (bf16[768,2304]{1,0:T(8,128)(2,1)}, bf16[768,2304]{1,0:T(8,128)(2,1)}, u32[]{:S(2)}, u32[]{:S(2)}) collective-permute-start(bf16[768,2304]{1,0:T(8,128)(2,1)} %wg0.2), channel_id=1, source_target_pairs={{0,2},{2,0},{1,3},{3,1},{4,6},{6,4},{5,7},{7,5},{8,10},{10,8},{9,1... | collective-permute-start | bytes 10616840 | tf_op jit(solution)/shard_map/ppermute | solution.py:28
  1.2 72.5 %collective-permute-start.2 = (bf16[768,2304]{1,0:T(8,128)(2,1)}, bf16[768,2304]{1,0:T(8,128)(2,1)}, u32[]{:S(2)}, u32[]{:S(2)}) collective-permute-start(bf16[768,2304]{1,0:T(8,128)(2,1)} %wu0.1), channel_id=1, source_target_pairs={{0,2},{2,0},{1,3},{3,1},{4,6},{6,4},{5,7},{7,5},{8,10},{10,8},{9,1... | collective-permute-start | bytes 10616840 | tf_op jit(solution)/shard_map/ppermute | solution.py:28
  1.3 72.4 %collective-permute-start.3 = (bf16[768,2304]{1,0:T(8,128)(2,1)}, bf16[768,2304]{1,0:T(8,128)(2,1)}, u32[]{:S(2)}, u32[]{:S(2)}) collective-permute-start(bf16[768,2304]{1,0:T(8,128)(2,1)} %wd0.1), channel_id=1, source_target_pairs={{0,2},{2,0},{1,3},{3,1},{4,6},{6,4},{5,7},{7,5},{8,10},{10,8},{9,1... | collective-permute-start | bytes 10616840 | tf_op jit(solution)/shard_map/ppermute | solution.py:28
  1.7 70.8 %collective-permute-start = (f32[768]{0:T(1024)}, f32[768]{0:T(1024)S(1)}, u32[]{:S(2)}, u32[]{:S(2)}) collective-permute-start(f32[768]{0:T(1024)} %param.31), channel_id=1, source_target_pairs={{0,2},{2,0},{1,3},{3,1},{4,6},{6,4},{5,7},{7,5},{8,10},{10,8},{9,1... | collective-permute-start | bytes 9224 | tf_op jit(solution)/shard_map/ppermute | solution.py:28
  1.8 71.3 %collective-permute-start.4 = (f32[768]{0:T(1024)}, f32[768]{0:T(1024)S(1)}, u32[]{:S(2)}, u32[]{:S(2)}) collective-permute-start(f32[768]{0:T(1024)} %param.20), channel_id=1, source_target_pairs={{0,2},{2,0},{1,3},{3,1},{4,6},{6,4},{5,7},{7,5},{8,10},{10,8},{9,1... | collective-permute-start | bytes 9224 | tf_op jit(solution)/shard_map/ppermute | solution.py:28
  5.1 67.4 %copy-start.2 = (f32[768]{0:T(1024)S(1)}, f32[768]{0:T(1024)}, u32[]{:S(2)}) copy-start(f32[768]{0:T(1024)} %param.31) | copy-start | bytes 9220
  5.1 68.0 %copy-start = (f32[768]{0:T(1024)S(1)}, f32[768]{0:T(1024)}, u32[]{:S(2)}) copy-start(f32[768]{0:T(1024)} %param.20) | copy-start | bytes 9220
  330.2 227.4 %copy-start.1 = (f32[1024]{0:T(1024)S(1)}, f32[1024]{0:T(1024)}, u32[]{:S(2)}) copy-start(f32[1024]{0:T(1024)} %param.29) | copy-start | bytes 12292
  556.4 24.8 %collective-permute-start.5 = (f32[768]{0:T(1024)S(1)}, f32[768]{0:T(1024)S(1)}, u32[]{:S(2)}, u32[]{:S(2)}) collective-permute-start(f32[768]{0:T(1024)S(1)} %get-tuple-element.142), channel_id=1, source_target_pairs={{0,1},{1,0},{2,3},{3,2},{4,5},{5,4},{6,7},{7,6},{8,9},{9,8},{10,11... | collective-permute-start | bytes 9224 | tf_op jit(solution)/shard_map/ppermute | solution.py:28
